TPU v7x, 512 devices: a whole 4x8x8 slice. The times are simulated.
512 devices in a mesh: ctx: 64 (over z, x, core), tp: 8 (over y).
Axes of the slice: x: 4, y: 8, z: 8, core: 2. Of those that a mesh axis runs over, the one named last changes fastest.
Arguments:
- queries: bfloat16 [32768, 4096], P('ctx', 'tp'), may hold values from -6 to 6
- keys: bfloat16 [32768, 4096], P('ctx', 'tp'), may hold values from -6 to 6
- values: bfloat16 [32768, 4096], P('ctx', 'tp'), may hold values from -6 to 6
- out_weight: bfloat16 [4096, 4096], P('tp', 'ctx'), may hold values from -0.09375 to 0.09375
Outputs:
- mixed: bfloat16 [32768, 4096], P(('ctx', 'tp'))
All inputs are finite; a program needn't handle non-finite values.
Results may differ from a plain program's by a relative error of at most 0.018.
Values may be sent and summed in bfloat16 or wider, within the bound.
No kernel may reach another device: no remote copies, remote signals or barrier semaphores. Data moves between devices by JAX's collectives and lax.ppermute only.
A program may use at most 64 MiB of HBM per device.

v0:
```python
import jax
import jax.numpy as jnp
from jax import lax
from jax.sharding import PartitionSpec as P

HD = 128


def prefix(part, axis, combine, identity):
    place = lax.axis_index(axis)
    gathered = lax.all_gather(part, axis)
    state = jnp.zeros_like(part) + jnp.asarray(identity, part.dtype)

    def one(step, state):
        return combine(state, lax.dynamic_index_in_dim(gathered, step, 0, False))

    return lax.fori_loop(0, place, one, state)


def add_states(earlier, later):
    return earlier + later


def on_device(queries, keys, values, out_weight):
    tok_rows = queries.shape[0]
    head_dim = HD
    heads_here = queries.shape[1] // head_dim
    block_len = min(tok_rows, 512)
    blocks = tok_rows // block_len
    shape = (blocks, block_len, heads_here, head_dim)
    q_blk = queries.reshape(shape)
    k_blk = keys.reshape(shape)
    v_blk = values.reshape(shape)
    block_state = jnp.einsum("nthd,nthe->nhde", k_blk, v_blk, preferred_element_type=jnp.float32)
    own_total = jnp.sum(block_state, axis=0)
    inside = jnp.cumsum(block_state, axis=0) - block_state
    zeros_state = jnp.zeros_like(own_total)
    before = prefix(own_total, "ctx", add_states, zeros_state)
    carried = (before[None] + inside).astype(jnp.bfloat16)
    causal = jnp.arange(block_len)[:, None] >= jnp.arange(block_len)[None, :]
    scores = jnp.einsum("nthd,nshd->nhts", q_blk, k_blk, preferred_element_type=jnp.float32)
    scores = jnp.where(causal[None, None], scores, 0.0).astype(jnp.bfloat16)
    intra = jnp.einsum("nhts,nshe->nthe", scores, v_blk, preferred_element_type=jnp.float32)
    inter = jnp.einsum("nthd,nhde->nthe", q_blk, carried, preferred_element_type=jnp.float32)
    attended = inter + intra
    normed = attended / jnp.sqrt(jnp.mean(attended * attended, axis=-1, keepdims=True) + 1e-06)
    normed = normed.astype(jnp.bfloat16).reshape(tok_rows, heads_here * head_dim)
    terms = jnp.dot(
        normed,
        lax.all_gather(out_weight, "ctx", axis=1, tiled=True),
        preferred_element_type=jnp.float32,
    )
    summed = lax.psum_scatter(terms.astype(jnp.bfloat16), "tp", scatter_dimension=0, tiled=True)
    return summed


def solution(mesh):
    placed = (P("ctx", "tp"), P("ctx", "tp"), P("ctx", "tp"), P("tp", "ctx"))
    return jax.shard_map(
        on_device, mesh=mesh, in_specs=placed, out_specs=P(("ctx", "tp"), None), check_vma=False
    )
```

profile of v0, /device:TPU:1, one launch (start us, length us, event | category | flops | bytes accessed | tf_op | source)
XLA Modules:
  0.0 274.9 jit_solution(6830236183896022547)
XLA Ops:
  6.5 0.0 copy-start
  6.5 0.0 all-gather.6.cloned.1.call-start
  6.5 1.3 copy.16
  7.9 1.3 copy.17
  9.1 1.0 fusion.14
  10.1 0.0 copy-start.1
  10.1 0.0 all-gather.6.cloned.1.call-update
  10.1 0.0 all-gather.4.cloned.1.call-start
  10.2 0.7 all-gather.4.cloned.1.call-update
  10.9 0.0 reduce-scatter.2.cloned.1.call-start
  10.9 0.1 iota_compare_fusion
  11.0 111.6 %all-gather.6.cloned.1.call-done = f32[256,128,128]{2,1,0:T(8,128)} async-done(((f32[4,128,128]{2,1,0:T(8,128)}), f32[256,128,128]{2,1,0:T(8,128)}) %all-gather.6.cloned.1.call-update) | async-done | bytes 16777232 | tf_op jit(solution)/shard_map/all_gather | solution.py:11
  122.6 1.0 while.10
  122.6 1.0 bitcast_add_fusion.2
  123.7 0.0 copy-done
  123.7 0.0 copy-done.1
  123.7 1.3 fusion.6
  125.0 2.6 multiply_reduce_fusion
  127.6 0.1 divide_convert_fusion
  127.7 79.9 %all-gather.4.cloned.1.call-done = bf16[512,4096]{0,1:T(8,128)(2,1)} async-done(((bf16[512,64]{0,1:T(8,128)(2,1)}), bf16[512,4096]{0,1:T(8,128)(2,1)}) %all-gather.4.cloned.1.call-update) | async-done | bytes 4194320 | tf_op jit(solution)/shard_map/all_gather | solution.py:50
  207.6 6.5 %convolution_convert_fusion = bf16[512,4096]{1,0:T(8,128)(2,1)} fusion(bf16[512,512]{0,1:T(8,128)(2,1)S(1)} %bitcast.44, bf16[512,4096]{0,1:T(8,128)(2,1)} %all-gather.4.cloned.1.call-done), kind=kOutput, calls=%fused_computation.1 | convolution fusion | flops 2149580800 | bytes 8912896 | tf_op jit(solution)/shard_map/dot_general | solution.py:48
  214.1 0.0 reduce-scatter.2.cloned.1.call-update
  214.1 54.2 %reduce-scatter.2.cloned.1.call-done = bf16[64,4096]{1,0:T(8,128)(2,1)} async-done(((bf16[512,4096]{1,0:T(8,128)(2,1)}), bf16[64,4096]{1,0:T(8,128)(2,1)}) %reduce-scatter.2.cloned.1.call-update) | async-done | bytes 524304 | tf_op jit(solution)/shard_map/reduce_scatter | solution.py:53
  (2 shorter events, 0.0 us)
Async XLA Ops:
  6.5 117.1 %copy-start = (bf16[512,512]{1,0:T(8,128)(2,1)S(1)}, bf16[512,512]{1,0:T(8,128)(2,1)}, u32[]{:S(2)}) copy-start(bf16[512,512]{1,0:T(8,128)(2,1)} %param.6) | copy-start | bytes 1572868
  6.5 116.1 %all-gather.6.cloned.1.call-start = ((), (), s32[]{:S(2)}) async-start(), calls=%async_computation.3 | async-start | bytes 17039360 | tf_op jit(solution)/shard_map/all_gather | solution.py:11
  10.1 113.6 %copy-start.1 = (f32[4,128,128]{2,1,0:T(8,128)S(1)}, f32[4,128,128]{2,1,0:T(8,128)}, u32[]{:S(2)}) copy-start(f32[4,128,128]{2,1,0:T(8,128)} %fusion.14) | copy-start | bytes 786436
  10.1 197.4 %all-gather.4.cloned.1.call-start = ((), (), s32[]{:S(2)}) async-start(), calls=%async_computation.1 | async-start | bytes 4259840 | tf_op jit(solution)/shard_map/all_gather | solution.py:50
  10.9 257.5 %reduce-scatter.2.cloned.1.call-start = ((), (), s32[]{:S(2)}) async-start(), calls=%async_computation.2 | async-start | bytes 4718592 | tf_op jit(solution)/shard_map/reduce_scatter | solution.py:53
Sparse Core Ops, SparseCore 0:
  10.7 111.8 all-gather.5
  125.9 81.5 all-gather.3
  214.3 54.0 reduce-scatter.1
where the time goes:
time: 277 us; the launch traced here: 275 us
  waiting for transfers between devices  246 us (89%)
  between operations  13.2 us (5%)
  matrix products  11.4 us (4%)
    all_gather x1, waiting for transfers between devices, prefix(): gathered = lax.all_gather(part, axis)  112 us
    all_gather x1, waiting for transfers between devices, on_device(): lax.all_gather(out_weight, 'ctx', axis=1, tiled=True)  79.9 us
    reduce_scatter x1, waiting for transfers between devices, on_device(): lax.psum_scatter(terms.astype(jnp.bfloat16), 'tp', scatter_dimension=0, t...  54.2 us
    dot_general x1, matrix products, on_device(): jnp.dot(normed, lax.all_gather(out_weight, 'ctx', axis=1, tiled=True), pr...  6.53 us
  transfers between devices with their start and end apart: 3, of which 3 were waited for; matrix products, arithmetic and copies ran while one was open for 2% of the time, Pallas kernels for 0%

commit v1 on v0

v1 whole, which is shorter than its diff:
```python
import jax
import jax.numpy as jnp
from jax import lax
from jax.experimental import pallas as pl
from jax.experimental.pallas import tpu as pltpu
from jax.sharding import Mesh, PartitionSpec as P

HD = 128
F32 = jnp.float32
BF16 = jnp.bfloat16
Z, X, C, Y = 8, 4, 2, 8


def state_kernel(k_ref, v_ref, s_ref):
    for h in range(4):
        cols = slice(h * HD, (h + 1) * HD)
        s = lax.dot_general(
            k_ref[:, cols], v_ref[:, cols], (((0,), (0,)), ((), ())), preferred_element_type=F32
        )
        s_ref[cols, :] = s.astype(BF16)


def states(keys, values):
    return pl.pallas_call(
        state_kernel,
        out_shape=jax.ShapeDtypeStruct((4 * HD, HD), BF16),
        compiler_params=pltpu.CompilerParams(vmem_limit_bytes=16 * 2**20),
        cost_estimate=pl.CostEstimate(flops=2 * 512 * 512 * 128, bytes_accessed=2**20, transcendentals=0),
    )(keys, values)


def attention_kernel(q_ref, k_ref, v_ref, c_ref, o_ref):
    half = 256
    row = lax.broadcasted_iota(jnp.int32, (half, half), 0)
    col = lax.broadcasted_iota(jnp.int32, (half, half), 1)
    causal = row >= col
    nt = (((1,), (1,)), ((), ()))

    def masked(q, k):
        s = lax.dot_general(q, k, nt, preferred_element_type=F32)
        return jnp.where(causal, s, 0.0).astype(BF16)

    def norm(a):
        r = lax.rsqrt(jnp.mean(a * a, axis=-1, keepdims=True) + 1e-06)
        return (a * r).astype(BF16)

    c = c_ref[...]
    q0, q1 = q_ref[:half], q_ref[half:]
    k0, k1 = k_ref[:half], k_ref[half:]
    v0, v1 = v_ref[:half], v_ref[half:]
    a0 = jnp.dot(q0, c, preferred_element_type=F32)
    a0 += jnp.dot(masked(q0, k0), v0, preferred_element_type=F32)
    o_ref[:half] = norm(a0)
    a1 = jnp.dot(q1, c, preferred_element_type=F32)
    s10 = lax.dot_general(q1, k0, nt, preferred_element_type=F32).astype(BF16)
    a1 += jnp.dot(s10, v0, preferred_element_type=F32)
    a1 += jnp.dot(masked(q1, k1), v1, preferred_element_type=F32)
    o_ref[half:] = norm(a1)


def attention(queries, keys, values, carried):
    by_head = pl.BlockSpec((512, HD), lambda h: (0, h))
    return pl.pallas_call(
        attention_kernel,
        grid=(4,),
        in_specs=[by_head, by_head, by_head, pl.BlockSpec((HD, HD), lambda h: (h, 0))],
        out_specs=by_head,
        out_shape=jax.ShapeDtypeStruct((512, 512), BF16),
        compiler_params=pltpu.CompilerParams(vmem_limit_bytes=24 * 2**20),
        cost_estimate=pl.CostEstimate(flops=2**29, bytes_accessed=2**21, transcendentals=2048),
    )(queries, keys, values, carried)


def project_kernel(n_ref, w_ref, o_ref):
    n = n_ref[...]
    w = jnp.concatenate([w_ref[0, c, x] for x in range(X) for c in range(C)], axis=0)
    o = lax.dot_general(n, w, (((1,), (1,)), ((), ())), preferred_element_type=F32)
    o_ref[...] = o.astype(BF16)


def project(normed, weight):
    return pl.pallas_call(
        project_kernel,
        grid=(Z,),
        in_specs=[
            pl.BlockSpec((512, 512), lambda z: (0, 0)),
            pl.BlockSpec((1, C, X, 64, 512), lambda z: (z, 0, 0, 0, 0)),
        ],
        out_specs=pl.BlockSpec((512, 512), lambda z: (0, z)),
        out_shape=jax.ShapeDtypeStruct((512, 4096), BF16),
        compiler_params=pltpu.CompilerParams(vmem_limit_bytes=24 * 2**20),
        cost_estimate=pl.CostEstimate(flops=2**31, bytes_accessed=2**23, transcendentals=0),
    )(normed, weight)


def everywhere(part, axis, size):
    return lax.all_to_all(jnp.broadcast_to(part[None], (size,) + part.shape), axis, 0, 0)


def on_device(queries, keys, values, out_weight):
    plane = ("x", "core")
    w_x = everywhere(out_weight.T, "x", X)
    w_x, keys, values = lax.optimization_barrier((w_x, keys, values))
    weight = lax.all_gather(w_x.reshape(X * 64, 512), ("z", "core"), axis=0, tiled=True)
    weight = weight.reshape(Z, C, X, 64, 512)

    state = states(keys, values).reshape(8, 64, HD)
    pieces = lax.all_to_all(state, plane, 0, 0).astype(F32)
    place = lax.axis_index("z")
    running = jnp.zeros((64, HD), F32)
    earlier = []
    for i in range(8):
        earlier.append(running)
        running = running + pieces[i]
    earlier = jnp.stack(earlier)
    totals = everywhere(running.astype(BF16), "z", Z)
    mask = (jnp.arange(Z) < place)[:, None, None]
    before = jnp.sum(jnp.where(mask, totals, 0).astype(F32), axis=0)
    carried = (earlier + before[None]).astype(BF16)
    carried = lax.all_to_all(carried, plane, 0, 0).reshape(4 * HD, HD)

    normed = attention(queries, keys, values, carried)
    terms = project(normed, weight)
    return lax.psum_scatter(terms, "tp", scatter_dimension=0, tiled=True)


def solution(mesh):
    split = Mesh(mesh.devices.reshape(Z, X, C, Y), ("z", "x", "core", "tp"))
    ctx = ("z", "x", "core")
    placed = (P(ctx, "tp"), P(ctx, "tp"), P(ctx, "tp"), P("tp", ctx))
    return jax.shard_map(
        on_device, mesh=split, in_specs=placed, out_specs=P((*ctx, "tp"), None), check_vma=False
    )
```

time: 277 us -> 141 us (0.51)
  waiting for transfers between devices: 246 us -> 73.8 us
  blocking collectives: 0 us -> 21.5 us
  starting transfers between devices: 0.08 us -> 15.5 us
  matrix products: 11.4 us -> 0 us
  Pallas kernels: 0 us -> 8.23 us
  local copies, waits for them, and re-layouts: 2.59 us -> 7.86 us
    all_gather x2 -> x1, waiting for transfers between devices: 191 us -> 4.72 us  [on_device(): lax.all_gather(w_x.reshape(X * 64, 512), ('z', 'core'), axis=0, tiled=True)]
    all_to_all x0 -> x2, blocking collectives: none -> 21.5 us  [the longest x1 11.2 us: on_device(): carried = lax.all_to_all(carried, plane, 0, 0).reshape(4 * HD, HD)]
    all_to_all x0 -> x2, starting transfers between devices: none -> 15.4 us  [the longest x1 9.61 us: on_device(): pieces = lax.all_to_all(state, plane, 0, 0).astype(F32)]
    all_to_all x0 -> x2, waiting for transfers between devices: none -> 13.5 us  [the longest x1 8.21 us: everywhere(): lax.all_to_all(jnp.broadcast_to(part[None], (size,) + part.shape), axis,...]
    dot_general x4 -> x0, matrix products: 11.4 us -> none  [the longest x1 6.53 us: on_device(): jnp.dot(normed, lax.all_gather(out_weight, 'ctx', axis=1, tiled=True), pr...]
    pallas_call x0 -> x3, Pallas kernels: none -> 8.23 us  [the longest x1 3.98 us: project(): pl.pallas_call(project_kernel, grid=(Z,), in_specs=[pl.BlockSpec((512, 51...]
    unnamed x4 -> x18, local copies, waits for them, and re-layouts: 0.01 us -> 6.24 us
  transfers between devices with their start and end apart: 3 -> 4, of which waited for: 3 -> 4; matrix products, arithmetic and copies ran while one was open for 2% -> 1% of each run, Pallas kernels for 0% -> 3%
where the time goes in v1:
time: 141 us
  waiting for transfers between devices  73.8 us (52%)
  blocking collectives  21.5 us (15%)
  starting transfers between devices  15.5 us (11%)
  between operations  13.5 us (10%)
  Pallas kernels  8.23 us (6%)
  local copies, waits for them, and re-layouts  7.86 us (6%)
    reduce_scatter x1, waiting for transfers between devices, on_device(): return lax.psum_scatter(terms, 'tp', scatter_dimension=0, tiled=True)  55.6 us
    all_to_all x1, blocking collectives, on_device(): carried = lax.all_to_all(carried, plane, 0, 0).reshape(4 * HD, HD)  11.2 us
    all_to_all x1, blocking collectives, everywhere(): lax.all_to_all(jnp.broadcast_to(part[None], (size,) + part.shape), axis,...  10.3 us
    all_to_all x1, starting transfers between devices, on_device(): pieces = lax.all_to_all(state, plane, 0, 0).astype(F32)  9.61 us
    all_to_all x1, waiting for transfers between devices, everywhere(): lax.all_to_all(jnp.broadcast_to(part[None], (size,) + part.shape), axis,...  8.21 us
    unnamed x18, local copies, waits for them, and re-layouts  6.24 us
    all_to_all x1, starting transfers between devices, everywhere(): lax.all_to_all(jnp.broadcast_to(part[None], (size,) + part.shape), axis,...  5.8 us
    all_to_all x1, waiting for transfers between devices, on_device(): pieces = lax.all_to_all(state, plane, 0, 0).astype(F32)  5.28 us
  transfers between devices with their start and end apart: 4, of which 4 were waited for; matrix products, arithmetic and copies ran while one was open for 1% of the time, Pallas kernels for 3%

profile of v1, /device:TPU:1, one launch (start us, length us, event | category | flops | bytes accessed | tf_op | source)
XLA Modules:
  0.0 140.6 jit_solution(4684262304013062719)
XLA Ops:
  6.5 0.0 copy-start.5
  6.5 0.0 copy-start.3
  6.5 0.0 all-gather.2.cloned.1.call-start
  6.5 0.9 broadcast_in_dim.28
  7.5 10.3 %all_to_all.20 = bf16[4,64,512]{2,1,0:T(8,128)(2,1)} all-to-all(bf16[4,64,512]{2,1,0:T(8,128)(2,1)S(1)} %broadcast_in_dim.28), channel_id=1, replica_groups=mesh['z'=8,'x'=4,'core'=2,'tp'=8] {'x'}, dimensions={0} | all-to-all | bytes 524288 | tf_op jit(solution)/shard_map/all_to_all | solution.py:97
  17.8 0.0 all-gather.2.cloned.1.call-update
  17.8 0.0 copy-start.2
  17.8 1.0 copy-done.2
  18.8 0.0 copy-start.4
  18.8 1.0 copy-done.4
  19.9 0.0 copy-start.6
  19.9 1.0 shard_map.46
  20.9 9.6 %all-to-all-start.1 = ((bf16[8,64,128]{2,1,0:T(8,128)(2,1)}), bf16[8,64,128]{2,1,0:T(8,128)(2,1)S(1)}, u32[]{:S(2)}, u32[]{:S(2)}) async-start(bf16[8,64,128]{2,1,0:T(8,128)(2,1)} %bitcast.1), calls=%async_computation.1 | async-start | bytes 262144 | tf_op jit(solution)/shard_map/all_to_all | solution.py:108
  30.5 5.3 %all-to-all-done.1 = bf16[8,64,128]{2,1,0:T(8,128)(2,1)S(1)} async-done(((bf16[8,64,128]{2,1,0:T(8,128)(2,1)}), bf16[8,64,128]{2,1,0:T(8,128)(2,1)S(1)}, u32[]{:S(2)}, u32[]{:S(2)}) %all-to-all-start.1) | async-done | bytes 131104 | tf_op jit(solution)/shard_map/all_to_all | solution.py:108
  35.9 0.7 broadcast_in_dim.31
  36.5 5.8 %all-to-all-start.2 = ((bf16[8,64,128]{2,1,0:T(8,128)(2,1)}), bf16[8,64,128]{2,1,0:T(8,128)(2,1)S(1)}, u32[]{:S(2)}, u32[]{:S(2)}) async-start(bf16[8,64,128]{2,1,0:T(8,128)(2,1)} %broadcast_in_dim.31), calls=%async_computation.2 | async-start | bytes 262144 | tf_op jit(solution)/shard_map/all_to_all | solution.py:97
  42.4 0.0 reduce-scatter.2.cloned.1.call-start
  42.5 8.2 %all-to-all-done.2 = bf16[8,64,128]{2,1,0:T(8,128)(2,1)S(1)} async-done(((bf16[8,64,128]{2,1,0:T(8,128)(2,1)}), bf16[8,64,128]{2,1,0:T(8,128)(2,1)S(1)}, u32[]{:S(2)}, u32[]{:S(2)}) %all-to-all-start.2) | async-done | bytes 131104 | tf_op jit(solution)/shard_map/all_to_all | solution.py:97
  50.7 0.1 convert_reduce_fusion
  50.8 11.2 %all_to_all.21 = bf16[8,64,128]{2,1,0:T(8,128)(2,1)S(1)} all-to-all(bf16[8,64,128]{2,1,0:T(8,128)(2,1)S(1)} %add_convert_fusion), channel_id=1, replica_groups=mesh['z'=8,'x'=4,'core'=2,'tp'=8] {'x','core'}, dimensions={0} | all-to-all | bytes 262144 | tf_op jit(solution)/shard_map/all_to_all | solution.py:120
  62.0 0.0 copy-done.5
  62.0 0.0 copy-done.3
  62.0 0.0 copy-done.6
  62.0 3.2 %shard_map.47.n_ref = bf16[512,512]{1,0:T(8,128)(2,1)S(1)} custom-call(bf16[512,512]{1,0:T(8,128)(2,1)S(1)} %copy-done.6, bf16[512,512]{1,0:T(8,128)(2,1)S(1)} %copy-done.3, bf16[512,512]{1,0:T(8,128)(2,1)S(1)} %copy-done.5, bf16[512,128]{1,0:T(8,128)(2,1)S(1)} %bitcast.8), custom_call_target="tpu_custom_call" | custom-call | flops 536870912 | bytes 2097152 | tf_op jit(solution)/shard_map/pallas_call | solution.py:63
  65.3 4.7 %all-gather.2.cloned.1.call-done = bf16[4096,512]{1,0:T(8,128)(2,1)} async-done(((bf16[256,512]{1,0:T(8,128)(2,1)}), bf16[4096,512]{1,0:T(8,128)(2,1)}) %all-gather.2.cloned.1.call-update) | async-done | bytes 4194320 | tf_op jit(solution)/shard_map/all_gather | solution.py:104
  70.0 0.0 copy-start.1
  70.0 2.2 %copy-done.1 = bf16[4096,512]{1,0:T(8,128)(2,1)S(1)} copy-done((bf16[4096,512]{1,0:T(8,128)(2,1)S(1)}, bf16[4096,512]{1,0:T(8,128)(2,1)}, u32[]{:S(2)}) %copy-start.1) | copy-done | bytes 4194328
  72.2 4.0 %shard_map.48 = bf16[512,4096]{1,0:T(8,128)(2,1)S(1)} custom-call(bf16[512,512]{1,0:T(8,128)(2,1)S(1)} %shard_map.47.n_ref, bf16[8,2,4,64,512]{4,3,2,1,0:T(8,128)(2,1)S(1)} %bitcast.7), custom_call_target="tpu_custom_call" | custom-call | flops 2147483648 | bytes 8388608 | tf_op jit(solution)/shard_map/pallas_call | solution.py:82
  76.2 0.0 copy-start
  76.2 1.9 %copy-done = bf16[512,4096]{1,0:T(8,128)(2,1)} copy-done((bf16[512,4096]{1,0:T(8,128)(2,1)}, bf16[512,4096]{1,0:T(8,128)(2,1)S(1)}, u32[]{:S(2)}) %copy-start) | copy-done | bytes 4194328
  78.1 0.0 reduce-scatter.2.cloned.1.call-update
  78.1 55.6 %reduce-scatter.2.cloned.1.call-done = bf16[64,4096]{1,0:T(8,128)(2,1)} async-done(((bf16[512,4096]{1,0:T(8,128)(2,1)}), bf16[64,4096]{1,0:T(8,128)(2,1)}) %reduce-scatter.2.cloned.1.call-update) | async-done | bytes 524304 | tf_op jit(solution)/shard_map/reduce_scatter | solution.py:124
  (11 shorter events, 0.1 us)
Async XLA Ops:
  6.5 55.5 %copy-start.5 = (bf16[512,512]{1,0:T(8,128)(2,1)S(1)}, bf16[512,512]{1,0:T(8,128)(2,1)}, u32[]{:S(2)}) copy-start(bf16[512,512]{1,0:T(8,128)(2,1)} %v_ref.1) | copy-start | bytes 1572868
  6.5 55.5 %copy-start.3 = (bf16[512,512]{1,0:T(8,128)(2,1)S(1)}, bf16[512,512]{1,0:T(8,128)(2,1)}, u32[]{:S(2)}) copy-start(bf16[512,512]{1,0:T(8,128)(2,1)} %k_ref.1) | copy-start | bytes 1572868
  6.5 63.4 %all-gather.2.cloned.1.call-start = ((), (), s32[]{:S(2)}) async-start(), calls=%async_computation.5 | async-start | bytes 4456448 | tf_op jit(solution)/shard_map/all_gather | solution.py:104
  17.8 1.0 copy-start.2
  18.8 1.0 copy-start.4
  19.9 42.1 %copy-start.6 = (bf16[512,512]{1,0:T(8,128)(2,1)S(1)}, bf16[512,512]{1,0:T(8,128)(2,1)}, u32[]{:S(2)}) copy-start(bf16[512,512]{1,0:T(8,128)(2,1)} %q_ref.1) | copy-start | bytes 1572868
  20.9 14.9 %all-to-all-start.1 = ((bf16[8,64,128]{2,1,0:T(8,128)(2,1)}), bf16[8,64,128]{2,1,0:T(8,128)(2,1)S(1)}, u32[]{:S(2)}, u32[]{:S(2)}) async-start(bf16[8,64,128]{2,1,0:T(8,128)(2,1)} %bitcast.1), calls=%async_computation.1 | async-start | bytes 262144 | tf_op jit(solution)/shard_map/all_to_all | solution.py:108
  36.5 14.1 %all-to-all-start.2 = ((bf16[8,64,128]{2,1,0:T(8,128)(2,1)}), bf16[8,64,128]{2,1,0:T(8,128)(2,1)S(1)}, u32[]{:S(2)}, u32[]{:S(2)}) async-start(bf16[8,64,128]{2,1,0:T(8,128)(2,1)} %broadcast_in_dim.31), calls=%async_computation.2 | async-start | bytes 262144 | tf_op jit(solution)/shard_map/all_to_all | solution.py:97
  42.4 91.4 %reduce-scatter.2.cloned.1.call-start = ((), (), s32[]{:S(2)}) async-start(), calls=%async_computation.6 | async-start | bytes 4718592 | tf_op jit(solution)/shard_map/reduce_scatter | solution.py:124
  70.0 2.2 %copy-start.1 = (bf16[4096,512]{1,0:T(8,128)(2,1)S(1)}, bf16[4096,512]{1,0:T(8,128)(2,1)}, u32[]{:S(2)}) copy-start(bf16[4096,512]{1,0:T(8,128)(2,1)} %all-gather.2.cloned.1.call-done) | copy-start | bytes 12582916
  76.2 2.0 %copy-start = (bf16[512,4096]{1,0:T(8,128)(2,1)}, bf16[512,4096]{1,0:T(8,128)(2,1)S(1)}, u32[]{:S(2)}) copy-start(bf16[512,4096]{1,0:T(8,128)(2,1)S(1)} %shard_map.48) | copy-start | bytes 12582916
Sparse Core Ops, SparseCore 0:
  17.9 52.0 all-gather.1
  78.3 55.4 reduce-scatter.1

commit v2 on v1

v2 whole, which is shorter than its diff:
```python
import jax
import jax.numpy as jnp
from jax import lax
from jax.experimental import pallas as pl
from jax.experimental.pallas import tpu as pltpu
from jax.sharding import Mesh, PartitionSpec as P

HD = 128
F32 = jnp.float32
BF16 = jnp.bfloat16
Z, X, C, Y = 8, 4, 2, 8
MIB = 2**20
NT = (((1,), (1,)), ((), ()))
TN = (((0,), (0,)), ((), ()))
VMEM = pl.BlockSpec(memory_space=pltpu.VMEM)
SMEM = pl.BlockSpec(memory_space=pltpu.SMEM)


def call(kernel, out_shape, operands, flops, moved, scalars=0, vmem=24):
    return pl.pallas_call(
        kernel,
        out_shape=out_shape,
        in_specs=[SMEM] * scalars + [VMEM] * (len(operands) - scalars),
        out_specs=jax.tree.map(lambda _: VMEM, out_shape),
        compiler_params=pltpu.CompilerParams(vmem_limit_bytes=vmem * MIB),
        cost_estimate=pl.CostEstimate(flops=flops, bytes_accessed=moved, transcendentals=0),
    )(*operands)


def state_kernel(k_ref, v_ref, s_ref):
    for h in range(4):
        cols = slice(h * HD, (h + 1) * HD)
        s = lax.dot_general(k_ref[:, cols], v_ref[:, cols], TN, preferred_element_type=F32)
        s_ref[cols, :] = s.astype(BF16)


def plane_kernel(p_ref, e_ref, t_ref):
    running = jnp.zeros(p_ref.shape[1:], F32)
    for i in range(C * X):
        e_ref[i] = running
        running = running + p_ref[i].astype(F32)
    total = running.astype(BF16)
    for i in range(Z):
        t_ref[i] = total


def carry_kernel(z_ref, t_ref, e_ref, c_ref):
    z = z_ref[0]
    before = jnp.zeros(t_ref.shape[1:], F32)
    for i in range(Z - 1):
        before = before + jnp.where(i < z, t_ref[i].astype(F32), 0.0)
    for i in range(C * X):
        c_ref[i] = (e_ref[i] + before).astype(BF16)


def attention_kernel(q_ref, k_ref, v_ref, c_ref, o_ref):
    half = 256
    row = lax.broadcasted_iota(jnp.int32, (half, half), 0)
    col = lax.broadcasted_iota(jnp.int32, (half, half), 1)
    causal = row >= col

    def masked(q, k):
        s = lax.dot_general(q, k, NT, preferred_element_type=F32)
        return jnp.where(causal, s, 0.0).astype(BF16)

    def norm(a):
        r = lax.rsqrt(jnp.mean(a * a, axis=-1, keepdims=True) + 1e-06)
        return (a * r).astype(BF16)

    for h in range(4):
        cols = slice(h * HD, (h + 1) * HD)
        c = c_ref[cols]
        q0, q1 = q_ref[:half, cols], q_ref[half:, cols]
        k0, k1 = k_ref[:half, cols], k_ref[half:, cols]
        v0, v1 = v_ref[:half, cols], v_ref[half:, cols]
        a0 = jnp.dot(q0, c, preferred_element_type=F32)
        a0 += jnp.dot(masked(q0, k0), v0, preferred_element_type=F32)
        o_ref[:half, cols] = norm(a0)
        a1 = jnp.dot(q1, c, preferred_element_type=F32)
        s10 = lax.dot_general(q1, k0, NT, preferred_element_type=F32).astype(BF16)
        a1 += jnp.dot(s10, v0, preferred_element_type=F32)
        a1 += jnp.dot(masked(q1, k1), v1, preferred_element_type=F32)
        o_ref[half:, cols] = norm(a1)


SHIFTS = (4, 3, 5, 2, 6, 1, 7, 0)


def project_kernel(y_ref, n_ref, w_ref, up_ref, down_ref, *refs):
    rest_refs, rows = refs[:-1], refs[-1]
    z = pl.program_id(0)

    @pl.when(z == 0)
    def _():
        for i, shift in enumerate(SHIFTS):
            at = pl.multiple_of(lax.rem(y_ref[0] + shift, Y) * 64, 64)
            rows[i * 64 : (i + 1) * 64] = n_ref[pl.ds(at, 64)]

    w = jnp.concatenate([w_ref[0, c, x] for x in range(X) for c in range(C)], axis=0)
    o = lax.dot_general(rows[...], w, NT, preferred_element_type=F32).astype(BF16)

    @pl.when(z < Z // 2)
    def _():
        up_ref[...] = o[:64]

    @pl.when(z >= Z // 2)
    def _():
        down_ref[...] = o[:64]

    for i, ref in enumerate(rest_refs):
        ref[...] = o[(i + 1) * 64 : (i + 2) * 64]


def project(y, normed, weight):
    half = Z // 2
    out = pl.BlockSpec((64, 512), lambda z: (0, z))
    up = pl.BlockSpec((64, 512), lambda z: (0, jnp.minimum(z, half - 1)))
    down = pl.BlockSpec((64, 512), lambda z: (0, jnp.maximum(z - half, 0)))
    return pl.pallas_call(
        project_kernel,
        grid=(Z,),
        in_specs=[
            SMEM,
            pl.BlockSpec((512, 512), lambda z: (0, 0)),
            pl.BlockSpec((1, C, X, 64, 512), lambda z: (z, 0, 0, 0, 0)),
        ],
        out_specs=[up, down] + [out] * 7,
        out_shape=[shape(64, 2048)] * 2 + [shape(64, 4096)] * 7,
        scratch_shapes=[pltpu.VMEM((512, 512), BF16)],
        compiler_params=pltpu.CompilerParams(vmem_limit_bytes=56 * MIB),
        cost_estimate=pl.CostEstimate(flops=2**31, bytes_accessed=8 * MIB, transcendentals=0),
    )(y, normed, weight)


def everywhere(part, axis, size):
    return lax.all_to_all(jnp.broadcast_to(part[None], (size,) + part.shape), axis, 0, 0)


def shape(*dims, dtype=BF16):
    return jax.ShapeDtypeStruct(dims, dtype)


def add(a, b):
    return (a.astype(F32) + b.astype(F32)).astype(BF16)


def on_device(queries, keys, values, out_weight):
    plane = ("x", "core")
    z, y = (lax.axis_index(a).astype(jnp.int32)[None] for a in ("z", "tp"))

    w_x = everywhere(out_weight.T, "x", X)
    state = call(state_kernel, shape(4 * HD, HD), (keys, values), 2**26, MIB, vmem=16)
    state, w_x = lax.optimization_barrier((state, w_x))
    weight = lax.all_gather(w_x.reshape(X * 64, 512), ("z", "core"), axis=0, tiled=True)
    weight = weight.reshape(Z, C, X, 64, 512)
    pieces = lax.all_to_all(state.reshape(8, 64, HD), plane, 0, 0)
    earlier, total = call(
        plane_kernel, (shape(8, 64, HD, dtype=F32), shape(8, 64, HD)), (pieces,), 2**17, 2**19, vmem=8
    )
    totals = lax.all_to_all(total, "z", 0, 0)
    carried = call(carry_kernel, shape(8, 64, HD), (z, totals, earlier), 2**18, 2**19, 1, vmem=8)
    carried = lax.all_to_all(carried, plane, 0, 0).reshape(4 * HD, HD)
    normed = call(
        attention_kernel, shape(512, 512), (queries, keys, values, carried), 2**29, 2 * MIB
    )

    up, down, u3, d3, u2, d2, u1, d1, mine = project(y, normed, weight)
    ring_up = [(i, (i + 1) % Y) for i in range(Y)]
    ring_down = [(i, (i - 1) % Y) for i in range(Y)]
    up = lax.ppermute(up, "tp", ring_up)
    down = lax.ppermute(down, "tp", ring_down)
    up = add(u3, jnp.pad(up, ((0, 0), (0, 2048))))
    down = add(d3, jnp.pad(down, ((0, 0), (2048, 0))))
    up = lax.ppermute(up, "tp", ring_up)
    down = lax.ppermute(down, "tp", ring_down)
    for u, d in ((u2, d2), (u1, d1)):
        up = lax.ppermute(add(u, up), "tp", ring_up)
        down = lax.ppermute(add(d, down), "tp", ring_down)
    return (mine.astype(F32) + up.astype(F32) + down.astype(F32)).astype(BF16)


def solution(mesh):
    split = Mesh(mesh.devices.reshape(Z, X, C, Y), ("z", "x", "core", "tp"))
    ctx = ("z", "x", "core")
    placed = (P(ctx, "tp"), P(ctx, "tp"), P(ctx, "tp"), P("tp", ctx))
    return jax.shard_map(
        on_device, mesh=split, in_specs=placed, out_specs=P((*ctx, "tp"), None), check_vma=False
    )
```

time: 141 us -> 153 us (1.085)
  the two profiles are of different devices: /device:TPU:1 before, /device:TPU:4 now
where the time goes in v2:
time: 153 us; the launch traced here: 152 us
  waiting for transfers between devices  54.1 us (35%)
  starting transfers between devices  50.2 us (33%)
  between operations  13.6 us (9%)
  Pallas kernels  12.3 us (8%)
  blocking collectives  8.78 us (6%)
  local copies, waits for them, and re-layouts  8.29 us (5%)
  other arithmetic  4.8 us (3%)
    ppermute x2, waiting for transfers between devices, on_device(): down = lax.ppermute(add(d, down), 'tp', ring_down)  14.6 us
    ppermute x2, waiting for transfers between devices, on_device(): down = lax.ppermute(down, 'tp', ring_down)  12.1 us
    ppermute x2, starting transfers between devices, on_device(): down = lax.ppermute(add(d, down), 'tp', ring_down)  11.2 us
    all_to_all x1, waiting for transfers between devices, on_device(): totals = lax.all_to_all(total, 'z', 0, 0)  10.9 us
    ppermute x2, starting transfers between devices, on_device(): down = lax.ppermute(down, 'tp', ring_down)  10.1 us
    all_to_all x1, starting transfers between devices, everywhere(): lax.all_to_all(jnp.broadcast_to(part[None], (size,) + part.shape), axis,...  9.26 us
    all_to_all x1, blocking collectives, on_device(): pieces = lax.all_to_all(state.reshape(8, 64, HD), plane, 0, 0)  8.78 us
    pallas_call x1, Pallas kernels, project(): pl.pallas_call(project_kernel, grid=(Z,), in_specs=[SMEM, pl.BlockSpec((5...  8.53 us
  transfers between devices with their start and end apart: 12, of which 9 were waited for; matrix products, arithmetic and copies ran while one was open for 3% of the time, Pallas kernels for 2%

profile of v2, /device:TPU:4, one launch (start us, length us, event | category | flops | bytes accessed | tf_op | source)
XLA Modules:
  0.0 152.1 jit_solution(14006092375573838533)
XLA Ops:
  6.5 1.6 %broadcast_in_dim.14 = bf16[4,64,512]{2,1,0:T(8,128)(2,1)} broadcast(bf16[64,512]{1,0:T(8,128)(2,1)} %bitcast.10), dimensions={1,2} | broadcast | bytes 327680 | tf_op jit(solution)/shard_map/broadcast_in_dim | solution.py:136
  8.1 9.3 %all-to-all-start = ((bf16[4,64,512]{2,1,0:T(8,128)(2,1)}), bf16[4,64,512]{2,1,0:T(8,128)(2,1)S(1)}, u32[]{:S(2)}, u32[]{:S(2)}) async-start(bf16[4,64,512]{2,1,0:T(8,128)(2,1)} %broadcast_in_dim.14), calls=%async_computation | async-start | bytes 524288 | tf_op jit(solution)/shard_map/all_to_all | solution.py:136
  17.4 1.0 copy-done
  18.4 1.0 copy-done.2
  19.8 1.3 all-to-all-done
  21.8 8.8 %all_to_all.20.p_ref = bf16[8,64,128]{2,1,0:T(8,128)(2,1)S(1)} all-to-all(bf16[8,64,128]{2,1,0:T(8,128)(2,1)S(1)} %bitcast.8), channel_id=1, replica_groups=mesh['z'=8,'x'=4,'core'=2,'tp'=8] {'x','core'}, dimensions={0} | all-to-all | bytes 262144 | tf_op jit(solution)/shard_map/all_to_all | solution.py:156
  31.3 5.9 %all-to-all-start.2 = ((bf16[8,64,128]{2,1,0:T(8,128)(2,1)}), bf16[8,64,128]{2,1,0:T(8,128)(2,1)S(1)}, u32[]{:S(2)}, u32[]{:S(2)}) async-start(bf16[8,64,128]{2,1,0:T(8,128)(2,1)} %get-tuple-element.19), calls=%async_computation.2 | async-start | bytes 262144 | tf_op jit(solution)/shard_map/all_to_all | solution.py:160
  37.1 10.9 %all-to-all-done.2.t_ref = bf16[8,64,128]{2,1,0:T(8,128)(2,1)S(1)} async-done(((bf16[8,64,128]{2,1,0:T(8,128)(2,1)}), bf16[8,64,128]{2,1,0:T(8,128)(2,1)S(1)}, u32[]{:S(2)}, u32[]{:S(2)}) %all-to-all-start.2) | async-done | bytes 131104 | tf_op jit(solution)/shard_map/all_to_all | solution.py:160
  48.7 6.1 %all-to-all-start.3 = ((bf16[8,64,128]{2,1,0:T(8,128)(2,1)}), bf16[8,64,128]{2,1,0:T(8,128)(2,1)S(1)}, u32[]{:S(2)}, u32[]{:S(2)}) async-start(bf16[8,64,128]{2,1,0:T(8,128)(2,1)} %shard_map.48), calls=%async_computation.3 | async-start | bytes 262144 | tf_op jit(solution)/shard_map/all_to_all | solution.py:162
  54.8 3.4 %all-to-all-done.3 = bf16[8,64,128]{2,1,0:T(8,128)(2,1)S(1)} async-done(((bf16[8,64,128]{2,1,0:T(8,128)(2,1)}), bf16[8,64,128]{2,1,0:T(8,128)(2,1)S(1)}, u32[]{:S(2)}, u32[]{:S(2)}) %all-to-all-start.3) | async-done | bytes 131104 | tf_op jit(solution)/shard_map/all_to_all | solution.py:162
  58.3 1.0 copy-done.1
  59.3 1.0 copy-done.3
  60.3 1.1 copy-done.4
  61.4 2.0 %shard_map.49.n_ref = bf16[512,512]{1,0:T(8,128)(2,1)S(1)} custom-call(bf16[512,512]{1,0:T(8,128)(2,1)S(1)} %copy-done.4, bf16[512,512]{1,0:T(8,128)(2,1)S(1)} %copy-done.1, bf16[512,512]{1,0:T(8,128)(2,1)S(1)} %copy-done.3, bf16[512,128]{1,0:T(8,128)(2,1)S(1)} %bitcast.7), custom_call_target="tpu_custom_call" | custom-call | flops 536870912 | bytes 2097152 | tf_op jit(solution)/shard_map/pallas_call | solution.py:20
  64.2 6.3 %all-gather.2.cloned.1.call-done = bf16[4096,512]{1,0:T(8,128)(2,1)} async-done(((bf16[256,512]{1,0:T(8,128)(2,1)}), bf16[4096,512]{1,0:T(8,128)(2,1)}) %all-gather.2.cloned.1.call-update) | async-done | bytes 4194320 | tf_op jit(solution)/shard_map/all_gather | solution.py:154
  70.6 8.5 %shard_map.50 = (bf16[64,2048]{1,0:T(8,128)(2,1)}, bf16[64,2048]{1,0:T(8,128)(2,1)}, bf16[64,4096]{1,0:T(8,128)(2,1)}, bf16[64,4096]{1,0:T(8,128)(2,1)}, bf16[64...) custom-call(s32[1]{0:T(128)} %bitcast.y_ref, ...), custom_call_target="tpu_custom_call" | custom-call | flops 2147483648 | bytes 8388608 | tf_op jit(solution)/shard_map/pallas_call | solution.py:119
  79.1 4.6 %collective-permute-start.4 = (bf16[64,2048]{1,0:T(8,128)(2,1)}, bf16[64,2048]{1,0:T(8,128)(2,1)S(1)}, u32[]{:S(2)}, u32[]{:S(2)}) collective-permute-start(bf16[64,2048]{1,0:T(8,128)(2,1)} %get-tuple-element.30), channel_id=1, source_target_pairs={{0,7},{1,0},{2,1},{3,2},{4,3},{5,4},{6,5},{7,6},{8,15},{9,8},{10,9... | collective-permute-start | bytes 786440 | tf_op jit(solution)/shard_map/ppermute | solution.py:171
  83.8 1.9 %collective-permute-start = (bf16[64,2048]{1,0:T(8,128)(2,1)}, bf16[64,2048]{1,0:T(8,128)(2,1)S(1)}, u32[]{:S(2)}, u32[]{:S(2)}) collective-permute-start(bf16[64,2048]{1,0:T(8,128)(2,1)} %get-tuple-element.26), channel_id=1, source_target_pairs={{0,1},{1,2},{2,3},{3,4},{4,5},{5,6},{6,7},{7,0},{8,9},{9,10},{10,1... | collective-permute-start | bytes 786440 | tf_op jit(solution)/shard_map/ppermute | solution.py:170
  85.7 4.3 %collective-permute-done.4 = bf16[64,2048]{1,0:T(8,128)(2,1)S(1)} collective-permute-done((bf16[64,2048]{1,0:T(8,128)(2,1)}, bf16[64,2048]{1,0:T(8,128)(2,1)S(1)}, u32[]{:S(2)}, u32[]{:S(2)}) %collective-permute-start.4) | collective-permute-done | bytes 262176 | tf_op jit(solution)/shard_map/ppermute | solution.py:171
  90.0 1.2 add_convert_fusion.3
  91.2 5.5 %collective-permute-start.5 = (bf16[64,4096]{1,0:T(8,128)(2,1)S(1)}, bf16[64,4096]{1,0:T(8,128)(2,1)S(1)}, u32[]{:S(2)}, u32[]{:S(2)}) collective-permute-start(bf16[64,4096]{1,0:T(8,128)(2,1)S(1)} %add_convert_fusion.3), channel_id=1, source_target_pairs={{0,7},{1,0},{2,1},{3,2},{4,3},{5,4},{6,5},{7,6},{8,15},{9,8},{10,9... | collective-permute-start | bytes 1572872 | tf_op jit(solution)/shard_map/ppermute | solution.py:175
  96.7 1.1 add_convert_fusion.6
  97.8 1.9 %collective-permute-start.1 = (bf16[64,4096]{1,0:T(8,128)(2,1)S(1)}, bf16[64,4096]{1,0:T(8,128)(2,1)S(1)}, u32[]{:S(2)}, u32[]{:S(2)}) collective-permute-start(bf16[64,4096]{1,0:T(8,128)(2,1)S(1)} %add_convert_fusion.6), channel_id=1, source_target_pairs={{0,1},{1,2},{2,3},{3,4},{4,5},{5,6},{6,7},{7,0},{8,9},{9,10},{10,1... | collective-permute-start | bytes 1572872 | tf_op jit(solution)/shard_map/ppermute | solution.py:174
  99.8 7.7 %collective-permute-done.5 = bf16[64,4096]{1,0:T(8,128)(2,1)S(1)} collective-permute-done((bf16[64,4096]{1,0:T(8,128)(2,1)S(1)}, bf16[64,4096]{1,0:T(8,128)(2,1)S(1)}, u32[]{:S(2)}, u32[]{:S(2)}) %collective-permute-start.5) | collective-permute-done | bytes 524320 | tf_op jit(solution)/shard_map/ppermute | solution.py:175
  107.5 1.2 add_convert_fusion.2
  108.7 5.6 %collective-permute-start.6 = (bf16[64,4096]{1,0:T(8,128)(2,1)S(1)}, bf16[64,4096]{1,0:T(8,128)(2,1)S(1)}, u32[]{:S(2)}, u32[]{:S(2)}) collective-permute-start(bf16[64,4096]{1,0:T(8,128)(2,1)S(1)} %add_convert_fusion.2), channel_id=1, source_target_pairs={{0,7},{1,0},{2,1},{3,2},{4,3},{5,4},{6,5},{7,6},{8,15},{9,8},{10,9... | collective-permute-start | bytes 1572872 | tf_op jit(solution)/shard_map/ppermute | solution.py:178
  114.4 1.9 %collective-permute-start.2 = (bf16[64,4096]{1,0:T(8,128)(2,1)S(1)}, bf16[64,4096]{1,0:T(8,128)(2,1)S(1)}, u32[]{:S(2)}, u32[]{:S(2)}) collective-permute-start(bf16[64,4096]{1,0:T(8,128)(2,1)S(1)} %add_convert_fusion.5), channel_id=1, source_target_pairs={{0,1},{1,2},{2,3},{3,4},{4,5},{5,6},{6,7},{7,0},{8,9},{9,10},{10,1... | collective-permute-start | bytes 1572872 | tf_op jit(solution)/shard_map/ppermute | solution.py:177
  116.3 7.8 %collective-permute-done.6 = bf16[64,4096]{1,0:T(8,128)(2,1)S(1)} collective-permute-done((bf16[64,4096]{1,0:T(8,128)(2,1)S(1)}, bf16[64,4096]{1,0:T(8,128)(2,1)S(1)}, u32[]{:S(2)}, u32[]{:S(2)}) %collective-permute-start.6) | collective-permute-done | bytes 524320 | tf_op jit(solution)/shard_map/ppermute | solution.py:178
  124.2 5.6 %collective-permute-start.7 = (bf16[64,4096]{1,0:T(8,128)(2,1)S(1)}, bf16[64,4096]{1,0:T(8,128)(2,1)S(1)}, u32[]{:S(2)}, u32[]{:S(2)}) collective-permute-start(bf16[64,4096]{1,0:T(8,128)(2,1)S(1)} %add_convert_fusion.1), channel_id=1, source_target_pairs={{0,7},{1,0},{2,1},{3,2},{4,3},{5,4},{6,5},{7,6},{8,15},{9,8},{10,9... | collective-permute-start | bytes 1572872 | tf_op jit(solution)/shard_map/ppermute | solution.py:178
  130.0 1.9 %collective-permute-start.3 = (bf16[64,4096]{1,0:T(8,128)(2,1)S(1)}, bf16[64,4096]{1,0:T(8,128)(2,1)S(1)}, u32[]{:S(2)}, u32[]{:S(2)}) collective-permute-start(bf16[64,4096]{1,0:T(8,128)(2,1)S(1)} %add_convert_fusion.4), channel_id=1, source_target_pairs={{0,1},{1,2},{2,3},{3,4},{4,5},{5,6},{6,7},{7,0},{8,9},{9,10},{10,1... | collective-permute-start | bytes 1572872 | tf_op jit(solution)/shard_map/ppermute | solution.py:177
  131.9 6.8 %collective-permute-done.7 = bf16[64,4096]{1,0:T(8,128)(2,1)S(1)} collective-permute-done((bf16[64,4096]{1,0:T(8,128)(2,1)S(1)}, bf16[64,4096]{1,0:T(8,128)(2,1)S(1)}, u32[]{:S(2)}, u32[]{:S(2)}) %collective-permute-start.7) | collective-permute-done | bytes 524320 | tf_op jit(solution)/shard_map/ppermute | solution.py:178
  138.8 5.5 %collective-permute-done.3 = bf16[64,4096]{1,0:T(8,128)(2,1)S(1)} collective-permute-done((bf16[64,4096]{1,0:T(8,128)(2,1)S(1)}, bf16[64,4096]{1,0:T(8,128)(2,1)S(1)}, u32[]{:S(2)}, u32[]{:S(2)}) %collective-permute-start.3) | collective-permute-done | bytes 524320 | tf_op jit(solution)/shard_map/ppermute | solution.py:177
  (29 shorter events, 4.6 us)
Async XLA Ops:
  8.1 13.0 %all-to-all-start = ((bf16[4,64,512]{2,1,0:T(8,128)(2,1)}), bf16[4,64,512]{2,1,0:T(8,128)(2,1)S(1)}, u32[]{:S(2)}, u32[]{:S(2)}) async-start(bf16[4,64,512]{2,1,0:T(8,128)(2,1)} %broadcast_in_dim.14), calls=%async_computation | async-start | bytes 524288 | tf_op jit(solution)/shard_map/all_to_all | solution.py:136
  17.4 53.2 %all-gather.2.cloned.1.call-start = ((), (), s32[]{:S(2)}) async-start(), calls=%async_computation.4 | async-start | bytes 4456448 | tf_op jit(solution)/shard_map/all_gather | solution.py:154
  17.4 1.0 copy-start
  18.4 1.0 copy-start.2
  21.1 0.7 copy-start.6
  31.3 16.7 %all-to-all-start.2 = ((bf16[8,64,128]{2,1,0:T(8,128)(2,1)}), bf16[8,64,128]{2,1,0:T(8,128)(2,1)S(1)}, u32[]{:S(2)}, u32[]{:S(2)}) async-start(bf16[8,64,128]{2,1,0:T(8,128)(2,1)} %get-tuple-element.19), calls=%async_computation.2 | async-start | bytes 262144 | tf_op jit(solution)/shard_map/all_to_all | solution.py:160
  48.7 9.6 %all-to-all-start.3 = ((bf16[8,64,128]{2,1,0:T(8,128)(2,1)}), bf16[8,64,128]{2,1,0:T(8,128)(2,1)S(1)}, u32[]{:S(2)}, u32[]{:S(2)}) async-start(bf16[8,64,128]{2,1,0:T(8,128)(2,1)} %shard_map.48), calls=%async_computation.3 | async-start | bytes 262144 | tf_op jit(solution)/shard_map/all_to_all | solution.py:162
  58.3 1.1 copy-start.1
  59.3 1.0 copy-start.3
  60.3 1.1 copy-start.4
  63.4 0.8 copy-start.5
  79.1 35.2 %copy-start.9 = (bf16[64,4096]{1,0:T(8,128)(2,1)S(1)}, bf16[64,4096]{1,0:T(8,128)(2,1)}, u32[]{:S(2)}) copy-start(bf16[64,4096]{1,0:T(8,128)(2,1)} %get-tuple-element.24) | copy-start | bytes 1572868
  79.1 45.0 %copy-start.8 = (bf16[64,4096]{1,0:T(8,128)(2,1)S(1)}, bf16[64,4096]{1,0:T(8,128)(2,1)}, u32[]{:S(2)}) copy-start(bf16[64,4096]{1,0:T(8,128)(2,1)} %get-tuple-element.27) | copy-start | bytes 1572868
  79.1 50.8 %copy-start.7 = (bf16[64,4096]{1,0:T(8,128)(2,1)S(1)}, bf16[64,4096]{1,0:T(8,128)(2,1)}, u32[]{:S(2)}) copy-start(bf16[64,4096]{1,0:T(8,128)(2,1)} %get-tuple-element.23) | copy-start | bytes 1572868
  79.1 10.9 %collective-permute-start.4 = (bf16[64,2048]{1,0:T(8,128)(2,1)}, bf16[64,2048]{1,0:T(8,128)(2,1)S(1)}, u32[]{:S(2)}, u32[]{:S(2)}) collective-permute-start(bf16[64,2048]{1,0:T(8,128)(2,1)} %get-tuple-element.30), channel_id=1, source_target_pairs={{0,7},{1,0},{2,1},{3,2},{4,3},{5,4},{6,5},{7,6},{8,15},{9,8},{10,9... | collective-permute-start | bytes 786440 | tf_op jit(solution)/shard_map/ppermute | solution.py:171
  83.8 13.0 %collective-permute-start = (bf16[64,2048]{1,0:T(8,128)(2,1)}, bf16[64,2048]{1,0:T(8,128)(2,1)S(1)}, u32[]{:S(2)}, u32[]{:S(2)}) collective-permute-start(bf16[64,2048]{1,0:T(8,128)(2,1)} %get-tuple-element.26), channel_id=1, source_target_pairs={{0,1},{1,2},{2,3},{3,4},{4,5},{5,6},{6,7},{7,0},{8,9},{9,10},{10,1... | collective-permute-start | bytes 786440 | tf_op jit(solution)/shard_map/ppermute | solution.py:170
  90.0 54.2 %copy-start.10 = (bf16[64,4096]{1,0:T(8,128)(2,1)S(1)}, bf16[64,4096]{1,0:T(8,128)(2,1)}, u32[]{:S(2)}) copy-start(bf16[64,4096]{1,0:T(8,128)(2,1)} %get-tuple-element.22) | copy-start | bytes 1572868
  91.2 16.3 %collective-permute-start.5 = (bf16[64,4096]{1,0:T(8,128)(2,1)S(1)}, bf16[64,4096]{1,0:T(8,128)(2,1)S(1)}, u32[]{:S(2)}, u32[]{:S(2)}) collective-permute-start(bf16[64,4096]{1,0:T(8,128)(2,1)S(1)} %add_convert_fusion.3), channel_id=1, source_target_pairs={{0,7},{1,0},{2,1},{3,2},{4,3},{5,4},{6,5},{7,6},{8,15},{9,8},{10,9... | collective-permute-start | bytes 1572872 | tf_op jit(solution)/shard_map/ppermute | solution.py:175
  97.8 16.4 %collective-permute-start.1 = (bf16[64,4096]{1,0:T(8,128)(2,1)S(1)}, bf16[64,4096]{1,0:T(8,128)(2,1)S(1)}, u32[]{:S(2)}, u32[]{:S(2)}) collective-permute-start(bf16[64,4096]{1,0:T(8,128)(2,1)S(1)} %add_convert_fusion.6), channel_id=1, source_target_pairs={{0,1},{1,2},{2,3},{3,4},{4,5},{5,6},{6,7},{7,0},{8,9},{9,10},{10,1... | collective-permute-start | bytes 1572872 | tf_op jit(solution)/shard_map/ppermute | solution.py:174
  108.7 15.5 %collective-permute-start.6 = (bf16[64,4096]{1,0:T(8,128)(2,1)S(1)}, bf16[64,4096]{1,0:T(8,128)(2,1)S(1)}, u32[]{:S(2)}, u32[]{:S(2)}) collective-permute-start(bf16[64,4096]{1,0:T(8,128)(2,1)S(1)} %add_convert_fusion.2), channel_id=1, source_target_pairs={{0,7},{1,0},{2,1},{3,2},{4,3},{5,4},{6,5},{7,6},{8,15},{9,8},{10,9... | collective-permute-start | bytes 1572872 | tf_op jit(solution)/shard_map/ppermute | solution.py:178
  114.4 15.4 %collective-permute-start.2 = (bf16[64,4096]{1,0:T(8,128)(2,1)S(1)}, bf16[64,4096]{1,0:T(8,128)(2,1)S(1)}, u32[]{:S(2)}, u32[]{:S(2)}) collective-permute-start(bf16[64,4096]{1,0:T(8,128)(2,1)S(1)} %add_convert_fusion.5), channel_id=1, source_target_pairs={{0,1},{1,2},{2,3},{3,4},{4,5},{5,6},{6,7},{7,0},{8,9},{9,10},{10,1... | collective-permute-start | bytes 1572872 | tf_op jit(solution)/shard_map/ppermute | solution.py:177
  124.2 14.5 %collective-permute-start.7 = (bf16[64,4096]{1,0:T(8,128)(2,1)S(1)}, bf16[64,4096]{1,0:T(8,128)(2,1)S(1)}, u32[]{:S(2)}, u32[]{:S(2)}) collective-permute-start(bf16[64,4096]{1,0:T(8,128)(2,1)S(1)} %add_convert_fusion.1), channel_id=1, source_target_pairs={{0,7},{1,0},{2,1},{3,2},{4,3},{5,4},{6,5},{7,6},{8,15},{9,8},{10,9... | collective-permute-start | bytes 1572872 | tf_op jit(solution)/shard_map/ppermute | solution.py:178
  130.0 14.2 %collective-permute-start.3 = (bf16[64,4096]{1,0:T(8,128)(2,1)S(1)}, bf16[64,4096]{1,0:T(8,128)(2,1)S(1)}, u32[]{:S(2)}, u32[]{:S(2)}) collective-permute-start(bf16[64,4096]{1,0:T(8,128)(2,1)S(1)} %add_convert_fusion.4), channel_id=1, source_target_pairs={{0,1},{1,2},{2,3},{3,4},{4,5},{5,6},{6,7},{7,0},{8,9},{9,10},{10,1... | collective-permute-start | bytes 1572872 | tf_op jit(solution)/shard_map/ppermute | solution.py:177
Sparse Core Ops, SparseCore 0:
  21.9 48.5 all-gather.1

commit v3 on v2

--- a/solution.py
+++ b/solution.py
@@ -83,53 +83,55 @@
         o_ref[half:, cols] = norm(a1)
 
 
-SHIFTS = (4, 3, 5, 2, 6, 1, 7, 0)
+def project(n_ref, y, shifts, own_ref, other_ref, store):
+    rows = [n_ref[pl.ds(pl.multiple_of(lax.rem(y + s, Y) * 64, 64), 64), :] for s in shifts]
+    n = jnp.concatenate(rows, axis=0)
+    for t in range(8):
+        parts = []
+        for i in range(4):
+            x, z = divmod(4 * t + i, Z)
+            parts += [own_ref[x, z], other_ref[x, z]]
+        o = lax.dot_general(n, jnp.concatenate(parts, axis=0), NT, preferred_element_type=F32)
+        store(t, o.astype(BF16))
 
 
-def project_kernel(y_ref, n_ref, w_ref, up_ref, down_ref, *refs):
-    rest_refs, rows = refs[:-1], refs[-1]
-    z = pl.program_id(0)
+def first_kernel(y_ref, n_ref, own_ref, other_ref, up_ref, down_ref):
+    def store(t, o):
+        ref = up_ref if t < 4 else down_ref
+        ref[:, t % 4 * 512 : t % 4 * 512 + 512] = o
 
-    @pl.when(z == 0)
-    def _():
-        for i, shift in enumerate(SHIFTS):
-            at = pl.multiple_of(lax.rem(y_ref[0] + shift, Y) * 64, 64)
-            rows[i * 64 : (i + 1) * 64] = n_ref[pl.ds(at, 64)]
-
-    w = jnp.concatenate([w_ref[0, c, x] for x in range(X) for c in range(C)], axis=0)
-    o = lax.dot_general(rows[...], w, NT, preferred_element_type=F32).astype(BF16)
-
-    @pl.when(z < Z // 2)
-    def _():
-        up_ref[...] = o[:64]
-
-    @pl.when(z >= Z // 2)
-    def _():
-        down_ref[...] = o[:64]
-
-    for i, ref in enumerate(rest_refs):
-        ref[...] = o[(i + 1) * 64 : (i + 2) * 64]
+    project(n_ref, y_ref[0], (4,), own_ref, other_ref, store)
 
 
-def project(y, normed, weight):
-    half = Z // 2
-    out = pl.BlockSpec((64, 512), lambda z: (0, z))
-    up = pl.BlockSpec((64, 512), lambda z: (0, jnp.minimum(z, half - 1)))
-    down = pl.BlockSpec((64, 512), lambda z: (0, jnp.maximum(z - half, 0)))
-    return pl.pallas_call(
-        project_kernel,
-        grid=(Z,),
-        in_specs=[
-            SMEM,
-            pl.BlockSpec((512, 512), lambda z: (0, 0)),
-            pl.BlockSpec((1, C, X, 64, 512), lambda z: (z, 0, 0, 0, 0)),
-        ],
-        out_specs=[up, down] + [out] * 7,
-        out_shape=[shape(64, 2048)] * 2 + [shape(64, 4096)] * 7,
-        scratch_shapes=[pltpu.VMEM((512, 512), BF16)],
-        compiler_params=pltpu.CompilerParams(vmem_limit_bytes=56 * MIB),
-        cost_estimate=pl.CostEstimate(flops=2**31, bytes_accessed=8 * MIB, transcendentals=0),
-    )(y, normed, weight)
+def rest_kernel(y_ref, n_ref, own_ref, other_ref, *out_refs):
+    def store(t, o):
+        for i, ref in enumerate(out_refs):
+            ref[:, t * 512 : (t + 1) * 512] = o[i * 64 : (i + 1) * 64]
+
+    project(n_ref, y_ref[0], (3, 5, 2, 6, 1, 7, 0), own_ref, other_ref, store)
+
+
+def half_step_kernel(u_ref, up_ref, d_ref, down_ref, uo_ref, do_ref):
+    uo_ref[:, :2048] = add(u_ref[:, :2048], up_ref[...])
+    uo_ref[:, 2048:] = u_ref[:, 2048:]
+    do_ref[:, :2048] = d_ref[:, :2048]
+    do_ref[:, 2048:] = add(d_ref[:, 2048:], down_ref[...])
+
+
+def step_kernel(u_ref, up_ref, d_ref, down_ref, uo_ref, do_ref):
+    uo_ref[...] = add(u_ref[...], up_ref[...])
+    do_ref[...] = add(d_ref[...], down_ref[...])
+
+
+def last_kernel(place_ref, m_ref, up_ref, down_ref, o_ref):
+    x, core = place_ref[0], place_ref[1]
+    for t in range(X * Z):
+        dx, z = divmod(t, Z)
+        cols = slice(t * 128, (t + 1) * 128)
+        o = m_ref[:, cols].astype(F32) + up_ref[:, cols].astype(F32) + down_ref[:, cols].astype(F32)
+        o = jnp.where(core == 0, o, pltpu.roll(o, 64, 1))
+        at = pl.multiple_of((z * X + lax.rem(x + dx, X)) * 128, 128)
+        o_ref[:, pl.ds(at, 128)] = o.astype(BF16)
 
 
 def everywhere(part, axis, size):
@@ -146,37 +148,44 @@
 
 def on_device(queries, keys, values, out_weight):
     plane = ("x", "core")
-    z, y = (lax.axis_index(a).astype(jnp.int32)[None] for a in ("z", "tp"))
+    z, x, y, core = (lax.axis_index(a).astype(jnp.int32) for a in ("z", "x", "tp", "core"))
 
-    w_x = everywhere(out_weight.T, "x", X)
+    w_z = everywhere(out_weight.T, "z", Z)
     state = call(state_kernel, shape(4 * HD, HD), (keys, values), 2**26, MIB, vmem=16)
-    state, w_x = lax.optimization_barrier((state, w_x))
-    weight = lax.all_gather(w_x.reshape(X * 64, 512), ("z", "core"), axis=0, tiled=True)
-    weight = weight.reshape(Z, C, X, 64, 512)
+    state, w_z = lax.optimization_barrier((state, w_z))
     pieces = lax.all_to_all(state.reshape(8, 64, HD), plane, 0, 0)
+    pieces, w_z = lax.optimization_barrier((pieces, w_z))
+    own = [w_z] + [lax.ppermute(w_z, "x", [((i + d) % X, i) for i in range(X)]) for d in (1, 2, 3)]
     earlier, total = call(
         plane_kernel, (shape(8, 64, HD, dtype=F32), shape(8, 64, HD)), (pieces,), 2**17, 2**19, vmem=8
     )
     totals = lax.all_to_all(total, "z", 0, 0)
-    carried = call(carry_kernel, shape(8, 64, HD), (z, totals, earlier), 2**18, 2**19, 1, vmem=8)
+    carried = call(carry_kernel, shape(8, 64, HD), (z[None], totals, earlier), 2**18, 2**19, 1, vmem=8)
     carried = lax.all_to_all(carried, plane, 0, 0).reshape(4 * HD, HD)
+    carried, *own = lax.optimization_barrier((carried, *own))
+    own = jnp.stack(own)
+    other = lax.ppermute(own, "core", [(0, 1), (1, 0)])
     normed = call(
         attention_kernel, shape(512, 512), (queries, keys, values, carried), 2**29, 2 * MIB
     )
 
-    up, down, u3, d3, u2, d2, u1, d1, mine = project(y, normed, weight)
-    ring_up = [(i, (i + 1) % Y) for i in range(Y)]
-    ring_down = [(i, (i - 1) % Y) for i in range(Y)]
-    up = lax.ppermute(up, "tp", ring_up)
-    down = lax.ppermute(down, "tp", ring_down)
-    up = add(u3, jnp.pad(up, ((0, 0), (0, 2048))))
-    down = add(d3, jnp.pad(down, ((0, 0), (2048, 0))))
-    up = lax.ppermute(up, "tp", ring_up)
-    down = lax.ppermute(down, "tp", ring_down)
-    for u, d in ((u2, d2), (u1, d1)):
-        up = lax.ppermute(add(u, up), "tp", ring_up)
-        down = lax.ppermute(add(d, down), "tp", ring_down)
-    return (mine.astype(F32) + up.astype(F32) + down.astype(F32)).astype(BF16)
+    operands = (y[None], normed, own, other)
+    up, down = call(first_kernel, (shape(64, 2048),) * 2, operands, 2**28, 5 * MIB, 1)
+    u3, d3, u2, d2, u1, d1, mine = call(
+        rest_kernel, (shape(64, 4096),) * 7, operands, 2**31, 8 * MIB, 1, vmem=32
+    )
+
+    def ring(up, down):
+        up = lax.ppermute(up, "tp", [(i, (i + 1) % Y) for i in range(Y)])
+        down = lax.ppermute(down, "tp", [(i, (i - 1) % Y) for i in range(Y)])
+        return lax.optimization_barrier((up, down))
+
+    up, down = ring(up, down)
+    for kernel, u, d in ((half_step_kernel, u3, d3), (step_kernel, u2, d2), (step_kernel, u1, d1)):
+        up, down = call(kernel, (shape(64, 4096),) * 2, (u, up, d, down), 2**20, 3 * MIB, vmem=16)
+        up, down = ring(up, down)
+    place = jnp.stack([x, core])
+    return call(last_kernel, shape(64, 4096), (place, mine, up, down), 2**20, 2 * MIB, 1, vmem=16)
 
 
 def solution(mesh):

time: 153 us -> 154 us (level)
  the two profiles are of different devices: /device:TPU:4 before, /device:TPU:16 now
where the time goes in v3:
time: 154 us; the launch traced here: 153 us
  waiting for transfers between devices  63.8 us (41%)
  starting transfers between devices  48.3 us (31%)
  blocking collectives  21.1 us (14%)
  Pallas kernels  12 us (8%)
  local copies, waits for them, and re-layouts  5.57 us (4%)
  other arithmetic  1.94 us (1%)
    ppermute x4, waiting for transfers between devices, ring(): up = lax.ppermute(up, 'tp', [(i, (i + 1) % Y) for i in range(Y)])  23.4 us
    ppermute x4, waiting for transfers between devices, ring(): down = lax.ppermute(down, 'tp', [(i, (i - 1) % Y) for i in range(Y)])  15.2 us
    ppermute x4, starting transfers between devices, ring(): up = lax.ppermute(up, 'tp', [(i, (i + 1) % Y) for i in range(Y)])  15.2 us
    all_to_all x1, waiting for transfers between devices, everywhere(): lax.all_to_all(jnp.broadcast_to(part[None], (size,) + part.shape), axis,...  15.1 us
    pallas_call x10, Pallas kernels, call(): pl.pallas_call(kernel, out_shape=out_shape, in_specs=[SMEM] * scalars + [...  12 us
    all_to_all x1, blocking collectives, on_device(): carried = lax.all_to_all(carried, plane, 0, 0).reshape(4 * HD, HD)  10.9 us
    all_to_all x1, starting transfers between devices, everywhere(): lax.all_to_all(jnp.broadcast_to(part[None], (size,) + part.shape), axis,...  10.3 us
    all_to_all x1, blocking collectives, on_device(): pieces = lax.all_to_all(state.reshape(8, 64, HD), plane, 0, 0)  10.2 us
  transfers between devices with their start and end apart: 14, of which 11 were waited for; matrix products, arithmetic and copies ran while one was open for 0% of the time, Pallas kernels for 4%

profile of v3, /device:TPU:16, one launch (start us, length us, event | category | flops | bytes accessed | tf_op | source)
XLA Modules:
  0.0 152.9 jit_solution(3619171348576882097)
XLA Ops:
  0.0 1.7 %broadcast_in_dim.14 = bf16[8,64,512]{2,1,0:T(8,128)(2,1)} broadcast(bf16[64,512]{1,0:T(8,128)(2,1)} %bitcast.15), dimensions={1,2} | broadcast | bytes 589824 | tf_op jit(solution)/shard_map/broadcast_in_dim | solution.py:138
  1.7 10.3 %all-to-all-start = ((bf16[8,64,512]{2,1,0:T(8,128)(2,1)}), bf16[8,64,512]{2,1,0:T(8,128)(2,1)S(1)}, u32[]{:S(2)}, u32[]{:S(2)}) async-start(bf16[8,64,512]{2,1,0:T(8,128)(2,1)} %broadcast_in_dim.14), calls=%async_computation | async-start | bytes 1048576 | tf_op jit(solution)/shard_map/all_to_all | solution.py:138
  14.4 15.1 %all-to-all-done = bf16[8,64,512]{2,1,0:T(8,128)(2,1)S(1)} async-done(((bf16[8,64,512]{2,1,0:T(8,128)(2,1)}), bf16[8,64,512]{2,1,0:T(8,128)(2,1)S(1)}, u32[]{:S(2)}, u32[]{:S(2)}) %all-to-all-start) | async-done | bytes 524320 | tf_op jit(solution)/shard_map/all_to_all | solution.py:138
  29.5 10.2 %all_to_all.20.p_ref = bf16[8,64,128]{2,1,0:T(8,128)(2,1)S(1)} all-to-all(bf16[8,64,128]{2,1,0:T(8,128)(2,1)S(1)} %bitcast.12), channel_id=1, replica_groups=mesh['z'=8,'x'=4,'core'=2,'tp'=8] {'x','core'}, dimensions={0} | all-to-all | bytes 262144 | tf_op jit(solution)/shard_map/all_to_all | solution.py:156
  39.7 3.1 %collective-permute-start = (bf16[8,64,512]{2,1,0:T(8,128)(2,1)S(1)}, bf16[8,64,512]{2,1,0:T(8,128)(2,1)S(1)}, u32[]{:S(2)}, u32[]{:S(2)}) collective-permute-start(bf16[8,64,512]{2,1,0:T(8,128)(2,1)S(1)} %all-to-all-done), channel_id=1, source_target_pairs={{16,0},{32,16},{48,32},{0,48},{17,1},{33,17},{49,33},{1,49},{18,2}... | collective-permute-start | bytes 1572872 | tf_op jit(solution)/shard_map/ppermute | solution.py:158
  42.8 3.4 %collective-permute-start.1 = (bf16[8,64,512]{2,1,0:T(8,128)(2,1)S(1)}, bf16[8,64,512]{2,1,0:T(8,128)(2,1)}, u32[]{:S(2)}, u32[]{:S(2)}) collective-permute-start(bf16[8,64,512]{2,1,0:T(8,128)(2,1)S(1)} %all-to-all-done), channel_id=1, source_target_pairs={{32,0},{48,16},{0,32},{16,48},{33,1},{49,17},{1,33},{17,49},{34,2}... | collective-permute-start | bytes 1572872 | tf_op jit(solution)/shard_map/ppermute | solution.py:158
  46.2 1.9 %collective-permute-start.2 = (bf16[8,64,512]{2,1,0:T(8,128)(2,1)S(1)}, bf16[8,64,512]{2,1,0:T(8,128)(2,1)}, u32[]{:S(2)}, u32[]{:S(2)}) collective-permute-start(bf16[8,64,512]{2,1,0:T(8,128)(2,1)S(1)} %all-to-all-done), channel_id=1, source_target_pairs={{48,0},{0,16},{16,32},{32,48},{49,1},{1,17},{17,33},{33,49},{50,2}... | collective-permute-start | bytes 1572872 | tf_op jit(solution)/shard_map/ppermute | solution.py:158
  48.8 3.4 %all-to-all-start.2 = ((bf16[8,64,128]{2,1,0:T(8,128)(2,1)}), bf16[8,64,128]{2,1,0:T(8,128)(2,1)S(1)}, u32[]{:S(2)}, u32[]{:S(2)}) async-start(bf16[8,64,128]{2,1,0:T(8,128)(2,1)} %get-tuple-element.42), calls=%async_computation.2 | async-start | bytes 262144 | tf_op jit(solution)/shard_map/all_to_all | solution.py:162
  52.2 9.0 %all-to-all-done.2.t_ref = bf16[8,64,128]{2,1,0:T(8,128)(2,1)S(1)} async-done(((bf16[8,64,128]{2,1,0:T(8,128)(2,1)}), bf16[8,64,128]{2,1,0:T(8,128)(2,1)S(1)}, u32[]{:S(2)}, u32[]{:S(2)}) %all-to-all-start.2) | async-done | bytes 131104 | tf_op jit(solution)/shard_map/all_to_all | solution.py:162
  61.2 10.9 %all_to_all.21 = bf16[8,64,128]{2,1,0:T(8,128)(2,1)S(1)} all-to-all(bf16[8,64,128]{2,1,0:T(8,128)(2,1)S(1)} %shard_map.48), channel_id=1, replica_groups=mesh['z'=8,'x'=4,'core'=2,'tp'=8] {'x','core'}, dimensions={0} | all-to-all | bytes 262144 | tf_op jit(solution)/shard_map/all_to_all | solution.py:164
  72.9 1.9 %pad_maximum_fusion.own_ref = bf16[4,8,64,512]{3,2,1,0:T(8,128)(2,1)S(1)} fusion(bf16[1,8,64,512]{3,2,1,0:T(8,128)(2,1)} %bitcast.10, bf16[1,8,64,512]{3,2,1,0:T(8,128)(2,1)} %bitcast.9, bf16[1,8,64,512]{3,2,1,0:T(8,128)(2,1)} %bitcast.14, bf16[1,8,64,512]{3,2,1,0:T(8,128)(2,1)} %bitcast.13), kind=kLoop, calls=%fused_computation | loop fusion | flops 3145728 | bytes 4194304 | tf_op jit(solution)/shard_map/stack | solution.py:166
  74.7 1.9 %collective-permute-start.3 = (bf16[4,8,64,512]{3,2,1,0:T(8,128)(2,1)S(1)}, bf16[4,8,64,512]{3,2,1,0:T(8,128)(2,1)}, u32[]{:S(2)}, u32[]{:S(2)}) collective-permute-start(bf16[4,8,64,512]{3,2,1,0:T(8,128)(2,1)S(1)} %pad_maximum_fusion.own_ref), channel_id=1, source_target_pairs={{0,8},{8,0},{1,9},{9,1},{2,10},{10,2},{3,11},{11,3},{4,12},{12,4},... | collective-permute-start | bytes 6291464 | tf_op jit(solution)/shard_map/ppermute | solution.py:167
  77.7 2.0 %shard_map.49.n_ref = bf16[512,512]{1,0:T(8,128)(2,1)S(1)} custom-call(bf16[512,512]{1,0:T(8,128)(2,1)S(1)} %copy-done.4, bf16[512,512]{1,0:T(8,128)(2,1)S(1)} %copy-done.1, bf16[512,512]{1,0:T(8,128)(2,1)S(1)} %copy-done.3, bf16[512,128]{1,0:T(8,128)(2,1)S(1)} %bitcast.11), custom_call_target="tpu_custom_call" | custom-call | flops 536870912 | bytes 2097152 | tf_op jit(solution)/shard_map/pallas_call | solution.py:20
  79.8 1.2 collective-permute-done.3.other_ref
  80.9 3.0 %shard_map.51 = (bf16[64,2048]{1,0:T(8,128)(2,1)S(1)}, bf16[64,2048]{1,0:T(8,128)(2,1)S(1)}) custom-call(s32[1]{0:T(128)} %bitcast.2.y_ref, bf16[512,512]{1,0:T(8,128)(2,1)S(1)} %shard_map.49.n_ref, bf16[4,8,64,512]{3,2,1,0:T(8,128)(2,1)S(1)} %pad_maximum_fusion.own_ref, bf16[4,8,64,512]{3,2,1,0:T(8,128)(2,1)} %collective-permute-done.3.other_ref), custom_call_target="tpu_custom_call" | custom-call | flops 268435456 | bytes 5242880 | tf_op jit(solution)/shard_map/pallas_call | solution.py:20
  83.9 3.5 %collective-permute-start.4 = (bf16[64,2048]{1,0:T(8,128)(2,1)S(1)}, bf16[64,2048]{1,0:T(8,128)(2,1)S(1)}, u32[]{:S(2)}, u32[]{:S(2)}) collective-permute-start(bf16[64,2048]{1,0:T(8,128)(2,1)S(1)} %get-tuple-element.54), channel_id=1, source_target_pairs={{0,1},{1,2},{2,3},{3,4},{4,5},{5,6},{6,7},{7,0},{8,9},{9,10},{10,1... | collective-permute-start | bytes 786440 | tf_op jit(solution)/shard_map/ppermute | solution.py:179
  87.4 2.4 %collective-permute-start.5 = (bf16[64,2048]{1,0:T(8,128)(2,1)S(1)}, bf16[64,2048]{1,0:T(8,128)(2,1)S(1)}, u32[]{:S(2)}, u32[]{:S(2)}) collective-permute-start(bf16[64,2048]{1,0:T(8,128)(2,1)S(1)} %get-tuple-element.55), channel_id=1, source_target_pairs={{0,7},{1,0},{2,1},{3,2},{4,3},{5,4},{6,5},{7,6},{8,15},{9,8},{10,9... | collective-permute-start | bytes 786440 | tf_op jit(solution)/shard_map/ppermute | solution.py:180
  89.7 3.7 %shard_map.50 = (bf16[64,4096]{1,0:T(8,128)(2,1)S(1)}, bf16[64,4096]{1,0:T(8,128)(2,1)S(1)}, bf16[64,4096]{1,0:T(8,128)(2,1)S(1)}, bf16[64,4096]{1,0:T(8,128)(2,...) custom-call(s32[1]{0:T(128)} %bitcast.2.y_ref, ...), custom_call_target="tpu_custom_call" | custom-call | flops 2147483648 | bytes 8388608 | tf_op jit(solution)/shard_map/pallas_call | solution.py:20
  94.1 4.3 %collective-permute-done.5.down_ref = bf16[64,2048]{1,0:T(8,128)(2,1)S(1)} collective-permute-done((bf16[64,2048]{1,0:T(8,128)(2,1)S(1)}, bf16[64,2048]{1,0:T(8,128)(2,1)S(1)}, u32[]{:S(2)}, u32[]{:S(2)}) %collective-permute-start.5) | collective-permute-done | bytes 262176 | tf_op jit(solution)/shard_map/ppermute | solution.py:180
  98.5 4.9 %collective-permute-start.6 = (bf16[64,4096]{1,0:T(8,128)(2,1)S(1)}, bf16[64,4096]{1,0:T(8,128)(2,1)S(1)}, u32[]{:S(2)}, u32[]{:S(2)}) collective-permute-start(bf16[64,4096]{1,0:T(8,128)(2,1)S(1)} %get-tuple-element.59), channel_id=1, source_target_pairs={{0,1},{1,2},{2,3},{3,4},{4,5},{5,6},{6,7},{7,0},{8,9},{9,10},{10,1... | collective-permute-start | bytes 1572872 | tf_op jit(solution)/shard_map/ppermute | solution.py:179
  103.4 1.9 %collective-permute-start.7 = (bf16[64,4096]{1,0:T(8,128)(2,1)S(1)}, bf16[64,4096]{1,0:T(8,128)(2,1)S(1)}, u32[]{:S(2)}, u32[]{:S(2)}) collective-permute-start(bf16[64,4096]{1,0:T(8,128)(2,1)S(1)} %get-tuple-element.60), channel_id=1, source_target_pairs={{0,7},{1,0},{2,1},{3,2},{4,3},{5,4},{6,5},{7,6},{8,15},{9,8},{10,9... | collective-permute-start | bytes 1572872 | tf_op jit(solution)/shard_map/ppermute | solution.py:180
  105.3 8.4 %collective-permute-done.6.up_ref = bf16[64,4096]{1,0:T(8,128)(2,1)S(1)} collective-permute-done((bf16[64,4096]{1,0:T(8,128)(2,1)S(1)}, bf16[64,4096]{1,0:T(8,128)(2,1)S(1)}, u32[]{:S(2)}, u32[]{:S(2)}) %collective-permute-start.6) | collective-permute-done | bytes 524320 | tf_op jit(solution)/shard_map/ppermute | solution.py:179
  113.7 4.1 %collective-permute-done.7.down_ref = bf16[64,4096]{1,0:T(8,128)(2,1)S(1)} collective-permute-done((bf16[64,4096]{1,0:T(8,128)(2,1)S(1)}, bf16[64,4096]{1,0:T(8,128)(2,1)S(1)}, u32[]{:S(2)}, u32[]{:S(2)}) %collective-permute-start.7) | collective-permute-done | bytes 524320 | tf_op jit(solution)/shard_map/ppermute | solution.py:180
  118.1 3.4 %collective-permute-start.8 = (bf16[64,4096]{1,0:T(8,128)(2,1)S(1)}, bf16[64,4096]{1,0:T(8,128)(2,1)S(1)}, u32[]{:S(2)}, u32[]{:S(2)}) collective-permute-start(bf16[64,4096]{1,0:T(8,128)(2,1)S(1)} %get-tuple-element.64), channel_id=1, source_target_pairs={{0,1},{1,2},{2,3},{3,4},{4,5},{5,6},{6,7},{7,0},{8,9},{9,10},{10,1... | collective-permute-start | bytes 1572872 | tf_op jit(solution)/shard_map/ppermute | solution.py:179
  121.5 2.4 %collective-permute-start.9 = (bf16[64,4096]{1,0:T(8,128)(2,1)S(1)}, bf16[64,4096]{1,0:T(8,128)(2,1)S(1)}, u32[]{:S(2)}, u32[]{:S(2)}) collective-permute-start(bf16[64,4096]{1,0:T(8,128)(2,1)S(1)} %get-tuple-element.65), channel_id=1, source_target_pairs={{0,7},{1,0},{2,1},{3,2},{4,3},{5,4},{6,5},{7,6},{8,15},{9,8},{10,9... | collective-permute-start | bytes 1572872 | tf_op jit(solution)/shard_map/ppermute | solution.py:180
  123.9 7.6 %collective-permute-done.8.up_ref = bf16[64,4096]{1,0:T(8,128)(2,1)S(1)} collective-permute-done((bf16[64,4096]{1,0:T(8,128)(2,1)S(1)}, bf16[64,4096]{1,0:T(8,128)(2,1)S(1)}, u32[]{:S(2)}, u32[]{:S(2)}) %collective-permute-start.8) | collective-permute-done | bytes 524320 | tf_op jit(solution)/shard_map/ppermute | solution.py:179
  131.6 3.4 %collective-permute-done.9.down_ref = bf16[64,4096]{1,0:T(8,128)(2,1)S(1)} collective-permute-done((bf16[64,4096]{1,0:T(8,128)(2,1)S(1)}, bf16[64,4096]{1,0:T(8,128)(2,1)S(1)}, u32[]{:S(2)}, u32[]{:S(2)}) %collective-permute-start.9) | collective-permute-done | bytes 524320 | tf_op jit(solution)/shard_map/ppermute | solution.py:180
  135.2 3.4 %collective-permute-start.10 = (bf16[64,4096]{1,0:T(8,128)(2,1)S(1)}, bf16[64,4096]{1,0:T(8,128)(2,1)S(1)}, u32[]{:S(2)}, u32[]{:S(2)}) collective-permute-start(bf16[64,4096]{1,0:T(8,128)(2,1)S(1)} %get-tuple-element.69), channel_id=1, source_target_pairs={{0,1},{1,2},{2,3},{3,4},{4,5},{5,6},{6,7},{7,0},{8,9},{9,10},{10,1... | collective-permute-start | bytes 1572872 | tf_op jit(solution)/shard_map/ppermute | solution.py:179
  138.6 2.4 %collective-permute-start.11 = (bf16[64,4096]{1,0:T(8,128)(2,1)S(1)}, bf16[64,4096]{1,0:T(8,128)(2,1)S(1)}, u32[]{:S(2)}, u32[]{:S(2)}) collective-permute-start(bf16[64,4096]{1,0:T(8,128)(2,1)S(1)} %get-tuple-element.70), channel_id=1, source_target_pairs={{0,7},{1,0},{2,1},{3,2},{4,3},{5,4},{6,5},{7,6},{8,15},{9,8},{10,9... | collective-permute-start | bytes 1572872 | tf_op jit(solution)/shard_map/ppermute | solution.py:180
  141.2 6.6 %collective-permute-done.10.up_ref = bf16[64,4096]{1,0:T(8,128)(2,1)S(1)} collective-permute-done((bf16[64,4096]{1,0:T(8,128)(2,1)S(1)}, bf16[64,4096]{1,0:T(8,128)(2,1)S(1)}, u32[]{:S(2)}, u32[]{:S(2)}) %collective-permute-start.10) | collective-permute-done | bytes 524320 | tf_op jit(solution)/shard_map/ppermute | solution.py:179
  147.8 3.4 %collective-permute-done.11.down_ref = bf16[64,4096]{1,0:T(8,128)(2,1)S(1)} collective-permute-done((bf16[64,4096]{1,0:T(8,128)(2,1)S(1)}, bf16[64,4096]{1,0:T(8,128)(2,1)S(1)}, u32[]{:S(2)}, u32[]{:S(2)}) %collective-permute-start.11) | collective-permute-done | bytes 524320 | tf_op jit(solution)/shard_map/ppermute | solution.py:180
  151.2 1.7 %shard_map.55 = bf16[64,4096]{1,0:T(8,128)(2,1)} custom-call(s32[2]{0:T(128)S(1)} %pad_add_fusion.place_ref, bf16[64,4096]{1,0:T(8,128)(2,1)S(1)} %get-tuple-element.50.m_ref, bf16[64,4096]{1,0:T(8,128)(2,1)S(1)} %collective-permute-done.10.up_ref, bf16[64,4096]{1,0:T(8,128)(2,1)S(1)} %collective-permute-done.11.down_ref), custom_call_target="tpu_custom_call" | custom-call | flops 1048576 | bytes 2097152 | tf_op jit(solution)/shard_map/pallas_call | solution.py:20
  (25 shorter events, 6.3 us)
Async XLA Ops:
  1.7 27.8 %all-to-all-start = ((bf16[8,64,512]{2,1,0:T(8,128)(2,1)}), bf16[8,64,512]{2,1,0:T(8,128)(2,1)S(1)}, u32[]{:S(2)}, u32[]{:S(2)}) async-start(bf16[8,64,512]{2,1,0:T(8,128)(2,1)} %broadcast_in_dim.14), calls=%async_computation | async-start | bytes 1048576 | tf_op jit(solution)/shard_map/all_to_all | solution.py:138
  12.0 1.0 copy-start
  13.0 1.0 copy-start.2
  29.5 42.6 %copy-start.5 = (bf16[8,64,512]{2,1,0:T(8,128)(2,1)}, bf16[8,64,512]{2,1,0:T(8,128)(2,1)S(1)}, u32[]{:S(2)}) copy-start(bf16[8,64,512]{2,1,0:T(8,128)(2,1)S(1)} %all-to-all-done) | copy-start | bytes 1572868
  39.7 32.4 %collective-permute-start = (bf16[8,64,512]{2,1,0:T(8,128)(2,1)S(1)}, bf16[8,64,512]{2,1,0:T(8,128)(2,1)S(1)}, u32[]{:S(2)}, u32[]{:S(2)}) collective-permute-start(bf16[8,64,512]{2,1,0:T(8,128)(2,1)S(1)} %all-to-all-done), channel_id=1, source_target_pairs={{16,0},{32,16},{48,32},{0,48},{17,1},{33,17},{49,33},{1,49},{18,2}... | collective-permute-start | bytes 1572872 | tf_op jit(solution)/shard_map/ppermute | solution.py:158
  42.8 29.3 %collective-permute-start.1 = (bf16[8,64,512]{2,1,0:T(8,128)(2,1)S(1)}, bf16[8,64,512]{2,1,0:T(8,128)(2,1)}, u32[]{:S(2)}, u32[]{:S(2)}) collective-permute-start(bf16[8,64,512]{2,1,0:T(8,128)(2,1)S(1)} %all-to-all-done), channel_id=1, source_target_pairs={{32,0},{48,16},{0,32},{16,48},{33,1},{49,17},{1,33},{17,49},{34,2}... | collective-permute-start | bytes 1572872 | tf_op jit(solution)/shard_map/ppermute | solution.py:158
  46.2 25.9 %collective-permute-start.2 = (bf16[8,64,512]{2,1,0:T(8,128)(2,1)S(1)}, bf16[8,64,512]{2,1,0:T(8,128)(2,1)}, u32[]{:S(2)}, u32[]{:S(2)}) collective-permute-start(bf16[8,64,512]{2,1,0:T(8,128)(2,1)S(1)} %all-to-all-done), channel_id=1, source_target_pairs={{48,0},{0,16},{16,32},{32,48},{49,1},{1,17},{17,33},{33,49},{50,2}... | collective-permute-start | bytes 1572872 | tf_op jit(solution)/shard_map/ppermute | solution.py:158
  48.8 12.4 %all-to-all-start.2 = ((bf16[8,64,128]{2,1,0:T(8,128)(2,1)}), bf16[8,64,128]{2,1,0:T(8,128)(2,1)S(1)}, u32[]{:S(2)}, u32[]{:S(2)}) async-start(bf16[8,64,128]{2,1,0:T(8,128)(2,1)} %get-tuple-element.42), calls=%async_computation.2 | async-start | bytes 262144 | tf_op jit(solution)/shard_map/all_to_all | solution.py:162
  72.1 0.8 copy-start.6
  72.9 3.8 %copy-start.1 = (bf16[512,512]{1,0:T(8,128)(2,1)S(1)}, bf16[512,512]{1,0:T(8,128)(2,1)}, u32[]{:S(2)}) copy-start(bf16[512,512]{1,0:T(8,128)(2,1)} %k_ref.3) | copy-start | bytes 1572868
  72.9 3.8 %copy-start.3 = (bf16[512,512]{1,0:T(8,128)(2,1)S(1)}, bf16[512,512]{1,0:T(8,128)(2,1)}, u32[]{:S(2)}) copy-start(bf16[512,512]{1,0:T(8,128)(2,1)} %v_ref.3) | copy-start | bytes 1572868
  74.7 6.2 %collective-permute-start.3 = (bf16[4,8,64,512]{3,2,1,0:T(8,128)(2,1)S(1)}, bf16[4,8,64,512]{3,2,1,0:T(8,128)(2,1)}, u32[]{:S(2)}, u32[]{:S(2)}) collective-permute-start(bf16[4,8,64,512]{3,2,1,0:T(8,128)(2,1)S(1)} %pad_maximum_fusion.own_ref), channel_id=1, source_target_pairs={{0,8},{8,0},{1,9},{9,1},{2,10},{10,2},{3,11},{11,3},{4,12},{12,4},... | collective-permute-start | bytes 6291464 | tf_op jit(solution)/shard_map/ppermute | solution.py:167
  76.7 1.0 copy-start.4
  83.9 10.2 %collective-permute-start.4 = (bf16[64,2048]{1,0:T(8,128)(2,1)S(1)}, bf16[64,2048]{1,0:T(8,128)(2,1)S(1)}, u32[]{:S(2)}, u32[]{:S(2)}) collective-permute-start(bf16[64,2048]{1,0:T(8,128)(2,1)S(1)} %get-tuple-element.54), channel_id=1, source_target_pairs={{0,1},{1,2},{2,3},{3,4},{4,5},{5,6},{6,7},{7,0},{8,9},{9,10},{10,1... | collective-permute-start | bytes 786440 | tf_op jit(solution)/shard_map/ppermute | solution.py:179
  87.4 11.0 %collective-permute-start.5 = (bf16[64,2048]{1,0:T(8,128)(2,1)S(1)}, bf16[64,2048]{1,0:T(8,128)(2,1)S(1)}, u32[]{:S(2)}, u32[]{:S(2)}) collective-permute-start(bf16[64,2048]{1,0:T(8,128)(2,1)S(1)} %get-tuple-element.55), channel_id=1, source_target_pairs={{0,7},{1,0},{2,1},{3,2},{4,3},{5,4},{6,5},{7,6},{8,15},{9,8},{10,9... | collective-permute-start | bytes 786440 | tf_op jit(solution)/shard_map/ppermute | solution.py:180
  98.5 15.2 %collective-permute-start.6 = (bf16[64,4096]{1,0:T(8,128)(2,1)S(1)}, bf16[64,4096]{1,0:T(8,128)(2,1)S(1)}, u32[]{:S(2)}, u32[]{:S(2)}) collective-permute-start(bf16[64,4096]{1,0:T(8,128)(2,1)S(1)} %get-tuple-element.59), channel_id=1, source_target_pairs={{0,1},{1,2},{2,3},{3,4},{4,5},{5,6},{6,7},{7,0},{8,9},{9,10},{10,1... | collective-permute-start | bytes 1572872 | tf_op jit(solution)/shard_map/ppermute | solution.py:179
  103.4 14.4 %collective-permute-start.7 = (bf16[64,4096]{1,0:T(8,128)(2,1)S(1)}, bf16[64,4096]{1,0:T(8,128)(2,1)S(1)}, u32[]{:S(2)}, u32[]{:S(2)}) collective-permute-start(bf16[64,4096]{1,0:T(8,128)(2,1)S(1)} %get-tuple-element.60), channel_id=1, source_target_pairs={{0,7},{1,0},{2,1},{3,2},{4,3},{5,4},{6,5},{7,6},{8,15},{9,8},{10,9... | collective-permute-start | bytes 1572872 | tf_op jit(solution)/shard_map/ppermute | solution.py:180
  118.1 13.5 %collective-permute-start.8 = (bf16[64,4096]{1,0:T(8,128)(2,1)S(1)}, bf16[64,4096]{1,0:T(8,128)(2,1)S(1)}, u32[]{:S(2)}, u32[]{:S(2)}) collective-permute-start(bf16[64,4096]{1,0:T(8,128)(2,1)S(1)} %get-tuple-element.64), channel_id=1, source_target_pairs={{0,1},{1,2},{2,3},{3,4},{4,5},{5,6},{6,7},{7,0},{8,9},{9,10},{10,1... | collective-permute-start | bytes 1572872 | tf_op jit(solution)/shard_map/ppermute | solution.py:179
  121.5 13.5 %collective-permute-start.9 = (bf16[64,4096]{1,0:T(8,128)(2,1)S(1)}, bf16[64,4096]{1,0:T(8,128)(2,1)S(1)}, u32[]{:S(2)}, u32[]{:S(2)}) collective-permute-start(bf16[64,4096]{1,0:T(8,128)(2,1)S(1)} %get-tuple-element.65), channel_id=1, source_target_pairs={{0,7},{1,0},{2,1},{3,2},{4,3},{5,4},{6,5},{7,6},{8,15},{9,8},{10,9... | collective-permute-start | bytes 1572872 | tf_op jit(solution)/shard_map/ppermute | solution.py:180
  135.2 12.6 %collective-permute-start.10 = (bf16[64,4096]{1,0:T(8,128)(2,1)S(1)}, bf16[64,4096]{1,0:T(8,128)(2,1)S(1)}, u32[]{:S(2)}, u32[]{:S(2)}) collective-permute-start(bf16[64,4096]{1,0:T(8,128)(2,1)S(1)} %get-tuple-element.69), channel_id=1, source_target_pairs={{0,1},{1,2},{2,3},{3,4},{4,5},{5,6},{6,7},{7,0},{8,9},{9,10},{10,1... | collective-permute-start | bytes 1572872 | tf_op jit(solution)/shard_map/ppermute | solution.py:179
  138.6 12.6 %collective-permute-start.11 = (bf16[64,4096]{1,0:T(8,128)(2,1)S(1)}, bf16[64,4096]{1,0:T(8,128)(2,1)S(1)}, u32[]{:S(2)}, u32[]{:S(2)}) collective-permute-start(bf16[64,4096]{1,0:T(8,128)(2,1)S(1)} %get-tuple-element.70), channel_id=1, source_target_pairs={{0,7},{1,0},{2,1},{3,2},{4,3},{5,4},{6,5},{7,6},{8,15},{9,8},{10,9... | collective-permute-start | bytes 1572872 | tf_op jit(solution)/shard_map/ppermute | solution.py:180

commit v4 on v1

--- a/solution.py
+++ b/solution.py
@@ -9,23 +9,58 @@
 F32 = jnp.float32
 BF16 = jnp.bfloat16
 Z, X, C, Y = 8, 4, 2, 8
+MIB = 2**20
+NT = (((1,), (1,)), ((), ()))
+TN = (((0,), (0,)), ((), ()))
+VMEM = pl.BlockSpec(memory_space=pltpu.VMEM)
+SMEM = pl.BlockSpec(memory_space=pltpu.SMEM)
+
+
+def call(kernel, out_shape, operands, flops, moved, scalars=0, vmem=24):
+    return pl.pallas_call(
+        kernel,
+        out_shape=out_shape,
+        in_specs=[SMEM] * scalars + [VMEM] * (len(operands) - scalars),
+        out_specs=jax.tree.map(lambda _: VMEM, out_shape),
+        compiler_params=pltpu.CompilerParams(vmem_limit_bytes=vmem * MIB),
+        cost_estimate=pl.CostEstimate(flops=flops, bytes_accessed=moved, transcendentals=0),
+    )(*operands)
+
+
+def plane_kernel(p_ref, e_ref, t_ref):
+    running = jnp.zeros(p_ref.shape[1:], F32)
+    for i in range(C * X):
+        e_ref[i] = running
+        running = running + p_ref[i].astype(F32)
+    total = running.astype(BF16)
+    for i in range(Z):
+        t_ref[i] = total
+
+
+def carry_kernel(z_ref, t_ref, e_ref, c_ref):
+    z = z_ref[0]
+    before = jnp.zeros(t_ref.shape[1:], F32)
+    for i in range(Z - 1):
+        before = before + jnp.where(i < z, t_ref[i].astype(F32), 0.0)
+    for i in range(C * X):
+        c_ref[i] = (e_ref[i] + before).astype(BF16)
 
 
 def state_kernel(k_ref, v_ref, s_ref):
-    for h in range(4):
-        cols = slice(h * HD, (h + 1) * HD)
-        s = lax.dot_general(
-            k_ref[:, cols], v_ref[:, cols], (((0,), (0,)), ((), ())), preferred_element_type=F32
-        )
-        s_ref[cols, :] = s.astype(BF16)
+    s = lax.dot_general(k_ref[...], v_ref[...], TN, preferred_element_type=F32)
+    s_ref[...] = s.astype(BF16)
 
 
 def states(keys, values):
+    by_head = pl.BlockSpec((512, HD), lambda h: (0, h))
     return pl.pallas_call(
         state_kernel,
-        out_shape=jax.ShapeDtypeStruct((4 * HD, HD), BF16),
-        compiler_params=pltpu.CompilerParams(vmem_limit_bytes=16 * 2**20),
-        cost_estimate=pl.CostEstimate(flops=2 * 512 * 512 * 128, bytes_accessed=2**20, transcendentals=0),
+        grid=(4,),
+        in_specs=[by_head, by_head],
+        out_specs=pl.BlockSpec((HD, HD), lambda h: (h, 0)),
+        out_shape=shape(4 * HD, HD),
+        compiler_params=pltpu.CompilerParams(vmem_limit_bytes=56 * MIB),
+        cost_estimate=pl.CostEstimate(flops=2**26, bytes_accessed=MIB, transcendentals=0),
     )(keys, values)
 
 
@@ -66,7 +101,7 @@
         in_specs=[by_head, by_head, by_head, pl.BlockSpec((HD, HD), lambda h: (h, 0))],
         out_specs=by_head,
         out_shape=jax.ShapeDtypeStruct((512, 512), BF16),
-        compiler_params=pltpu.CompilerParams(vmem_limit_bytes=24 * 2**20),
+        compiler_params=pltpu.CompilerParams(vmem_limit_bytes=56 * MIB),
         cost_estimate=pl.CostEstimate(flops=2**29, bytes_accessed=2**21, transcendentals=2048),
     )(queries, keys, values, carried)
 
@@ -88,9 +123,13 @@
         ],
         out_specs=pl.BlockSpec((512, 512), lambda z: (0, z)),
         out_shape=jax.ShapeDtypeStruct((512, 4096), BF16),
-        compiler_params=pltpu.CompilerParams(vmem_limit_bytes=24 * 2**20),
+        compiler_params=pltpu.CompilerParams(vmem_limit_bytes=56 * MIB),
         cost_estimate=pl.CostEstimate(flops=2**31, bytes_accessed=2**23, transcendentals=0),
     )(normed, weight)
+
+
+def shape(*dims, dtype=BF16):
+    return jax.ShapeDtypeStruct(dims, dtype)
 
 
 def everywhere(part, axis, size):
@@ -105,18 +144,13 @@
     weight = weight.reshape(Z, C, X, 64, 512)
 
     state = states(keys, values).reshape(8, 64, HD)
-    pieces = lax.all_to_all(state, plane, 0, 0).astype(F32)
-    place = lax.axis_index("z")
-    running = jnp.zeros((64, HD), F32)
-    earlier = []
-    for i in range(8):
-        earlier.append(running)
-        running = running + pieces[i]
-    earlier = jnp.stack(earlier)
-    totals = everywhere(running.astype(BF16), "z", Z)
-    mask = (jnp.arange(Z) < place)[:, None, None]
-    before = jnp.sum(jnp.where(mask, totals, 0).astype(F32), axis=0)
-    carried = (earlier + before[None]).astype(BF16)
+    pieces = lax.all_to_all(state, plane, 0, 0)
+    earlier, total = call(
+        plane_kernel, (shape(8, 64, HD, dtype=F32), shape(8, 64, HD)), (pieces,), 2**17, 2**19, vmem=8
+    )
+    totals = lax.all_to_all(total, "z", 0, 0)
+    z = lax.axis_index("z").astype(jnp.int32)[None]
+    carried = call(carry_kernel, shape(8, 64, HD), (z, totals, earlier), 2**18, 2**19, 1, vmem=8)
     carried = lax.all_to_all(carried, plane, 0, 0).reshape(4 * HD, HD)
 
     normed = attention(queries, keys, values, carried)

time: 141 us -> 142 us (level)
  blocking collectives: 21.5 us -> 37.4 us
  Pallas kernels: 8.23 us -> 17.9 us
  starting transfers between devices: 15.5 us -> 5.84 us
  waiting for transfers between devices: 73.8 us -> 65.8 us
  local copies, waits for them, and re-layouts: 7.86 us -> 0.86 us
    all_to_all x0 -> x1, blocking collectives: none -> 14.9 us  [on_device(): pieces = lax.all_to_all(state, plane, 0, 0)]
    all_to_all x2 -> x1, starting transfers between devices: 15.4 us -> 5.8 us  [on_device(): totals = lax.all_to_all(total, 'z', 0, 0)]
    unnamed x18 -> x0, local copies, waits for them, and re-layouts: 6.24 us -> none
    all_to_all x2 -> x1, waiting for transfers between devices: 13.5 us -> 7.72 us  [on_device(): totals = lax.all_to_all(total, 'z', 0, 0)]
    pallas_call x1, Pallas kernels: 3.98 us -> 8.46 us  [project(): pl.pallas_call(project_kernel, grid=(Z,), in_specs=[pl.BlockSpec((512, 51...]
    pallas_call x1 -> x3, Pallas kernels: 1 us -> 4.4 us  [the longest x1 3.67 us: states(): pl.pallas_call(state_kernel, grid=(4,), in_specs=[by_head, by_head], out_...]
    all_gather x1, waiting for transfers between devices: 4.72 us -> 2 us  [on_device(): lax.all_gather(w_x.reshape(X * 64, 512), ('z', 'core'), axis=0, tiled=True)]
    pallas_call x1, Pallas kernels: 3.24 us -> 5 us  [attention(): pl.pallas_call(attention_kernel, grid=(4,), in_specs=[by_head, by_head, b...]
  transfers between devices with their start and end apart: 4 -> 3, of which waited for: 4 -> 3; matrix products, arithmetic and copies ran while one was open for 1% -> 0% of each run, Pallas kernels for 3% -> 7%
where the time goes in v4:
time: 142 us; the launch traced here: 141 us
  waiting for transfers between devices  65.8 us (46%)
  blocking collectives  37.4 us (26%)
  Pallas kernels  17.9 us (13%)
  between operations  13.4 us (9%)
  starting transfers between devices  5.84 us (4%)
    reduce_scatter x1, waiting for transfers between devices, on_device(): return lax.psum_scatter(terms, 'tp', scatter_dimension=0, tiled=True)  56 us
    all_to_all x1, blocking collectives, on_device(): pieces = lax.all_to_all(state, plane, 0, 0)  14.9 us
    all_to_all x1, blocking collectives, on_device(): carried = lax.all_to_all(carried, plane, 0, 0).reshape(4 * HD, HD)  12.2 us
    all_to_all x1, blocking collectives, everywhere(): lax.all_to_all(jnp.broadcast_to(part[None], (size,) + part.shape), axis,...  10.3 us
    pallas_call x1, Pallas kernels, project(): pl.pallas_call(project_kernel, grid=(Z,), in_specs=[pl.BlockSpec((512, 51...  8.46 us
    all_to_all x1, waiting for transfers between devices, on_device(): totals = lax.all_to_all(total, 'z', 0, 0)  7.72 us
    all_to_all x1, starting transfers between devices, on_device(): totals = lax.all_to_all(total, 'z', 0, 0)  5.8 us
    pallas_call x1, Pallas kernels, attention(): pl.pallas_call(attention_kernel, grid=(4,), in_specs=[by_head, by_head, b...  5 us
  transfers between devices with their start and end apart: 3, of which 3 were waited for; matrix products, arithmetic and copies ran while one was open for 0% of the time, Pallas kernels for 7%

profile of v4, /device:TPU:1, one launch (start us, length us, event | category | flops | bytes accessed | tf_op | source)
XLA Modules:
  0.0 141.2 jit_solution(14694132921084204321)
XLA Ops:
  6.5 0.0 all-gather.2.cloned.1.call-start
  6.5 0.9 broadcast_in_dim.4
  7.4 10.3 %all_to_all.20 = bf16[4,64,512]{2,1,0:T(8,128)(2,1)} all-to-all(bf16[4,64,512]{2,1,0:T(8,128)(2,1)S(1)} %broadcast_in_dim.4), channel_id=1, replica_groups=mesh['z'=8,'x'=4,'core'=2,'tp'=8] {'x'}, dimensions={0} | all-to-all | bytes 524288 | tf_op jit(solution)/shard_map/all_to_all | solution.py:136
  17.7 0.0 all-gather.2.cloned.1.call-update
  17.7 3.7 %shard_map.46 = bf16[512,128]{1,0:T(8,128)(2,1)} custom-call(bf16[512,512]{1,0:T(8,128)(2,1)} %k_ref.1, bf16[512,512]{1,0:T(8,128)(2,1)} %v_ref.1), custom_call_target="tpu_custom_call" | custom-call | flops 67108864 | bytes 1048576 | tf_op jit(solution)/shard_map/pallas_call | solution.py:56
  21.4 14.9 %all_to_all.21.p_ref = bf16[8,64,128]{2,1,0:T(8,128)(2,1)S(1)} all-to-all(bf16[8,64,128]{2,1,0:T(8,128)(2,1)} %bitcast.9), channel_id=1, replica_groups=mesh['z'=8,'x'=4,'core'=2,'tp'=8] {'x','core'}, dimensions={0} | all-to-all | bytes 262144 | tf_op jit(solution)/shard_map/all_to_all | solution.py:147
  36.3 0.7 shard_map.47
  36.9 5.8 %all-to-all-start.2 = ((bf16[8,64,128]{2,1,0:T(8,128)(2,1)}), bf16[8,64,128]{2,1,0:T(8,128)(2,1)S(1)}, u32[]{:S(2)}, u32[]{:S(2)}) async-start(bf16[8,64,128]{2,1,0:T(8,128)(2,1)} %get-tuple-element.12), calls=%async_computation.2 | async-start | bytes 262144 | tf_op jit(solution)/shard_map/all_to_all | solution.py:151
  42.7 0.0 reduce-scatter.2.cloned.1.call-start
  42.8 7.7 %all-to-all-done.2.t_ref = bf16[8,64,128]{2,1,0:T(8,128)(2,1)S(1)} async-done(((bf16[8,64,128]{2,1,0:T(8,128)(2,1)}), bf16[8,64,128]{2,1,0:T(8,128)(2,1)S(1)}, u32[]{:S(2)}, u32[]{:S(2)}) %all-to-all-start.2) | async-done | bytes 131104 | tf_op jit(solution)/shard_map/all_to_all | solution.py:151
  50.6 12.2 %all_to_all.22 = bf16[8,64,128]{2,1,0:T(8,128)(2,1)} all-to-all(bf16[8,64,128]{2,1,0:T(8,128)(2,1)S(1)} %shard_map.48), channel_id=1, replica_groups=mesh['z'=8,'x'=4,'core'=2,'tp'=8] {'x','core'}, dimensions={0} | all-to-all | bytes 262144 | tf_op jit(solution)/shard_map/all_to_all | solution.py:154
  62.8 5.0 %shard_map.49.n_ref = bf16[512,512]{1,0:T(8,128)(2,1)} custom-call(bf16[512,512]{1,0:T(8,128)(2,1)} %q_ref.1, bf16[512,512]{1,0:T(8,128)(2,1)} %k_ref.1, bf16[512,512]{1,0:T(8,128)(2,1)} %v_ref.1, bf16[512,128]{1,0:T(8,128)(2,1)} %bitcast.8), custom_call_target="tpu_custom_call" | custom-call | flops 536870912 | bytes 2097152 | tf_op jit(solution)/shard_map/pallas_call | solution.py:98
  67.8 2.0 %all-gather.2.cloned.1.call-done = bf16[4096,512]{1,0:T(8,128)(2,1)} async-done(((bf16[256,512]{1,0:T(8,128)(2,1)}), bf16[4096,512]{1,0:T(8,128)(2,1)}) %all-gather.2.cloned.1.call-update) | async-done | bytes 4194320 | tf_op jit(solution)/shard_map/all_gather | solution.py:143
  69.8 8.5 %shard_map.50 = bf16[512,4096]{1,0:T(8,128)(2,1)} custom-call(bf16[512,512]{1,0:T(8,128)(2,1)} %shard_map.49.n_ref, bf16[8,2,4,64,512]{4,3,2,1,0:T(8,128)(2,1)} %bitcast.6), custom_call_target="tpu_custom_call" | custom-call | flops 2147483648 | bytes 8388608 | tf_op jit(solution)/shard_map/pallas_call | solution.py:117
  78.3 0.0 reduce-scatter.2.cloned.1.call-update
  78.3 56.0 %reduce-scatter.2.cloned.1.call-done = bf16[64,4096]{1,0:T(8,128)(2,1)} async-done(((bf16[512,4096]{1,0:T(8,128)(2,1)}), bf16[64,4096]{1,0:T(8,128)(2,1)}) %reduce-scatter.2.cloned.1.call-update) | async-done | bytes 524304 | tf_op jit(solution)/shard_map/reduce_scatter | solution.py:158
  (1 shorter events, 0.0 us)
Async XLA Ops:
  6.5 63.3 %all-gather.2.cloned.1.call-start = ((), (), s32[]{:S(2)}) async-start(), calls=%async_computation.5 | async-start | bytes 4456448 | tf_op jit(solution)/shard_map/all_gather | solution.py:143
  36.9 13.6 %all-to-all-start.2 = ((bf16[8,64,128]{2,1,0:T(8,128)(2,1)}), bf16[8,64,128]{2,1,0:T(8,128)(2,1)S(1)}, u32[]{:S(2)}, u32[]{:S(2)}) async-start(bf16[8,64,128]{2,1,0:T(8,128)(2,1)} %get-tuple-element.12), calls=%async_computation.2 | async-start | bytes 262144 | tf_op jit(solution)/shard_map/all_to_all | solution.py:151
  42.7 91.6 %reduce-scatter.2.cloned.1.call-start = ((), (), s32[]{:S(2)}) async-start(), calls=%async_computation.6 | async-start | bytes 4718592 | tf_op jit(solution)/shard_map/reduce_scatter | solution.py:158
Sparse Core Ops, SparseCore 0:
  17.8 51.9 all-gather.1
  78.4 55.8 reduce-scatter.1

commit v5 on v4

--- a/solution.py
+++ b/solution.py
@@ -14,6 +14,7 @@
 TN = (((0,), (0,)), ((), ()))
 VMEM = pl.BlockSpec(memory_space=pltpu.VMEM)
 SMEM = pl.BlockSpec(memory_space=pltpu.SMEM)
+HBM = pl.BlockSpec(memory_space=pltpu.HBM)
 
 
 def call(kernel, out_shape, operands, flops, moved, scalars=0, vmem=24):
@@ -46,85 +47,113 @@
         c_ref[i] = (e_ref[i] + before).astype(BF16)
 
 
-def state_kernel(k_ref, v_ref, s_ref):
-    s = lax.dot_general(k_ref[...], v_ref[...], TN, preferred_element_type=F32)
-    s_ref[...] = s.astype(BF16)
+def fetch(sources, buffers, sems):
+    copies = [
+        pltpu.make_async_copy(source, buffer, sems.at[i])
+        for i, (source, buffer) in enumerate(zip(sources, buffers))
+    ]
+    for copy in copies:
+        copy.start()
+    for copy in copies:
+        copy.wait()
+
+
+def state_kernel(k_hbm, v_hbm, s_ref, k_ref, v_ref, sems):
+    fetch((k_hbm, v_hbm), (k_ref, v_ref), sems)
+    for h in range(4):
+        cols = slice(h * HD, (h + 1) * HD)
+        s = lax.dot_general(k_ref[:, cols], v_ref[:, cols], TN, preferred_element_type=F32)
+        s_ref[cols, :] = s.astype(BF16)
 
 
 def states(keys, values):
-    by_head = pl.BlockSpec((512, HD), lambda h: (0, h))
     return pl.pallas_call(
         state_kernel,
-        grid=(4,),
-        in_specs=[by_head, by_head],
-        out_specs=pl.BlockSpec((HD, HD), lambda h: (h, 0)),
+        in_specs=[HBM] * 2,
+        out_specs=VMEM,
         out_shape=shape(4 * HD, HD),
+        scratch_shapes=[pltpu.VMEM((512, 512), BF16)] * 2 + [pltpu.SemaphoreType.DMA((2,))],
         compiler_params=pltpu.CompilerParams(vmem_limit_bytes=56 * MIB),
         cost_estimate=pl.CostEstimate(flops=2**26, bytes_accessed=MIB, transcendentals=0),
     )(keys, values)
 
 
-def attention_kernel(q_ref, k_ref, v_ref, c_ref, o_ref):
+def attention_kernel(q_hbm, k_hbm, v_hbm, c_ref, o_ref, q_ref, k_ref, v_ref, sems):
+    fetch((q_hbm, k_hbm, v_hbm), (q_ref, k_ref, v_ref), sems)
     half = 256
     row = lax.broadcasted_iota(jnp.int32, (half, half), 0)
     col = lax.broadcasted_iota(jnp.int32, (half, half), 1)
     causal = row >= col
-    nt = (((1,), (1,)), ((), ()))
 
     def masked(q, k):
-        s = lax.dot_general(q, k, nt, preferred_element_type=F32)
+        s = lax.dot_general(q, k, NT, preferred_element_type=F32)
         return jnp.where(causal, s, 0.0).astype(BF16)
 
     def norm(a):
         r = lax.rsqrt(jnp.mean(a * a, axis=-1, keepdims=True) + 1e-06)
         return (a * r).astype(BF16)
 
-    c = c_ref[...]
-    q0, q1 = q_ref[:half], q_ref[half:]
-    k0, k1 = k_ref[:half], k_ref[half:]
-    v0, v1 = v_ref[:half], v_ref[half:]
-    a0 = jnp.dot(q0, c, preferred_element_type=F32)
-    a0 += jnp.dot(masked(q0, k0), v0, preferred_element_type=F32)
-    o_ref[:half] = norm(a0)
-    a1 = jnp.dot(q1, c, preferred_element_type=F32)
-    s10 = lax.dot_general(q1, k0, nt, preferred_element_type=F32).astype(BF16)
-    a1 += jnp.dot(s10, v0, preferred_element_type=F32)
-    a1 += jnp.dot(masked(q1, k1), v1, preferred_element_type=F32)
-    o_ref[half:] = norm(a1)
+    for h in range(4):
+        cols = slice(h * HD, (h + 1) * HD)
+        c = c_ref[cols]
+        q0, q1 = q_ref[:half, cols], q_ref[half:, cols]
+        k0, k1 = k_ref[:half, cols], k_ref[half:, cols]
+        v0, v1 = v_ref[:half, cols], v_ref[half:, cols]
+        a0 = jnp.dot(q0, c, preferred_element_type=F32)
+        a0 += jnp.dot(masked(q0, k0), v0, preferred_element_type=F32)
+        o_ref[:half, cols] = norm(a0)
+        a1 = jnp.dot(q1, c, preferred_element_type=F32)
+        s10 = lax.dot_general(q1, k0, NT, preferred_element_type=F32).astype(BF16)
+        a1 += jnp.dot(s10, v0, preferred_element_type=F32)
+        a1 += jnp.dot(masked(q1, k1), v1, preferred_element_type=F32)
+        o_ref[half:, cols] = norm(a1)
 
 
 def attention(queries, keys, values, carried):
-    by_head = pl.BlockSpec((512, HD), lambda h: (0, h))
     return pl.pallas_call(
         attention_kernel,
-        grid=(4,),
-        in_specs=[by_head, by_head, by_head, pl.BlockSpec((HD, HD), lambda h: (h, 0))],
-        out_specs=by_head,
-        out_shape=jax.ShapeDtypeStruct((512, 512), BF16),
+        in_specs=[HBM] * 3 + [VMEM],
+        out_specs=VMEM,
+        out_shape=shape(512, 512),
+        scratch_shapes=[pltpu.VMEM((512, 512), BF16)] * 3 + [pltpu.SemaphoreType.DMA((3,))],
         compiler_params=pltpu.CompilerParams(vmem_limit_bytes=56 * MIB),
-        cost_estimate=pl.CostEstimate(flops=2**29, bytes_accessed=2**21, transcendentals=2048),
+        cost_estimate=pl.CostEstimate(flops=2**29, bytes_accessed=2 * MIB, transcendentals=2048),
     )(queries, keys, values, carried)
 
 
-def project_kernel(n_ref, w_ref, o_ref):
+def project_kernel(n_ref, w_hbm, o_hbm, w_buf, o_buf, in_sems, out_sems):
+    incoming = [pltpu.make_async_copy(w_hbm.at[z], w_buf.at[z], in_sems.at[z]) for z in range(Z)]
+    for copy in incoming:
+        copy.start()
     n = n_ref[...]
-    w = jnp.concatenate([w_ref[0, c, x] for x in range(X) for c in range(C)], axis=0)
-    o = lax.dot_general(n, w, (((1,), (1,)), ((), ())), preferred_element_type=F32)
-    o_ref[...] = o.astype(BF16)
+    outgoing = []
+    for z in range(Z):
+        incoming[z].wait()
+        w = jnp.concatenate([w_buf[z, c, x] for x in range(X) for c in range(C)], axis=0)
+        o = lax.dot_general(n, w, NT, preferred_element_type=F32)
+        cols = slice(z * 512, (z + 1) * 512)
+        o_buf[:, cols] = o.astype(BF16)
+        copy = pltpu.make_async_copy(o_buf.at[:, cols], o_hbm.at[:, cols], out_sems.at[z])
+        copy.start()
+        outgoing.append(copy)
+    for copy in outgoing:
+        copy.wait()
 
 
 def project(normed, weight):
     return pl.pallas_call(
         project_kernel,
-        grid=(Z,),
-        in_specs=[
-            pl.BlockSpec((512, 512), lambda z: (0, 0)),
-            pl.BlockSpec((1, C, X, 64, 512), lambda z: (z, 0, 0, 0, 0)),
+        in_specs=[VMEM, HBM],
+        out_specs=HBM,
+        out_shape=shape(512, 4096),
+        scratch_shapes=[
+            pltpu.VMEM((Z, C, X, 64, 512), BF16),
+            pltpu.VMEM((512, 4096), BF16),
+            pltpu.SemaphoreType.DMA((Z,)),
+            pltpu.SemaphoreType.DMA((Z,)),
         ],
-        out_specs=pl.BlockSpec((512, 512), lambda z: (0, z)),
-        out_shape=jax.ShapeDtypeStruct((512, 4096), BF16),
         compiler_params=pltpu.CompilerParams(vmem_limit_bytes=56 * MIB),
-        cost_estimate=pl.CostEstimate(flops=2**31, bytes_accessed=2**23, transcendentals=0),
+        cost_estimate=pl.CostEstimate(flops=2**31, bytes_accessed=8 * MIB, transcendentals=0),
     )(normed, weight)
 
 
@@ -139,7 +168,7 @@
 def on_device(queries, keys, values, out_weight):
     plane = ("x", "core")
     w_x = everywhere(out_weight.T, "x", X)
-    w_x, keys, values = lax.optimization_barrier((w_x, keys, values))
+    w_x, keys = lax.optimization_barrier((w_x, keys))
     weight = lax.all_gather(w_x.reshape(X * 64, 512), ("z", "core"), axis=0, tiled=True)
     weight = weight.reshape(Z, C, X, 64, 512)
 

time: 142 us -> 139 us (0.979)
  waiting for transfers between devices: 65.8 us -> 69.2 us
  Pallas kernels: 17.9 us -> 14.9 us
  blocking collectives: 37.4 us -> 34.7 us
    pallas_call x3, Pallas kernels: 17.1 us -> 14.2 us  [the longest x1 6.85 us: project(): pl.pallas_call(project_kernel, in_specs=[VMEM, HBM], out_specs=HBM, out_s...]
    all_to_all x1, blocking collectives: 12.2 us -> 9.48 us  [on_device(): carried = lax.all_to_all(carried, plane, 0, 0).reshape(4 * HD, HD)]
    all_to_all x1, waiting for transfers between devices: 7.72 us -> 10.1 us  [on_device(): totals = lax.all_to_all(total, 'z', 0, 0)]
    all_gather x1, waiting for transfers between devices: 2 us -> 3.68 us  [on_device(): lax.all_gather(w_x.reshape(X * 64, 512), ('z', 'core'), axis=0, tiled=True)]
  transfers between devices with their start and end apart: 3 -> 3, of which waited for: 3 -> 3; matrix products, arithmetic and copies ran while one was open for 0% -> 0% of each run, Pallas kernels for 7% -> 6%
where the time goes in v5:
time: 139 us
  waiting for transfers between devices  69.2 us (50%)
  blocking collectives  34.7 us (25%)
  Pallas kernels  14.9 us (11%)
  between operations  13.4 us (10%)
  starting transfers between devices  5.84 us (4%)
    reduce_scatter x1, waiting for transfers between devices, on_device(): return lax.psum_scatter(terms, 'tp', scatter_dimension=0, tiled=True)  55.4 us
    all_to_all x1, blocking collectives, on_device(): pieces = lax.all_to_all(state, plane, 0, 0)  14.9 us
    all_to_all x1, blocking collectives, everywhere(): lax.all_to_all(jnp.broadcast_to(part[None], (size,) + part.shape), axis,...  10.3 us
    all_to_all x1, waiting for transfers between devices, on_device(): totals = lax.all_to_all(total, 'z', 0, 0)  10.1 us
    all_to_all x1, blocking collectives, on_device(): carried = lax.all_to_all(carried, plane, 0, 0).reshape(4 * HD, HD)  9.48 us
    pallas_call x1, Pallas kernels, project(): pl.pallas_call(project_kernel, in_specs=[VMEM, HBM], out_specs=HBM, out_s...  6.85 us
    all_to_all x1, starting transfers between devices, on_device(): totals = lax.all_to_all(total, 'z', 0, 0)  5.8 us
    pallas_call x1, Pallas kernels, attention(): pl.pallas_call(attention_kernel, in_specs=[HBM] * 3 + [VMEM], out_specs=V...  5.14 us
  transfers between devices with their start and end apart: 3, of which 3 were waited for; matrix products, arithmetic and copies ran while one was open for 0% of the time, Pallas kernels for 6%

profile of v5, /device:TPU:1, one launch (start us, length us, event | category | flops | bytes accessed | tf_op | source)
XLA Modules:
  0.0 139.0 jit_solution(6585845636107306320)
XLA Ops:
  6.5 0.0 all-gather.2.cloned.1.call-start
  6.5 0.9 broadcast_in_dim.4
  7.4 10.3 %all_to_all.20 = bf16[4,64,512]{2,1,0:T(8,128)(2,1)} all-to-all(bf16[4,64,512]{2,1,0:T(8,128)(2,1)S(1)} %broadcast_in_dim.4), channel_id=1, replica_groups=mesh['z'=8,'x'=4,'core'=2,'tp'=8] {'x'}, dimensions={0} | all-to-all | bytes 524288 | tf_op jit(solution)/shard_map/all_to_all | solution.py:165
  17.7 0.0 all-gather.2.cloned.1.call-update
  17.7 2.2 %shard_map.46 = bf16[512,128]{1,0:T(8,128)(2,1)} custom-call(bf16[512,512]{1,0:T(8,128)(2,1)} %k_hbm.1, bf16[512,512]{1,0:T(8,128)(2,1)} %v_hbm.3), custom_call_target="tpu_custom_call" | custom-call | flops 67108864 | bytes 1048576 | tf_op jit(solution)/shard_map/pallas_call | solution.py:70
  19.9 14.9 %all_to_all.21.p_ref = bf16[8,64,128]{2,1,0:T(8,128)(2,1)S(1)} all-to-all(bf16[8,64,128]{2,1,0:T(8,128)(2,1)} %bitcast.9), channel_id=1, replica_groups=mesh['z'=8,'x'=4,'core'=2,'tp'=8] {'x','core'}, dimensions={0} | all-to-all | bytes 262144 | tf_op jit(solution)/shard_map/all_to_all | solution.py:176
  34.8 0.7 shard_map.47
  35.5 5.8 %all-to-all-start.2 = ((bf16[8,64,128]{2,1,0:T(8,128)(2,1)}), bf16[8,64,128]{2,1,0:T(8,128)(2,1)S(1)}, u32[]{:S(2)}, u32[]{:S(2)}) async-start(bf16[8,64,128]{2,1,0:T(8,128)(2,1)} %get-tuple-element.10), calls=%async_computation.2 | async-start | bytes 262144 | tf_op jit(solution)/shard_map/all_to_all | solution.py:180
  41.3 0.0 reduce-scatter.2.cloned.1.call-start
  41.4 10.1 %all-to-all-done.2.t_ref = bf16[8,64,128]{2,1,0:T(8,128)(2,1)S(1)} async-done(((bf16[8,64,128]{2,1,0:T(8,128)(2,1)}), bf16[8,64,128]{2,1,0:T(8,128)(2,1)S(1)}, u32[]{:S(2)}, u32[]{:S(2)}) %all-to-all-start.2) | async-done | bytes 131104 | tf_op jit(solution)/shard_map/all_to_all | solution.py:180
  51.5 9.5 %all_to_all.22 = bf16[8,64,128]{2,1,0:T(8,128)(2,1)} all-to-all(bf16[8,64,128]{2,1,0:T(8,128)(2,1)S(1)} %shard_map.48), channel_id=1, replica_groups=mesh['z'=8,'x'=4,'core'=2,'tp'=8] {'x','core'}, dimensions={0} | all-to-all | bytes 262144 | tf_op jit(solution)/shard_map/all_to_all | solution.py:183
  61.0 5.1 %shard_map.49.n_ref = bf16[512,512]{1,0:T(8,128)(2,1)} custom-call(bf16[512,512]{1,0:T(8,128)(2,1)} %q_hbm.1, bf16[512,512]{1,0:T(8,128)(2,1)} %k_hbm.1, bf16[512,512]{1,0:T(8,128)(2,1)} %v_hbm.3, bf16[512,128]{1,0:T(8,128)(2,1)} %bitcast.8), custom_call_target="tpu_custom_call" | custom-call | flops 536870912 | bytes 2097152 | tf_op jit(solution)/shard_map/pallas_call | solution.py:113
  66.1 3.7 %all-gather.2.cloned.1.call-done = bf16[4096,512]{1,0:T(8,128)(2,1)} async-done(((bf16[256,512]{1,0:T(8,128)(2,1)}), bf16[4096,512]{1,0:T(8,128)(2,1)}) %all-gather.2.cloned.1.call-update) | async-done | bytes 4194320 | tf_op jit(solution)/shard_map/all_gather | solution.py:172
  69.8 6.8 %shard_map.50 = bf16[512,4096]{1,0:T(8,128)(2,1)} custom-call(bf16[512,512]{1,0:T(8,128)(2,1)} %shard_map.49.n_ref, bf16[8,2,4,64,512]{4,3,2,1,0:T(8,128)(2,1)} %bitcast.6), custom_call_target="tpu_custom_call" | custom-call | flops 2147483648 | bytes 8388608 | tf_op jit(solution)/shard_map/pallas_call | solution.py:144
  76.7 0.0 reduce-scatter.2.cloned.1.call-update
  76.7 55.4 %reduce-scatter.2.cloned.1.call-done = bf16[64,4096]{1,0:T(8,128)(2,1)} async-done(((bf16[512,4096]{1,0:T(8,128)(2,1)}), bf16[64,4096]{1,0:T(8,128)(2,1)}) %reduce-scatter.2.cloned.1.call-update) | async-done | bytes 524304 | tf_op jit(solution)/shard_map/reduce_scatter | solution.py:187
  (1 shorter events, 0.0 us)
Async XLA Ops:
  6.5 63.3 %all-gather.2.cloned.1.call-start = ((), (), s32[]{:S(2)}) async-start(), calls=%async_computation.5 | async-start | bytes 4456448 | tf_op jit(solution)/shard_map/all_gather | solution.py:172
  35.5 15.9 %all-to-all-start.2 = ((bf16[8,64,128]{2,1,0:T(8,128)(2,1)}), bf16[8,64,128]{2,1,0:T(8,128)(2,1)S(1)}, u32[]{:S(2)}, u32[]{:S(2)}) async-start(bf16[8,64,128]{2,1,0:T(8,128)(2,1)} %get-tuple-element.10), calls=%async_computation.2 | async-start | bytes 262144 | tf_op jit(solution)/shard_map/all_to_all | solution.py:180
  41.3 90.8 %reduce-scatter.2.cloned.1.call-start = ((), (), s32[]{:S(2)}) async-start(), calls=%async_computation.6 | async-start | bytes 4718592 | tf_op jit(solution)/shard_map/reduce_scatter | solution.py:187
Sparse Core Ops, SparseCore 0:
  17.8 51.9 all-gather.1
  76.8 55.2 reduce-scatter.1

commit v6 on v5

--- a/solution.py
+++ b/solution.py
@@ -9,6 +9,8 @@
 F32 = jnp.float32
 BF16 = jnp.bfloat16
 Z, X, C, Y = 8, 4, 2, 8
+MAIN, SIDE = 6, 2
+SHIFTS = (4, 3, 5, 2, 6, 1, 7, 0)
 MIB = 2**20
 NT = (((1,), (1,)), ((), ()))
 TN = (((0,), (0,)), ((), ()))
@@ -121,18 +123,25 @@
     )(queries, keys, values, carried)
 
 
+def tile(n, w, z):
+    w = jnp.concatenate([w[z, c, x] for x in range(X) for c in range(C)], axis=0)
+    return lax.dot_general(n, w, NT, preferred_element_type=F32).astype(BF16)
+
+
 def project_kernel(n_ref, w_hbm, o_hbm, w_buf, o_buf, in_sems, out_sems):
-    incoming = [pltpu.make_async_copy(w_hbm.at[z], w_buf.at[z], in_sems.at[z]) for z in range(Z)]
-    for copy in incoming:
-        copy.start()
+    pairs = range(MAIN // 2)
+    incoming = []
+    for i in pairs:
+        two = pl.ds(2 * i, 2)
+        incoming.append(pltpu.make_async_copy(w_hbm.at[two], w_buf.at[two], in_sems.at[i]))
+        incoming[i].start()
     n = n_ref[...]
     outgoing = []
-    for z in range(Z):
-        incoming[z].wait()
-        w = jnp.concatenate([w_buf[z, c, x] for x in range(X) for c in range(C)], axis=0)
-        o = lax.dot_general(n, w, NT, preferred_element_type=F32)
+    for z in range(MAIN):
+        if z % 2 == 0:
+            incoming[z // 2].wait()
         cols = slice(z * 512, (z + 1) * 512)
-        o_buf[:, cols] = o.astype(BF16)
+        o_buf[:, cols] = tile(n, w_buf, z)
         copy = pltpu.make_async_copy(o_buf.at[:, cols], o_hbm.at[:, cols], out_sems.at[z])
         copy.start()
         outgoing.append(copy)
@@ -145,16 +154,61 @@
         project_kernel,
         in_specs=[VMEM, HBM],
         out_specs=HBM,
-        out_shape=shape(512, 4096),
+        out_shape=shape(512, MAIN * 512),
         scratch_shapes=[
-            pltpu.VMEM((Z, C, X, 64, 512), BF16),
-            pltpu.VMEM((512, 4096), BF16),
-            pltpu.SemaphoreType.DMA((Z,)),
-            pltpu.SemaphoreType.DMA((Z,)),
+            pltpu.VMEM((MAIN, C, X, 64, 512), BF16),
+            pltpu.VMEM((512, MAIN * 512), BF16),
+            pltpu.SemaphoreType.DMA((MAIN // 2,)),
+            pltpu.SemaphoreType.DMA((MAIN,)),
         ],
         compiler_params=pltpu.CompilerParams(vmem_limit_bytes=56 * MIB),
-        cost_estimate=pl.CostEstimate(flops=2**31, bytes_accessed=8 * MIB, transcendentals=0),
+        cost_estimate=pl.CostEstimate(flops=2**31, bytes_accessed=6 * MIB, transcendentals=0),
     )(normed, weight)
+
+
+def side_kernel(y_ref, n_ref, w_ref, up_ref, down_ref, *refs):
+    starts = [pl.multiple_of(lax.rem(y_ref[0] + s, Y) * 64, 64) for s in SHIFTS]
+    n = jnp.concatenate([n_ref[pl.ds(at, 64), :] for at in starts], axis=0)
+    for z in range(SIDE):
+        o = tile(n, w_ref, z)
+        (up_ref if z < SIDE // 2 else down_ref)[...] = o[:64]
+        for i, ref in enumerate(refs):
+            ref[:, z * 512 : (z + 1) * 512] = o[(i + 1) * 64 : (i + 2) * 64]
+
+
+def half_step_kernel(u_ref, up_ref, d_ref, down_ref, uo_ref, do_ref):
+    half = up_ref.shape[1]
+    uo_ref[:, :half] = add(u_ref[:, :half], up_ref[...])
+    uo_ref[:, half:] = u_ref[:, half:]
+    do_ref[:, :half] = d_ref[:, :half]
+    do_ref[:, half:] = add(d_ref[:, half:], down_ref[...])
+
+
+def step_kernel(u_ref, up_ref, d_ref, down_ref, uo_ref, do_ref):
+    uo_ref[...] = add(u_ref[...], up_ref[...])
+    do_ref[...] = add(d_ref[...], down_ref[...])
+
+
+def add(a, b):
+    return (a.astype(F32) + b.astype(F32)).astype(BF16)
+
+
+def ring(up, down):
+    up = lax.ppermute(up, "tp", [(i, (i + 1) % Y) for i in range(Y)])
+    down = lax.ppermute(down, "tp", [(i, (i - 1) % Y) for i in range(Y)])
+    return lax.optimization_barrier((up, down))
+
+
+def ring_sum(y, normed, weight):
+    wide, half = shape(64, SIDE * 512), shape(64, SIDE * 256)
+    up, down, u3, d3, u2, d2, u1, d1, mine = call(
+        side_kernel, (half, half) + (wide,) * 7, (y, normed, weight), 2**29, 3 * MIB, 1, vmem=16
+    )
+    up, down = ring(up, down)
+    for kernel, u, d in ((half_step_kernel, u3, d3), (step_kernel, u2, d2), (step_kernel, u1, d1)):
+        up, down = call(kernel, (wide, wide), (u, up, d, down), 2**18, MIB, vmem=8)
+        up, down = ring(up, down)
+    return (mine.astype(F32) + up.astype(F32) + down.astype(F32)).astype(BF16)
 
 
 def shape(*dims, dtype=BF16):
@@ -184,7 +238,11 @@
 
     normed = attention(queries, keys, values, carried)
     terms = project(normed, weight)
-    return lax.psum_scatter(terms, "tp", scatter_dimension=0, tiled=True)
+    summed = lax.psum_scatter(terms, "tp", scatter_dimension=0, tiled=True)
+    side_weight, _ = lax.optimization_barrier((weight[MAIN:], terms))
+    y = lax.axis_index("tp").astype(jnp.int32)[None]
+    side = ring_sum(y, normed, side_weight)
+    return jnp.concatenate([summed, side], axis=1)
 
 
 def solution(mesh):

time: 139 us -> 138 us (level)
  waiting for transfers between devices: 69.2 us -> 38.9 us
  starting transfers between devices: 5.84 us -> 31.9 us
  other arithmetic: 0 us -> 1.88 us
    reduce_scatter x1, waiting for transfers between devices: 55.4 us -> 3.83 us  [on_device(): summed = lax.psum_scatter(terms, 'tp', scatter_dimension=0, tiled=True)]
    ppermute x0 -> x8, starting transfers between devices: none -> 26.1 us  [the longest x4 13.9 us: ring(): up = lax.ppermute(up, 'tp', [(i, (i + 1) % Y) for i in range(Y)])]
    ppermute x0 -> x8, waiting for transfers between devices: none -> 21.3 us  [the longest x4 11.7 us: ring(): up = lax.ppermute(up, 'tp', [(i, (i + 1) % Y) for i in range(Y)])]
    concatenate x0 -> x1, other arithmetic: none -> 1.82 us  [on_device(): return jnp.concatenate([summed, side], axis=1)]
    pallas_call x1, Pallas kernels: 6.85 us -> 5.43 us  [project(): pl.pallas_call(project_kernel, in_specs=[VMEM, HBM], out_specs=HBM, out_s...]
  transfers between devices with their start and end apart: 3 -> 11, of which waited for: 3 -> 10; matrix products, arithmetic and copies ran while one was open for 0% -> 1% of each run, Pallas kernels for 6% -> 7%
where the time goes in v6:
time: 138 us
  waiting for transfers between devices  38.9 us (28%)
  blocking collectives  34.7 us (25%)
  starting transfers between devices  31.9 us (23%)
  Pallas kernels  14.4 us (10%)
  between operations  13.6 us (10%)
  local copies, waits for them, and re-layouts  2.21 us (2%)
  other arithmetic  1.88 us (1%)
    all_to_all x1, blocking collectives, on_device(): pieces = lax.all_to_all(state, plane, 0, 0)  14.9 us
    ppermute x4, starting transfers between devices, ring(): up = lax.ppermute(up, 'tp', [(i, (i + 1) % Y) for i in range(Y)])  13.9 us
    ppermute x4, starting transfers between devices, ring(): down = lax.ppermute(down, 'tp', [(i, (i - 1) % Y) for i in range(Y)])  12.2 us
    ppermute x4, waiting for transfers between devices, ring(): up = lax.ppermute(up, 'tp', [(i, (i + 1) % Y) for i in range(Y)])  11.7 us
    all_to_all x1, blocking collectives, everywhere(): lax.all_to_all(jnp.broadcast_to(part[None], (size,) + part.shape), axis,...  10.3 us
    all_to_all x1, waiting for transfers between devices, on_device(): totals = lax.all_to_all(total, 'z', 0, 0)  10.1 us
    ppermute x4, waiting for transfers between devices, ring(): down = lax.ppermute(down, 'tp', [(i, (i - 1) % Y) for i in range(Y)])  9.57 us
    all_to_all x1, blocking collectives, on_device(): carried = lax.all_to_all(carried, plane, 0, 0).reshape(4 * HD, HD)  9.48 us
  transfers between devices with their start and end apart: 11, of which 10 were waited for; matrix products, arithmetic and copies ran while one was open for 1% of the time, Pallas kernels for 7%

profile of v6, /device:TPU:1, one launch (start us, length us, event | category | flops | bytes accessed | tf_op | source)
XLA Modules:
  0.0 137.5 jit_solution(8295122960003756680)
XLA Ops:
  6.5 0.9 broadcast_in_dim.12
  7.4 10.3 %all_to_all.20 = bf16[4,64,512]{2,1,0:T(8,128)(2,1)} all-to-all(bf16[4,64,512]{2,1,0:T(8,128)(2,1)S(1)} %broadcast_in_dim.12), channel_id=1, replica_groups=mesh['z'=8,'x'=4,'core'=2,'tp'=8] {'x'}, dimensions={0} | all-to-all | bytes 524288 | tf_op jit(solution)/shard_map/all_to_all | solution.py:219
  17.7 2.2 %shard_map.46 = bf16[512,128]{1,0:T(8,128)(2,1)} custom-call(bf16[512,512]{1,0:T(8,128)(2,1)} %k_hbm.1, bf16[512,512]{1,0:T(8,128)(2,1)} %v_hbm.3), custom_call_target="tpu_custom_call" | custom-call | flops 67108864 | bytes 1048576 | tf_op jit(solution)/shard_map/pallas_call | solution.py:72
  19.9 14.9 %all_to_all.21.p_ref = bf16[8,64,128]{2,1,0:T(8,128)(2,1)S(1)} all-to-all(bf16[8,64,128]{2,1,0:T(8,128)(2,1)} %bitcast.11), channel_id=1, replica_groups=mesh['z'=8,'x'=4,'core'=2,'tp'=8] {'x','core'}, dimensions={0} | all-to-all | bytes 262144 | tf_op jit(solution)/shard_map/all_to_all | solution.py:230
  34.8 0.7 shard_map.47
  35.5 5.8 %all-to-all-start.2 = ((bf16[8,64,128]{2,1,0:T(8,128)(2,1)}), bf16[8,64,128]{2,1,0:T(8,128)(2,1)S(1)}, u32[]{:S(2)}, u32[]{:S(2)}) async-start(bf16[8,64,128]{2,1,0:T(8,128)(2,1)} %get-tuple-element.34), calls=%async_computation.2 | async-start | bytes 262144 | tf_op jit(solution)/shard_map/all_to_all | solution.py:234
  41.4 10.1 %all-to-all-done.2.t_ref = bf16[8,64,128]{2,1,0:T(8,128)(2,1)S(1)} async-done(((bf16[8,64,128]{2,1,0:T(8,128)(2,1)}), bf16[8,64,128]{2,1,0:T(8,128)(2,1)S(1)}, u32[]{:S(2)}, u32[]{:S(2)}) %all-to-all-start.2) | async-done | bytes 131104 | tf_op jit(solution)/shard_map/all_to_all | solution.py:234
  51.5 9.5 %all_to_all.22 = bf16[8,64,128]{2,1,0:T(8,128)(2,1)} all-to-all(bf16[8,64,128]{2,1,0:T(8,128)(2,1)S(1)} %shard_map.48), channel_id=1, replica_groups=mesh['z'=8,'x'=4,'core'=2,'tp'=8] {'x','core'}, dimensions={0} | all-to-all | bytes 262144 | tf_op jit(solution)/shard_map/all_to_all | solution.py:237
  61.0 5.1 %shard_map.49.n_ref = bf16[512,512]{1,0:T(8,128)(2,1)} custom-call(bf16[512,512]{1,0:T(8,128)(2,1)} %q_hbm.1, bf16[512,512]{1,0:T(8,128)(2,1)} %k_hbm.1, bf16[512,512]{1,0:T(8,128)(2,1)} %v_hbm.3, bf16[512,128]{1,0:T(8,128)(2,1)} %bitcast.10), custom_call_target="tpu_custom_call" | custom-call | flops 536870912 | bytes 2097152 | tf_op jit(solution)/shard_map/pallas_call | solution.py:115
  66.1 3.7 %all-gather.2.cloned.1.call-done = bf16[4096,512]{1,0:T(8,128)(2,1)} async-done(((bf16[256,512]{1,0:T(8,128)(2,1)}), bf16[4096,512]{1,0:T(8,128)(2,1)}) %all-gather.2.cloned.1.call-update) | async-done | bytes 4194320 | tf_op jit(solution)/shard_map/all_gather | solution.py:226
  69.8 5.4 %shard_map.50 = bf16[512,3072]{1,0:T(8,128)(2,1)} custom-call(bf16[512,512]{1,0:T(8,128)(2,1)} %shard_map.49.n_ref, bf16[8,2,4,64,512]{4,3,2,1,0:T(8,128)(2,1)} %bitcast.12), custom_call_target="tpu_custom_call" | custom-call | flops 2147483648 | bytes 6291456 | tf_op jit(solution)/shard_map/pallas_call | solution.py:153
  75.3 1.3 slice.8
  76.6 0.7 shard_map.51
  77.4 3.1 %collective-permute-start = (bf16[64,512]{1,0:T(8,128)(2,1)S(1)}, bf16[64,512]{1,0:T(8,128)(2,1)S(1)}, u32[]{:S(2)}, u32[]{:S(2)}) collective-permute-start(bf16[64,512]{1,0:T(8,128)(2,1)S(1)} %get-tuple-element.42), channel_id=1, source_target_pairs={{0,1},{1,2},{2,3},{3,4},{4,5},{5,6},{6,7},{7,0},{8,9},{9,10},{10,1... | collective-permute-start | bytes 196616 | tf_op jit(solution)/shard_map/ppermute | solution.py:197
  80.5 3.4 %collective-permute-start.1 = (bf16[64,512]{1,0:T(8,128)(2,1)S(1)}, bf16[64,512]{1,0:T(8,128)(2,1)S(1)}, u32[]{:S(2)}, u32[]{:S(2)}) collective-permute-start(bf16[64,512]{1,0:T(8,128)(2,1)S(1)} %get-tuple-element.43), channel_id=1, source_target_pairs={{0,7},{1,0},{2,1},{3,2},{4,3},{5,4},{6,5},{7,6},{8,15},{9,8},{10,9... | collective-permute-start | bytes 196616 | tf_op jit(solution)/shard_map/ppermute | solution.py:198
  83.9 1.6 %collective-permute-done.1.down_ref = bf16[64,512]{1,0:T(8,128)(2,1)S(1)} collective-permute-done((bf16[64,512]{1,0:T(8,128)(2,1)S(1)}, bf16[64,512]{1,0:T(8,128)(2,1)S(1)}, u32[]{:S(2)}, u32[]{:S(2)}) %collective-permute-start.1) | collective-permute-done | bytes 65568 | tf_op jit(solution)/shard_map/ppermute | solution.py:198
  85.6 3.2 %collective-permute-start.2 = (bf16[64,1024]{1,0:T(8,128)(2,1)S(1)}, bf16[64,1024]{1,0:T(8,128)(2,1)S(1)}, u32[]{:S(2)}, u32[]{:S(2)}) collective-permute-start(bf16[64,1024]{1,0:T(8,128)(2,1)S(1)} %get-tuple-element.47), channel_id=1, source_target_pairs={{0,1},{1,2},{2,3},{3,4},{4,5},{5,6},{6,7},{7,0},{8,9},{9,10},{10,1... | collective-permute-start | bytes 393224 | tf_op jit(solution)/shard_map/ppermute | solution.py:197
  88.8 3.3 %collective-permute-start.3 = (bf16[64,1024]{1,0:T(8,128)(2,1)S(1)}, bf16[64,1024]{1,0:T(8,128)(2,1)S(1)}, u32[]{:S(2)}, u32[]{:S(2)}) collective-permute-start(bf16[64,1024]{1,0:T(8,128)(2,1)S(1)} %get-tuple-element.48), channel_id=1, source_target_pairs={{0,7},{1,0},{2,1},{3,2},{4,3},{5,4},{6,5},{7,6},{8,15},{9,8},{10,9... | collective-permute-start | bytes 393224 | tf_op jit(solution)/shard_map/ppermute | solution.py:198
  92.1 3.9 %collective-permute-done.2.up_ref = bf16[64,1024]{1,0:T(8,128)(2,1)S(1)} collective-permute-done((bf16[64,1024]{1,0:T(8,128)(2,1)S(1)}, bf16[64,1024]{1,0:T(8,128)(2,1)S(1)}, u32[]{:S(2)}, u32[]{:S(2)}) %collective-permute-start.2) | collective-permute-done | bytes 131104 | tf_op jit(solution)/shard_map/ppermute | solution.py:197
  96.0 3.2 %collective-permute-done.3.down_ref = bf16[64,1024]{1,0:T(8,128)(2,1)S(1)} collective-permute-done((bf16[64,1024]{1,0:T(8,128)(2,1)S(1)}, bf16[64,1024]{1,0:T(8,128)(2,1)S(1)}, u32[]{:S(2)}, u32[]{:S(2)}) %collective-permute-start.3) | collective-permute-done | bytes 131104 | tf_op jit(solution)/shard_map/ppermute | solution.py:198
  99.2 0.1 shard_map.53
  99.2 4.7 %collective-permute-start.4 = (bf16[64,1024]{1,0:T(8,128)(2,1)S(1)}, bf16[64,1024]{1,0:T(8,128)(2,1)S(1)}, u32[]{:S(2)}, u32[]{:S(2)}) collective-permute-start(bf16[64,1024]{1,0:T(8,128)(2,1)S(1)} %get-tuple-element.52), channel_id=1, source_target_pairs={{0,1},{1,2},{2,3},{3,4},{4,5},{5,6},{6,7},{7,0},{8,9},{9,10},{10,1... | collective-permute-start | bytes 393224 | tf_op jit(solution)/shard_map/ppermute | solution.py:197
  103.9 1.9 %collective-permute-start.5 = (bf16[64,1024]{1,0:T(8,128)(2,1)S(1)}, bf16[64,1024]{1,0:T(8,128)(2,1)S(1)}, u32[]{:S(2)}, u32[]{:S(2)}) collective-permute-start(bf16[64,1024]{1,0:T(8,128)(2,1)S(1)} %get-tuple-element.53), channel_id=1, source_target_pairs={{0,7},{1,0},{2,1},{3,2},{4,3},{5,4},{6,5},{7,6},{8,15},{9,8},{10,9... | collective-permute-start | bytes 393224 | tf_op jit(solution)/shard_map/ppermute | solution.py:198
  105.8 4.2 %collective-permute-done.4.up_ref = bf16[64,1024]{1,0:T(8,128)(2,1)S(1)} collective-permute-done((bf16[64,1024]{1,0:T(8,128)(2,1)S(1)}, bf16[64,1024]{1,0:T(8,128)(2,1)S(1)}, u32[]{:S(2)}, u32[]{:S(2)}) %collective-permute-start.4) | collective-permute-done | bytes 131104 | tf_op jit(solution)/shard_map/ppermute | solution.py:197
  110.0 2.9 %collective-permute-done.5.down_ref = bf16[64,1024]{1,0:T(8,128)(2,1)S(1)} collective-permute-done((bf16[64,1024]{1,0:T(8,128)(2,1)S(1)}, bf16[64,1024]{1,0:T(8,128)(2,1)S(1)}, u32[]{:S(2)}, u32[]{:S(2)}) %collective-permute-start.5) | collective-permute-done | bytes 131104 | tf_op jit(solution)/shard_map/ppermute | solution.py:198
  112.9 0.1 shard_map.54
  112.9 2.9 %collective-permute-start.6 = (bf16[64,1024]{1,0:T(8,128)(2,1)S(1)}, bf16[64,1024]{1,0:T(8,128)(2,1)S(1)}, u32[]{:S(2)}, u32[]{:S(2)}) collective-permute-start(bf16[64,1024]{1,0:T(8,128)(2,1)S(1)} %get-tuple-element.57), channel_id=1, source_target_pairs={{0,1},{1,2},{2,3},{3,4},{4,5},{5,6},{6,7},{7,0},{8,9},{9,10},{10,1... | collective-permute-start | bytes 393224 | tf_op jit(solution)/shard_map/ppermute | solution.py:197
  115.8 3.6 %collective-permute-start.7 = (bf16[64,1024]{1,0:T(8,128)(2,1)S(1)}, bf16[64,1024]{1,0:T(8,128)(2,1)S(1)}, u32[]{:S(2)}, u32[]{:S(2)}) collective-permute-start(bf16[64,1024]{1,0:T(8,128)(2,1)S(1)} %get-tuple-element.58), channel_id=1, source_target_pairs={{0,7},{1,0},{2,1},{3,2},{4,3},{5,4},{6,5},{7,6},{8,15},{9,8},{10,9... | collective-permute-start | bytes 393224 | tf_op jit(solution)/shard_map/ppermute | solution.py:198
  119.4 3.7 %collective-permute-done.6 = bf16[64,1024]{1,0:T(8,128)(2,1)S(1)} collective-permute-done((bf16[64,1024]{1,0:T(8,128)(2,1)S(1)}, bf16[64,1024]{1,0:T(8,128)(2,1)S(1)}, u32[]{:S(2)}, u32[]{:S(2)}) %collective-permute-start.6) | collective-permute-done | bytes 131104 | tf_op jit(solution)/shard_map/ppermute | solution.py:197
  123.1 1.9 %collective-permute-done.7 = bf16[64,1024]{1,0:T(8,128)(2,1)S(1)} collective-permute-done((bf16[64,1024]{1,0:T(8,128)(2,1)S(1)}, bf16[64,1024]{1,0:T(8,128)(2,1)S(1)}, u32[]{:S(2)}, u32[]{:S(2)}) %collective-permute-start.7) | collective-permute-done | bytes 131104 | tf_op jit(solution)/shard_map/ppermute | solution.py:198
  125.1 3.8 %reduce-scatter.2.cloned.1.call-done = bf16[64,3072]{1,0:T(8,128)(2,1)} async-done(((bf16[512,3072]{1,0:T(8,128)(2,1)}), bf16[64,3072]{1,0:T(8,128)(2,1)}) %reduce-scatter.2.cloned.1.call-update) | async-done | bytes 393232 | tf_op jit(solution)/shard_map/reduce_scatter | solution.py:241
  128.9 1.8 %pad_maximum_fusion = bf16[64,4096]{1,0:T(8,128)(2,1)} fusion(bf16[64,1024]{1,0:T(8,128)(2,1)S(1)} %add_convert_fusion, bf16[64,3072]{1,0:T(8,128)(2,1)} %reduce-scatter.2.cloned.1.call-done), kind=kLoop, calls=%fused_computation | loop fusion | flops 1048576 | bytes 1048576 | tf_op jit(solution)/shard_map/concatenate | solution.py:245
  (10 shorter events, 0.2 us)
Async XLA Ops:
  6.5 63.3 %all-gather.2.cloned.1.call-start = ((), (), s32[]{:S(2)}) async-start(), calls=%async_computation.5 | async-start | bytes 4456448 | tf_op jit(solution)/shard_map/all_gather | solution.py:226
  35.5 15.9 %all-to-all-start.2 = ((bf16[8,64,128]{2,1,0:T(8,128)(2,1)}), bf16[8,64,128]{2,1,0:T(8,128)(2,1)S(1)}, u32[]{:S(2)}, u32[]{:S(2)}) async-start(bf16[8,64,128]{2,1,0:T(8,128)(2,1)} %get-tuple-element.34), calls=%async_computation.2 | async-start | bytes 262144 | tf_op jit(solution)/shard_map/all_to_all | solution.py:234
  41.3 87.6 %reduce-scatter.2.cloned.1.call-start = ((), (), s32[]{:S(2)}) async-start(), calls=%async_computation.6 | async-start | bytes 3538944 | tf_op jit(solution)/shard_map/reduce_scatter | solution.py:241
  75.3 1.4 %copy-start = (bf16[512,512]{1,0:T(8,128)(2,1)S(1)}, bf16[512,512]{1,0:T(8,128)(2,1)}, u32[]{:S(2)}) copy-start(bf16[512,512]{1,0:T(8,128)(2,1)} %shard_map.49.n_ref) | copy-start | bytes 1572868
  77.4 6.5 %collective-permute-start = (bf16[64,512]{1,0:T(8,128)(2,1)S(1)}, bf16[64,512]{1,0:T(8,128)(2,1)S(1)}, u32[]{:S(2)}, u32[]{:S(2)}) collective-permute-start(bf16[64,512]{1,0:T(8,128)(2,1)S(1)} %get-tuple-element.42), channel_id=1, source_target_pairs={{0,1},{1,2},{2,3},{3,4},{4,5},{5,6},{6,7},{7,0},{8,9},{9,10},{10,1... | collective-permute-start | bytes 196616 | tf_op jit(solution)/shard_map/ppermute | solution.py:197
  80.5 5.0 %collective-permute-start.1 = (bf16[64,512]{1,0:T(8,128)(2,1)S(1)}, bf16[64,512]{1,0:T(8,128)(2,1)S(1)}, u32[]{:S(2)}, u32[]{:S(2)}) collective-permute-start(bf16[64,512]{1,0:T(8,128)(2,1)S(1)} %get-tuple-element.43), channel_id=1, source_target_pairs={{0,7},{1,0},{2,1},{3,2},{4,3},{5,4},{6,5},{7,6},{8,15},{9,8},{10,9... | collective-permute-start | bytes 196616 | tf_op jit(solution)/shard_map/ppermute | solution.py:198
  85.6 10.4 %collective-permute-start.2 = (bf16[64,1024]{1,0:T(8,128)(2,1)S(1)}, bf16[64,1024]{1,0:T(8,128)(2,1)S(1)}, u32[]{:S(2)}, u32[]{:S(2)}) collective-permute-start(bf16[64,1024]{1,0:T(8,128)(2,1)S(1)} %get-tuple-element.47), channel_id=1, source_target_pairs={{0,1},{1,2},{2,3},{3,4},{4,5},{5,6},{6,7},{7,0},{8,9},{9,10},{10,1... | collective-permute-start | bytes 393224 | tf_op jit(solution)/shard_map/ppermute | solution.py:197
  88.8 10.4 %collective-permute-start.3 = (bf16[64,1024]{1,0:T(8,128)(2,1)S(1)}, bf16[64,1024]{1,0:T(8,128)(2,1)S(1)}, u32[]{:S(2)}, u32[]{:S(2)}) collective-permute-start(bf16[64,1024]{1,0:T(8,128)(2,1)S(1)} %get-tuple-element.48), channel_id=1, source_target_pairs={{0,7},{1,0},{2,1},{3,2},{4,3},{5,4},{6,5},{7,6},{8,15},{9,8},{10,9... | collective-permute-start | bytes 393224 | tf_op jit(solution)/shard_map/ppermute | solution.py:198
  99.2 10.8 %collective-permute-start.4 = (bf16[64,1024]{1,0:T(8,128)(2,1)S(1)}, bf16[64,1024]{1,0:T(8,128)(2,1)S(1)}, u32[]{:S(2)}, u32[]{:S(2)}) collective-permute-start(bf16[64,1024]{1,0:T(8,128)(2,1)S(1)} %get-tuple-element.52), channel_id=1, source_target_pairs={{0,1},{1,2},{2,3},{3,4},{4,5},{5,6},{6,7},{7,0},{8,9},{9,10},{10,1... | collective-permute-start | bytes 393224 | tf_op jit(solution)/shard_map/ppermute | solution.py:197
  103.9 9.0 %collective-permute-start.5 = (bf16[64,1024]{1,0:T(8,128)(2,1)S(1)}, bf16[64,1024]{1,0:T(8,128)(2,1)S(1)}, u32[]{:S(2)}, u32[]{:S(2)}) collective-permute-start(bf16[64,1024]{1,0:T(8,128)(2,1)S(1)} %get-tuple-element.53), channel_id=1, source_target_pairs={{0,7},{1,0},{2,1},{3,2},{4,3},{5,4},{6,5},{7,6},{8,15},{9,8},{10,9... | collective-permute-start | bytes 393224 | tf_op jit(solution)/shard_map/ppermute | solution.py:198
  112.9 10.2 %collective-permute-start.6 = (bf16[64,1024]{1,0:T(8,128)(2,1)S(1)}, bf16[64,1024]{1,0:T(8,128)(2,1)S(1)}, u32[]{:S(2)}, u32[]{:S(2)}) collective-permute-start(bf16[64,1024]{1,0:T(8,128)(2,1)S(1)} %get-tuple-element.57), channel_id=1, source_target_pairs={{0,1},{1,2},{2,3},{3,4},{4,5},{5,6},{6,7},{7,0},{8,9},{9,10},{10,1... | collective-permute-start | bytes 393224 | tf_op jit(solution)/shard_map/ppermute | solution.py:197
  115.8 9.1 %collective-permute-start.7 = (bf16[64,1024]{1,0:T(8,128)(2,1)S(1)}, bf16[64,1024]{1,0:T(8,128)(2,1)S(1)}, u32[]{:S(2)}, u32[]{:S(2)}) collective-permute-start(bf16[64,1024]{1,0:T(8,128)(2,1)S(1)} %get-tuple-element.58), channel_id=1, source_target_pairs={{0,7},{1,0},{2,1},{3,2},{4,3},{5,4},{6,5},{7,6},{8,15},{9,8},{10,9... | collective-permute-start | bytes 393224 | tf_op jit(solution)/shard_map/ppermute | solution.py:198
Sparse Core Ops, SparseCore 0:
  17.8 51.9 all-gather.1
  75.4 53.4 reduce-scatter.1

commit v7 on v6

--- a/solution.py
+++ b/solution.py
@@ -9,7 +9,7 @@
 F32 = jnp.float32
 BF16 = jnp.bfloat16
 Z, X, C, Y = 8, 4, 2, 8
-MAIN, SIDE = 6, 2
+MAIN, SIDE = 5, 3
 SHIFTS = (4, 3, 5, 2, 6, 1, 7, 0)
 MIB = 2**20
 NT = (((1,), (1,)), ((), ()))
@@ -129,17 +129,16 @@
 
 
 def project_kernel(n_ref, w_hbm, o_hbm, w_buf, o_buf, in_sems, out_sems):
-    pairs = range(MAIN // 2)
-    incoming = []
-    for i in pairs:
-        two = pl.ds(2 * i, 2)
-        incoming.append(pltpu.make_async_copy(w_hbm.at[two], w_buf.at[two], in_sems.at[i]))
-        incoming[i].start()
+    incoming = {}
+    for i, z in enumerate(range(0, MAIN, 2)):
+        some = pl.ds(z, min(2, MAIN - z))
+        incoming[z] = pltpu.make_async_copy(w_hbm.at[some], w_buf.at[some], in_sems.at[i])
+        incoming[z].start()
     n = n_ref[...]
     outgoing = []
     for z in range(MAIN):
-        if z % 2 == 0:
-            incoming[z // 2].wait()
+        if z in incoming:
+            incoming[z].wait()
         cols = slice(z * 512, (z + 1) * 512)
         o_buf[:, cols] = tile(n, w_buf, z)
         copy = pltpu.make_async_copy(o_buf.at[:, cols], o_hbm.at[:, cols], out_sems.at[z])
@@ -158,7 +157,7 @@
         scratch_shapes=[
             pltpu.VMEM((MAIN, C, X, 64, 512), BF16),
             pltpu.VMEM((512, MAIN * 512), BF16),
-            pltpu.SemaphoreType.DMA((MAIN // 2,)),
+            pltpu.SemaphoreType.DMA((-(-MAIN // 2),)),
             pltpu.SemaphoreType.DMA((MAIN,)),
         ],
         compiler_params=pltpu.CompilerParams(vmem_limit_bytes=56 * MIB),
@@ -171,7 +170,9 @@
     n = jnp.concatenate([n_ref[pl.ds(at, 64), :] for at in starts], axis=0)
     for z in range(SIDE):
         o = tile(n, w_ref, z)
-        (up_ref if z < SIDE // 2 else down_ref)[...] = o[:64]
+        for at in (0, 256):
+            side, to = divmod(z * 512 + at, SIDE * 256)
+            (up_ref, down_ref)[side][:, to : to + 256] = o[:64, at : at + 256]
         for i, ref in enumerate(refs):
             ref[:, z * 512 : (z + 1) * 512] = o[(i + 1) * 64 : (i + 2) * 64]
 

time: 138 us -> 143 us (1.036)
  the two profiles are of different devices: /device:TPU:1 before, /device:TPU:4 now
where the time goes in v7:
time: 143 us; the launch traced here: 142 us
  waiting for transfers between devices  44 us (31%)
  starting transfers between devices  35 us (24%)
  blocking collectives  30.7 us (21%)
  Pallas kernels  14.5 us (10%)
  between operations  13.6 us (10%)
  local copies, waits for them, and re-layouts  2.43 us (2%)
  other arithmetic  1.87 us (1%)
    ppermute x4, waiting for transfers between devices, ring(): up = lax.ppermute(up, 'tp', [(i, (i + 1) % Y) for i in range(Y)])  16.4 us
    ppermute x4, starting transfers between devices, ring(): up = lax.ppermute(up, 'tp', [(i, (i + 1) % Y) for i in range(Y)])  16.4 us
    all_to_all x1, blocking collectives, everywhere(): lax.all_to_all(jnp.broadcast_to(part[None], (size,) + part.shape), axis,...  12.9 us
    ppermute x4, starting transfers between devices, ring(): down = lax.ppermute(down, 'tp', [(i, (i - 1) % Y) for i in range(Y)])  12.4 us
    all_to_all x1, waiting for transfers between devices, on_device(): totals = lax.all_to_all(total, 'z', 0, 0)  10.9 us
    ppermute x4, waiting for transfers between devices, ring(): down = lax.ppermute(down, 'tp', [(i, (i - 1) % Y) for i in range(Y)])  10.8 us
    all_to_all x1, blocking collectives, on_device(): pieces = lax.all_to_all(state, plane, 0, 0)  9.42 us
    all_to_all x1, blocking collectives, on_device(): carried = lax.all_to_all(carried, plane, 0, 0).reshape(4 * HD, HD)  8.38 us
  transfers between devices with their start and end apart: 11, of which 10 were waited for; matrix products, arithmetic and copies ran while one was open for 1% of the time, Pallas kernels for 7%

profile of v7, /device:TPU:4, one launch (start us, length us, event | category | flops | bytes accessed | tf_op | source)
XLA Modules:
  0.0 142.0 jit_solution(15717359284451638932)
XLA Ops:
  6.5 0.9 broadcast_in_dim.12
  7.4 12.9 %all_to_all.20 = bf16[4,64,512]{2,1,0:T(8,128)(2,1)} all-to-all(bf16[4,64,512]{2,1,0:T(8,128)(2,1)S(1)} %broadcast_in_dim.12), channel_id=1, replica_groups=mesh['z'=8,'x'=4,'core'=2,'tp'=8] {'x'}, dimensions={0} | all-to-all | bytes 524288 | tf_op jit(solution)/shard_map/all_to_all | solution.py:220
  20.3 2.2 %shard_map.46 = bf16[512,128]{1,0:T(8,128)(2,1)} custom-call(bf16[512,512]{1,0:T(8,128)(2,1)} %k_hbm.1, bf16[512,512]{1,0:T(8,128)(2,1)} %v_hbm.3), custom_call_target="tpu_custom_call" | custom-call | flops 67108864 | bytes 1048576 | tf_op jit(solution)/shard_map/pallas_call | solution.py:72
  22.6 9.4 %all_to_all.21.p_ref = bf16[8,64,128]{2,1,0:T(8,128)(2,1)S(1)} all-to-all(bf16[8,64,128]{2,1,0:T(8,128)(2,1)} %bitcast.12), channel_id=1, replica_groups=mesh['z'=8,'x'=4,'core'=2,'tp'=8] {'x','core'}, dimensions={0} | all-to-all | bytes 262144 | tf_op jit(solution)/shard_map/all_to_all | solution.py:231
  32.0 0.7 shard_map.47
  32.7 6.1 %all-to-all-start.2 = ((bf16[8,64,128]{2,1,0:T(8,128)(2,1)}), bf16[8,64,128]{2,1,0:T(8,128)(2,1)S(1)}, u32[]{:S(2)}, u32[]{:S(2)}) async-start(bf16[8,64,128]{2,1,0:T(8,128)(2,1)} %get-tuple-element.34), calls=%async_computation.2 | async-start | bytes 262144 | tf_op jit(solution)/shard_map/all_to_all | solution.py:235
  38.8 10.9 %all-to-all-done.2.t_ref = bf16[8,64,128]{2,1,0:T(8,128)(2,1)S(1)} async-done(((bf16[8,64,128]{2,1,0:T(8,128)(2,1)}), bf16[8,64,128]{2,1,0:T(8,128)(2,1)S(1)}, u32[]{:S(2)}, u32[]{:S(2)}) %all-to-all-start.2) | async-done | bytes 131104 | tf_op jit(solution)/shard_map/all_to_all | solution.py:235
  49.8 8.4 %all_to_all.22 = bf16[8,64,128]{2,1,0:T(8,128)(2,1)} all-to-all(bf16[8,64,128]{2,1,0:T(8,128)(2,1)S(1)} %shard_map.48), channel_id=1, replica_groups=mesh['z'=8,'x'=4,'core'=2,'tp'=8] {'x','core'}, dimensions={0} | all-to-all | bytes 262144 | tf_op jit(solution)/shard_map/all_to_all | solution.py:238
  58.1 5.1 %shard_map.49.n_ref = bf16[512,512]{1,0:T(8,128)(2,1)} custom-call(bf16[512,512]{1,0:T(8,128)(2,1)} %q_hbm.1, bf16[512,512]{1,0:T(8,128)(2,1)} %k_hbm.1, bf16[512,512]{1,0:T(8,128)(2,1)} %v_hbm.3, bf16[512,128]{1,0:T(8,128)(2,1)} %bitcast.11), custom_call_target="tpu_custom_call" | custom-call | flops 536870912 | bytes 2097152 | tf_op jit(solution)/shard_map/pallas_call | solution.py:115
  63.3 5.7 %all-gather.2.cloned.1.call-done = bf16[4096,512]{1,0:T(8,128)(2,1)} async-done(((bf16[256,512]{1,0:T(8,128)(2,1)}), bf16[4096,512]{1,0:T(8,128)(2,1)}) %all-gather.2.cloned.1.call-update) | async-done | bytes 4194320 | tf_op jit(solution)/shard_map/all_gather | solution.py:227
  69.0 5.1 %shard_map.50 = bf16[512,2560]{1,0:T(8,128)(2,1)} custom-call(bf16[512,512]{1,0:T(8,128)(2,1)} %shard_map.49.n_ref, bf16[8,2,4,64,512]{4,3,2,1,0:T(8,128)(2,1)} %bitcast.10), custom_call_target="tpu_custom_call" | custom-call | flops 2147483648 | bytes 6291456 | tf_op jit(solution)/shard_map/pallas_call | solution.py:152
  74.2 1.6 %slice.8 = bf16[1536,512]{1,0:T(8,128)(2,1)S(1)} slice(bf16[4096,512]{1,0:T(8,128)(2,1)} %all-gather.2.cloned.1.call-done), slice={[2560:4096], [0:512]} | slice | bytes 3145728 | tf_op jit(solution)/shard_map/slice | solution.py:243
  75.8 1.0 shard_map.51
  76.8 3.4 %collective-permute-start = (bf16[64,768]{1,0:T(8,128)(2,1)S(1)}, bf16[64,768]{1,0:T(8,128)(2,1)S(1)}, u32[]{:S(2)}, u32[]{:S(2)}) collective-permute-start(bf16[64,768]{1,0:T(8,128)(2,1)S(1)} %get-tuple-element.42), channel_id=1, source_target_pairs={{0,1},{1,2},{2,3},{3,4},{4,5},{5,6},{6,7},{7,0},{8,9},{9,10},{10,1... | collective-permute-start | bytes 294920 | tf_op jit(solution)/shard_map/ppermute | solution.py:198
  80.2 3.7 %collective-permute-start.1 = (bf16[64,768]{1,0:T(8,128)(2,1)S(1)}, bf16[64,768]{1,0:T(8,128)(2,1)S(1)}, u32[]{:S(2)}, u32[]{:S(2)}) collective-permute-start(bf16[64,768]{1,0:T(8,128)(2,1)S(1)} %get-tuple-element.43), channel_id=1, source_target_pairs={{0,7},{1,0},{2,1},{3,2},{4,3},{5,4},{6,5},{7,6},{8,15},{9,8},{10,9... | collective-permute-start | bytes 294920 | tf_op jit(solution)/shard_map/ppermute | solution.py:199
  83.9 1.0 collective-permute-done.up_ref
  84.9 1.9 %collective-permute-done.1.down_ref = bf16[64,768]{1,0:T(8,128)(2,1)S(1)} collective-permute-done((bf16[64,768]{1,0:T(8,128)(2,1)S(1)}, bf16[64,768]{1,0:T(8,128)(2,1)S(1)}, u32[]{:S(2)}, u32[]{:S(2)}) %collective-permute-start.1) | collective-permute-done | bytes 98336 | tf_op jit(solution)/shard_map/ppermute | solution.py:199
  86.9 3.5 %collective-permute-start.2 = (bf16[64,1536]{1,0:T(8,128)(2,1)S(1)}, bf16[64,1536]{1,0:T(8,128)(2,1)S(1)}, u32[]{:S(2)}, u32[]{:S(2)}) collective-permute-start(bf16[64,1536]{1,0:T(8,128)(2,1)S(1)} %get-tuple-element.47), channel_id=1, source_target_pairs={{0,1},{1,2},{2,3},{3,4},{4,5},{5,6},{6,7},{7,0},{8,9},{9,10},{10,1... | collective-permute-start | bytes 589832 | tf_op jit(solution)/shard_map/ppermute | solution.py:198
  90.3 3.8 %collective-permute-start.3 = (bf16[64,1536]{1,0:T(8,128)(2,1)S(1)}, bf16[64,1536]{1,0:T(8,128)(2,1)S(1)}, u32[]{:S(2)}, u32[]{:S(2)}) collective-permute-start(bf16[64,1536]{1,0:T(8,128)(2,1)S(1)} %get-tuple-element.48), channel_id=1, source_target_pairs={{0,7},{1,0},{2,1},{3,2},{4,3},{5,4},{6,5},{7,6},{8,15},{9,8},{10,9... | collective-permute-start | bytes 589832 | tf_op jit(solution)/shard_map/ppermute | solution.py:199
  94.2 7.1 %collective-permute-done.2.up_ref = bf16[64,1536]{1,0:T(8,128)(2,1)S(1)} collective-permute-done((bf16[64,1536]{1,0:T(8,128)(2,1)S(1)}, bf16[64,1536]{1,0:T(8,128)(2,1)S(1)}, u32[]{:S(2)}, u32[]{:S(2)}) %collective-permute-start.2) | collective-permute-done | bytes 196640 | tf_op jit(solution)/shard_map/ppermute | solution.py:198
  101.3 2.0 %collective-permute-done.3.down_ref = bf16[64,1536]{1,0:T(8,128)(2,1)S(1)} collective-permute-done((bf16[64,1536]{1,0:T(8,128)(2,1)S(1)}, bf16[64,1536]{1,0:T(8,128)(2,1)S(1)}, u32[]{:S(2)}, u32[]{:S(2)}) %collective-permute-start.3) | collective-permute-done | bytes 196640 | tf_op jit(solution)/shard_map/ppermute | solution.py:199
  103.3 0.1 shard_map.53
  103.4 5.5 %collective-permute-start.4 = (bf16[64,1536]{1,0:T(8,128)(2,1)S(1)}, bf16[64,1536]{1,0:T(8,128)(2,1)S(1)}, u32[]{:S(2)}, u32[]{:S(2)}) collective-permute-start(bf16[64,1536]{1,0:T(8,128)(2,1)S(1)} %get-tuple-element.52), channel_id=1, source_target_pairs={{0,1},{1,2},{2,3},{3,4},{4,5},{5,6},{6,7},{7,0},{8,9},{9,10},{10,1... | collective-permute-start | bytes 589832 | tf_op jit(solution)/shard_map/ppermute | solution.py:198
  109.0 1.9 %collective-permute-start.5 = (bf16[64,1536]{1,0:T(8,128)(2,1)S(1)}, bf16[64,1536]{1,0:T(8,128)(2,1)S(1)}, u32[]{:S(2)}, u32[]{:S(2)}) collective-permute-start(bf16[64,1536]{1,0:T(8,128)(2,1)S(1)} %get-tuple-element.53), channel_id=1, source_target_pairs={{0,7},{1,0},{2,1},{3,2},{4,3},{5,4},{6,5},{7,6},{8,15},{9,8},{10,9... | collective-permute-start | bytes 589832 | tf_op jit(solution)/shard_map/ppermute | solution.py:199
  110.9 6.6 %collective-permute-done.4.up_ref = bf16[64,1536]{1,0:T(8,128)(2,1)S(1)} collective-permute-done((bf16[64,1536]{1,0:T(8,128)(2,1)S(1)}, bf16[64,1536]{1,0:T(8,128)(2,1)S(1)}, u32[]{:S(2)}, u32[]{:S(2)}) %collective-permute-start.4) | collective-permute-done | bytes 196640 | tf_op jit(solution)/shard_map/ppermute | solution.py:198
  117.5 4.1 %collective-permute-done.5.down_ref = bf16[64,1536]{1,0:T(8,128)(2,1)S(1)} collective-permute-done((bf16[64,1536]{1,0:T(8,128)(2,1)S(1)}, bf16[64,1536]{1,0:T(8,128)(2,1)S(1)}, u32[]{:S(2)}, u32[]{:S(2)}) %collective-permute-start.5) | collective-permute-done | bytes 196640 | tf_op jit(solution)/shard_map/ppermute | solution.py:199
  121.6 0.1 shard_map.54
  121.7 4.0 %collective-permute-start.6 = (bf16[64,1536]{1,0:T(8,128)(2,1)S(1)}, bf16[64,1536]{1,0:T(8,128)(2,1)S(1)}, u32[]{:S(2)}, u32[]{:S(2)}) collective-permute-start(bf16[64,1536]{1,0:T(8,128)(2,1)S(1)} %get-tuple-element.57), channel_id=1, source_target_pairs={{0,1},{1,2},{2,3},{3,4},{4,5},{5,6},{6,7},{7,0},{8,9},{9,10},{10,1... | collective-permute-start | bytes 589832 | tf_op jit(solution)/shard_map/ppermute | solution.py:198
  125.7 3.0 %collective-permute-start.7 = (bf16[64,1536]{1,0:T(8,128)(2,1)S(1)}, bf16[64,1536]{1,0:T(8,128)(2,1)S(1)}, u32[]{:S(2)}, u32[]{:S(2)}) collective-permute-start(bf16[64,1536]{1,0:T(8,128)(2,1)S(1)} %get-tuple-element.58), channel_id=1, source_target_pairs={{0,7},{1,0},{2,1},{3,2},{4,3},{5,4},{6,5},{7,6},{8,15},{9,8},{10,9... | collective-permute-start | bytes 589832 | tf_op jit(solution)/shard_map/ppermute | solution.py:199
  128.7 1.7 %collective-permute-done.6 = bf16[64,1536]{1,0:T(8,128)(2,1)S(1)} collective-permute-done((bf16[64,1536]{1,0:T(8,128)(2,1)S(1)}, bf16[64,1536]{1,0:T(8,128)(2,1)S(1)}, u32[]{:S(2)}, u32[]{:S(2)}) %collective-permute-start.6) | collective-permute-done | bytes 196640 | tf_op jit(solution)/shard_map/ppermute | solution.py:198
  130.5 2.8 %collective-permute-done.7 = bf16[64,1536]{1,0:T(8,128)(2,1)S(1)} collective-permute-done((bf16[64,1536]{1,0:T(8,128)(2,1)S(1)}, bf16[64,1536]{1,0:T(8,128)(2,1)S(1)}, u32[]{:S(2)}, u32[]{:S(2)}) %collective-permute-start.7) | collective-permute-done | bytes 196640 | tf_op jit(solution)/shard_map/ppermute | solution.py:199
  133.4 1.8 %pad_maximum_fusion = bf16[64,4096]{1,0:T(8,128)(2,1)} fusion(bf16[64,1536]{1,0:T(8,128)(2,1)S(1)} %add_convert_fusion, bf16[64,2560]{1,0:T(8,128)(2,1)} %reduce-scatter.2.cloned.1.call-done), kind=kLoop, calls=%fused_computation | loop fusion | flops 1048576 | bytes 1048576 | tf_op jit(solution)/shard_map/concatenate | solution.py:246
  (10 shorter events, 0.3 us)
Async XLA Ops:
  6.5 62.5 %all-gather.2.cloned.1.call-start = ((), (), s32[]{:S(2)}) async-start(), calls=%async_computation.5 | async-start | bytes 4456448 | tf_op jit(solution)/shard_map/all_gather | solution.py:227
  32.7 17.1 %all-to-all-start.2 = ((bf16[8,64,128]{2,1,0:T(8,128)(2,1)}), bf16[8,64,128]{2,1,0:T(8,128)(2,1)S(1)}, u32[]{:S(2)}, u32[]{:S(2)}) async-start(bf16[8,64,128]{2,1,0:T(8,128)(2,1)} %get-tuple-element.34), calls=%async_computation.2 | async-start | bytes 262144 | tf_op jit(solution)/shard_map/all_to_all | solution.py:235
  38.8 94.6 %reduce-scatter.2.cloned.1.call-start = ((), (), s32[]{:S(2)}) async-start(), calls=%async_computation.6 | async-start | bytes 2949120 | tf_op jit(solution)/shard_map/reduce_scatter | solution.py:242
  74.2 1.6 %copy-start = (bf16[512,512]{1,0:T(8,128)(2,1)S(1)}, bf16[512,512]{1,0:T(8,128)(2,1)}, u32[]{:S(2)}) copy-start(bf16[512,512]{1,0:T(8,128)(2,1)} %shard_map.49.n_ref) | copy-start | bytes 1572868
  76.8 8.1 %collective-permute-start = (bf16[64,768]{1,0:T(8,128)(2,1)S(1)}, bf16[64,768]{1,0:T(8,128)(2,1)S(1)}, u32[]{:S(2)}, u32[]{:S(2)}) collective-permute-start(bf16[64,768]{1,0:T(8,128)(2,1)S(1)} %get-tuple-element.42), channel_id=1, source_target_pairs={{0,1},{1,2},{2,3},{3,4},{4,5},{5,6},{6,7},{7,0},{8,9},{9,10},{10,1... | collective-permute-start | bytes 294920 | tf_op jit(solution)/shard_map/ppermute | solution.py:198
  80.2 6.6 %collective-permute-start.1 = (bf16[64,768]{1,0:T(8,128)(2,1)S(1)}, bf16[64,768]{1,0:T(8,128)(2,1)S(1)}, u32[]{:S(2)}, u32[]{:S(2)}) collective-permute-start(bf16[64,768]{1,0:T(8,128)(2,1)S(1)} %get-tuple-element.43), channel_id=1, source_target_pairs={{0,7},{1,0},{2,1},{3,2},{4,3},{5,4},{6,5},{7,6},{8,15},{9,8},{10,9... | collective-permute-start | bytes 294920 | tf_op jit(solution)/shard_map/ppermute | solution.py:199
  86.9 14.5 %collective-permute-start.2 = (bf16[64,1536]{1,0:T(8,128)(2,1)S(1)}, bf16[64,1536]{1,0:T(8,128)(2,1)S(1)}, u32[]{:S(2)}, u32[]{:S(2)}) collective-permute-start(bf16[64,1536]{1,0:T(8,128)(2,1)S(1)} %get-tuple-element.47), channel_id=1, source_target_pairs={{0,1},{1,2},{2,3},{3,4},{4,5},{5,6},{6,7},{7,0},{8,9},{9,10},{10,1... | collective-permute-start | bytes 589832 | tf_op jit(solution)/shard_map/ppermute | solution.py:198
  90.3 13.0 %collective-permute-start.3 = (bf16[64,1536]{1,0:T(8,128)(2,1)S(1)}, bf16[64,1536]{1,0:T(8,128)(2,1)S(1)}, u32[]{:S(2)}, u32[]{:S(2)}) collective-permute-start(bf16[64,1536]{1,0:T(8,128)(2,1)S(1)} %get-tuple-element.48), channel_id=1, source_target_pairs={{0,7},{1,0},{2,1},{3,2},{4,3},{5,4},{6,5},{7,6},{8,15},{9,8},{10,9... | collective-permute-start | bytes 589832 | tf_op jit(solution)/shard_map/ppermute | solution.py:199
  103.4 14.1 %collective-permute-start.4 = (bf16[64,1536]{1,0:T(8,128)(2,1)S(1)}, bf16[64,1536]{1,0:T(8,128)(2,1)S(1)}, u32[]{:S(2)}, u32[]{:S(2)}) collective-permute-start(bf16[64,1536]{1,0:T(8,128)(2,1)S(1)} %get-tuple-element.52), channel_id=1, source_target_pairs={{0,1},{1,2},{2,3},{3,4},{4,5},{5,6},{6,7},{7,0},{8,9},{9,10},{10,1... | collective-permute-start | bytes 589832 | tf_op jit(solution)/shard_map/ppermute | solution.py:198
  109.0 12.6 %collective-permute-start.5 = (bf16[64,1536]{1,0:T(8,128)(2,1)S(1)}, bf16[64,1536]{1,0:T(8,128)(2,1)S(1)}, u32[]{:S(2)}, u32[]{:S(2)}) collective-permute-start(bf16[64,1536]{1,0:T(8,128)(2,1)S(1)} %get-tuple-element.53), channel_id=1, source_target_pairs={{0,7},{1,0},{2,1},{3,2},{4,3},{5,4},{6,5},{7,6},{8,15},{9,8},{10,9... | collective-permute-start | bytes 589832 | tf_op jit(solution)/shard_map/ppermute | solution.py:199
  121.7 8.8 %collective-permute-start.6 = (bf16[64,1536]{1,0:T(8,128)(2,1)S(1)}, bf16[64,1536]{1,0:T(8,128)(2,1)S(1)}, u32[]{:S(2)}, u32[]{:S(2)}) collective-permute-start(bf16[64,1536]{1,0:T(8,128)(2,1)S(1)} %get-tuple-element.57), channel_id=1, source_target_pairs={{0,1},{1,2},{2,3},{3,4},{4,5},{5,6},{6,7},{7,0},{8,9},{9,10},{10,1... | collective-permute-start | bytes 589832 | tf_op jit(solution)/shard_map/ppermute | solution.py:198
  125.7 7.6 %collective-permute-start.7 = (bf16[64,1536]{1,0:T(8,128)(2,1)S(1)}, bf16[64,1536]{1,0:T(8,128)(2,1)S(1)}, u32[]{:S(2)}, u32[]{:S(2)}) collective-permute-start(bf16[64,1536]{1,0:T(8,128)(2,1)S(1)} %get-tuple-element.58), channel_id=1, source_target_pairs={{0,7},{1,0},{2,1},{3,2},{4,3},{5,4},{6,5},{7,6},{8,15},{9,8},{10,9... | collective-permute-start | bytes 589832 | tf_op jit(solution)/shard_map/ppermute | solution.py:199
Sparse Core Ops, SparseCore 0:
  20.5 48.5 all-gather.1
  74.3 50.2 reduce-scatter.1

commit v8 on v7

--- a/solution.py
+++ b/solution.py
@@ -10,7 +10,6 @@
 BF16 = jnp.bfloat16
 Z, X, C, Y = 8, 4, 2, 8
 MAIN, SIDE = 5, 3
-SHIFTS = (4, 3, 5, 2, 6, 1, 7, 0)
 MIB = 2**20
 NT = (((1,), (1,)), ((), ()))
 TN = (((0,), (0,)), ((), ()))
@@ -165,51 +164,72 @@
     )(normed, weight)
 
 
-def side_kernel(y_ref, n_ref, w_ref, up_ref, down_ref, *refs):
-    starts = [pl.multiple_of(lax.rem(y_ref[0] + s, Y) * 64, 64) for s in SHIFTS]
-    n = jnp.concatenate([n_ref[pl.ds(at, 64), :] for at in starts], axis=0)
+def pair(own, other, core):
+    return jnp.where(core == 0, own, other), jnp.where(core == 0, other, own)
+
+
+def side_kernel(place_ref, n_ref, m_ref, w_ref, first_ref, *refs):
+    y, core = place_ref[0], place_ref[1]
+    shifts = [4] + [jnp.where(core == 0, 3 - i, 5 + i) for i in range(3)]
+    rows = []
+    for shift in shifts:
+        at = pl.ds(pl.multiple_of(lax.rem(y + shift, Y) * 64, 64), 64)
+        rows += pair(n_ref[at, :], m_ref[at, :], core)
+    rows.append(n_ref[pl.ds(pl.multiple_of(y * 64, 64), 64), :])
+    n = jnp.concatenate(rows, axis=0)
     for z in range(SIDE):
         o = tile(n, w_ref, z)
         for at in (0, 256):
             side, to = divmod(z * 512 + at, SIDE * 256)
-            (up_ref, down_ref)[side][:, to : to + 256] = o[:64, at : at + 256]
+
+            @pl.when(core == side)
+            def _(to=to, piece=o[:128, at : at + 256]):
+                first_ref[:, to : to + 256] = piece
+
+        cols = slice(z * 512, (z + 1) * 512)
         for i, ref in enumerate(refs):
-            ref[:, z * 512 : (z + 1) * 512] = o[(i + 1) * 64 : (i + 2) * 64]
-
-
-def half_step_kernel(u_ref, up_ref, d_ref, down_ref, uo_ref, do_ref):
-    half = up_ref.shape[1]
-    uo_ref[:, :half] = add(u_ref[:, :half], up_ref[...])
-    uo_ref[:, half:] = u_ref[:, half:]
-    do_ref[:, :half] = d_ref[:, :half]
-    do_ref[:, half:] = add(d_ref[:, half:], down_ref[...])
-
-
-def step_kernel(u_ref, up_ref, d_ref, down_ref, uo_ref, do_ref):
-    uo_ref[...] = add(u_ref[...], up_ref[...])
-    do_ref[...] = add(d_ref[...], down_ref[...])
+            ref[:, cols] = o[(i + 1) * 128 : (i + 1) * 128 + ref.shape[0]]
+
+
+def half_step_kernel(core_ref, p_ref, r_ref, o_ref):
+    half = r_ref.shape[1]
+    for side in range(C):
+        cols = slice(side * half, (side + 1) * half)
+        more = jnp.where(core_ref[0] == side, r_ref[...].astype(F32), 0.0)
+        o_ref[:, cols] = (p_ref[:, cols].astype(F32) + more).astype(BF16)
+
+
+def step_kernel(p_ref, r_ref, o_ref):
+    o_ref[...] = add(p_ref[...], r_ref[...])
+
+
+def split_kernel(core_ref, r_ref, keep_ref, send_ref):
+    keep_ref[...], send_ref[...] = pair(r_ref[:64], r_ref[64:], core_ref[0])
 
 
 def add(a, b):
     return (a.astype(F32) + b.astype(F32)).astype(BF16)
 
 
-def ring(up, down):
-    up = lax.ppermute(up, "tp", [(i, (i + 1) % Y) for i in range(Y)])
-    down = lax.ppermute(down, "tp", [(i, (i - 1) % Y) for i in range(Y)])
-    return lax.optimization_barrier((up, down))
-
-
-def ring_sum(y, normed, weight):
-    wide, half = shape(64, SIDE * 512), shape(64, SIDE * 256)
-    up, down, u3, d3, u2, d2, u1, d1, mine = call(
-        side_kernel, (half, half) + (wide,) * 7, (y, normed, weight), 2**29, 3 * MIB, 1, vmem=16
+def ring(part):
+    up = [(i, (i + 1) % Y) for i in range(Y)]
+    down = [(Y + i, Y + (i - 1) % Y) for i in range(Y)]
+    return lax.ppermute(part, ("core", "tp"), up + down)
+
+
+def ring_sum(y, core, normed, swapped, weight):
+    wide, half, mine = shape(128, SIDE * 512), shape(128, SIDE * 256), shape(64, SIDE * 512)
+    place = jnp.concatenate([y, core])
+    part, p3, p2, p1, mine = call(
+        side_kernel, (half, wide, wide, wide, mine), (place, normed, swapped, weight), 2**29, 3 * MIB, 1, vmem=16
     )
-    up, down = ring(up, down)
-    for kernel, u, d in ((half_step_kernel, u3, d3), (step_kernel, u2, d2), (step_kernel, u1, d1)):
-        up, down = call(kernel, (wide, wide), (u, up, d, down), 2**18, MIB, vmem=8)
-        up, down = ring(up, down)
-    return (mine.astype(F32) + up.astype(F32) + down.astype(F32)).astype(BF16)
+    part = call(half_step_kernel, wide, (core, p3, ring(part)), 2**18, MIB, 1, vmem=8)
+    part = call(step_kernel, wide, (p2, ring(part)), 2**18, MIB, vmem=8)
+    part = call(step_kernel, wide, (p1, ring(part)), 2**18, MIB, vmem=8)
+    size = shape(64, SIDE * 512)
+    keep, send = call(split_kernel, (size, size), (core, ring(part)), 2**18, MIB, 1, vmem=8)
+    got = lax.ppermute(send, "core", [(0, 1), (1, 0)])
+    return (mine.astype(F32) + keep.astype(F32) + got.astype(F32)).astype(BF16)
 
 
 def shape(*dims, dtype=BF16):
@@ -238,11 +258,14 @@
     carried = lax.all_to_all(carried, plane, 0, 0).reshape(4 * HD, HD)
 
     normed = attention(queries, keys, values, carried)
-    terms = project(normed, weight)
+    swapped = lax.ppermute(normed, "core", [(0, 1), (1, 0)])
+    swapped, main = lax.optimization_barrier((swapped, normed))
+    terms = project(main, weight)
     summed = lax.psum_scatter(terms, "tp", scatter_dimension=0, tiled=True)
     side_weight, _ = lax.optimization_barrier((weight[MAIN:], terms))
     y = lax.axis_index("tp").astype(jnp.int32)[None]
-    side = ring_sum(y, normed, side_weight)
+    core = lax.axis_index("core").astype(jnp.int32)[None]
+    side = ring_sum(y, core, normed, swapped, side_weight)
     return jnp.concatenate([summed, side], axis=1)
 
 

time: 143 us -> 148 us (1.035)
  the two profiles are of different devices: /device:TPU:4 before, /device:TPU:1 now
where the time goes in v8:
time: 148 us; the launch traced here: 147 us
  waiting for transfers between devices  44.5 us (30%)
  blocking collectives  34.6 us (23%)
  starting transfers between devices  34.4 us (23%)
  Pallas kernels  15.7 us (11%)
  between operations  13.5 us (9%)
  local copies, waits for them, and re-layouts  2.41 us (2%)
  other arithmetic  1.95 us (1%)
    ppermute x4, waiting for transfers between devices, ring(): return lax.ppermute(part, ('core', 'tp'), up + down)  31.5 us
    ppermute x4, starting transfers between devices, ring(): return lax.ppermute(part, ('core', 'tp'), up + down)  20.2 us
    all_to_all x1, blocking collectives, on_device(): pieces = lax.all_to_all(state, plane, 0, 0)  14.9 us
    all_to_all x1, blocking collectives, everywhere(): lax.all_to_all(jnp.broadcast_to(part[None], (size,) + part.shape), axis,...  10.3 us
    all_to_all x1, waiting for transfers between devices, on_device(): totals = lax.all_to_all(total, 'z', 0, 0)  10.1 us
    all_to_all x1, blocking collectives, on_device(): carried = lax.all_to_all(carried, plane, 0, 0).reshape(4 * HD, HD)  9.48 us
    all_to_all x1, starting transfers between devices, on_device(): totals = lax.all_to_all(total, 'z', 0, 0)  5.81 us
    ppermute x1, starting transfers between devices, ring_sum(): got = lax.ppermute(send, 'core', [(0, 1), (1, 0)])  5.58 us
  transfers between devices with their start and end apart: 9, of which 7 were waited for; matrix products, arithmetic and copies ran while one was open for 1% of the time, Pallas kernels for 7%

profile of v8, /device:TPU:1, one launch (start us, length us, event | category | flops | bytes accessed | tf_op | source)
XLA Modules:
  0.0 147.1 jit_solution(12825786538839463789)
XLA Ops:
  6.5 0.9 broadcast_in_dim.15
  7.4 10.3 %all_to_all.20 = bf16[4,64,512]{2,1,0:T(8,128)(2,1)} all-to-all(bf16[4,64,512]{2,1,0:T(8,128)(2,1)S(1)} %broadcast_in_dim.15), channel_id=1, replica_groups=mesh['z'=8,'x'=4,'core'=2,'tp'=8] {'x'}, dimensions={0} | all-to-all | bytes 524288 | tf_op jit(solution)/shard_map/all_to_all | solution.py:240
  17.7 2.2 %shard_map.46 = bf16[512,128]{1,0:T(8,128)(2,1)} custom-call(bf16[512,512]{1,0:T(8,128)(2,1)} %k_hbm.1, bf16[512,512]{1,0:T(8,128)(2,1)} %v_hbm.3), custom_call_target="tpu_custom_call" | custom-call | flops 67108864 | bytes 1048576 | tf_op jit(solution)/shard_map/pallas_call | solution.py:71
  19.9 14.9 %all_to_all.21.p_ref = bf16[8,64,128]{2,1,0:T(8,128)(2,1)S(1)} all-to-all(bf16[8,64,128]{2,1,0:T(8,128)(2,1)} %bitcast.13), channel_id=1, replica_groups=mesh['z'=8,'x'=4,'core'=2,'tp'=8] {'x','core'}, dimensions={0} | all-to-all | bytes 262144 | tf_op jit(solution)/shard_map/all_to_all | solution.py:251
  34.8 0.7 shard_map.47
  35.5 5.8 %all-to-all-start.2 = ((bf16[8,64,128]{2,1,0:T(8,128)(2,1)}), bf16[8,64,128]{2,1,0:T(8,128)(2,1)S(1)}, u32[]{:S(2)}, u32[]{:S(2)}) async-start(bf16[8,64,128]{2,1,0:T(8,128)(2,1)} %get-tuple-element.20), calls=%async_computation.2 | async-start | bytes 262144 | tf_op jit(solution)/shard_map/all_to_all | solution.py:255
  41.3 0.0 reduce-scatter.2.cloned.1.call-start
  41.4 10.1 %all-to-all-done.2.t_ref = bf16[8,64,128]{2,1,0:T(8,128)(2,1)S(1)} async-done(((bf16[8,64,128]{2,1,0:T(8,128)(2,1)}), bf16[8,64,128]{2,1,0:T(8,128)(2,1)S(1)}, u32[]{:S(2)}, u32[]{:S(2)}) %all-to-all-start.2) | async-done | bytes 131104 | tf_op jit(solution)/shard_map/all_to_all | solution.py:255
  51.5 9.5 %all_to_all.22 = bf16[8,64,128]{2,1,0:T(8,128)(2,1)} all-to-all(bf16[8,64,128]{2,1,0:T(8,128)(2,1)S(1)} %shard_map.48), channel_id=1, replica_groups=mesh['z'=8,'x'=4,'core'=2,'tp'=8] {'x','core'}, dimensions={0} | all-to-all | bytes 262144 | tf_op jit(solution)/shard_map/all_to_all | solution.py:258
  61.0 5.1 %shard_map.49.n_ref = bf16[512,512]{1,0:T(8,128)(2,1)} custom-call(bf16[512,512]{1,0:T(8,128)(2,1)} %q_hbm.1, bf16[512,512]{1,0:T(8,128)(2,1)} %k_hbm.1, bf16[512,512]{1,0:T(8,128)(2,1)} %v_hbm.3, bf16[512,128]{1,0:T(8,128)(2,1)} %bitcast.12), custom_call_target="tpu_custom_call" | custom-call | flops 536870912 | bytes 2097152 | tf_op jit(solution)/shard_map/pallas_call | solution.py:114
  66.1 2.8 %collective-permute-start = (bf16[512,512]{1,0:T(8,128)(2,1)}, bf16[512,512]{1,0:T(8,128)(2,1)S(1)}, u32[]{:S(2)}, u32[]{:S(2)}) collective-permute-start(bf16[512,512]{1,0:T(8,128)(2,1)} %shard_map.49.n_ref), channel_id=1, source_target_pairs={{0,8},{8,0},{1,9},{9,1},{2,10},{10,2},{3,11},{11,3},{4,12},{12,4},... | collective-permute-start | bytes 1572872 | tf_op jit(solution)/shard_map/ppermute | solution.py:261
  68.9 1.7 %collective-permute-done.m_ref = bf16[512,512]{1,0:T(8,128)(2,1)S(1)} collective-permute-done((bf16[512,512]{1,0:T(8,128)(2,1)}, bf16[512,512]{1,0:T(8,128)(2,1)S(1)}, u32[]{:S(2)}, u32[]{:S(2)}) %collective-permute-start) | collective-permute-done | bytes 524320 | tf_op jit(solution)/shard_map/ppermute | solution.py:261
  70.6 5.1 %shard_map.50 = bf16[512,2560]{1,0:T(8,128)(2,1)} custom-call(bf16[512,512]{1,0:T(8,128)(2,1)} %shard_map.49.n_ref, bf16[8,2,4,64,512]{4,3,2,1,0:T(8,128)(2,1)} %bitcast.11), custom_call_target="tpu_custom_call" | custom-call | flops 2147483648 | bytes 6291456 | tf_op jit(solution)/shard_map/pallas_call | solution.py:151
  75.8 0.1 pad_add_fusion.place_ref
  75.9 1.6 %slice.8 = bf16[1536,512]{1,0:T(8,128)(2,1)S(1)} slice(bf16[4096,512]{1,0:T(8,128)(2,1)} %all-gather.2.cloned.1.call-done), slice={[2560:4096], [0:512]} | slice | bytes 3145728 | tf_op jit(solution)/shard_map/slice | solution.py:265
  77.4 2.2 %shard_map.51 = (bf16[128,768]{1,0:T(8,128)(2,1)S(1)}, bf16[128,1536]{1,0:T(8,128)(2,1)S(1)}, bf16[128,1536]{1,0:T(8,128)(2,1)S(1)}, bf16[128,1536]{1,0:T(8,128)(2,1)S(1)}, bf16[64,1536]{1,0:T(8,128)(2,1)S(1)}) custom-call(s32[2]{0:T(128)S(1)} %pad_add_fusion.place_ref, bf16[512,512]{1,0:T(8,128)(2,1)S(1)} %copy-done, ...), custom_call_target="tpu_custom_call" | custom-call | flops 536870912 | bytes 3145728 | tf_op jit(solution)/shard_map/pallas_call | solution.py:22
  79.6 5.4 %collective-permute-start.1 = (bf16[128,768]{1,0:T(8,128)(2,1)S(1)}, bf16[128,768]{1,0:T(8,128)(2,1)S(1)}, u32[]{:S(2)}, u32[]{:S(2)}) collective-permute-start(bf16[128,768]{1,0:T(8,128)(2,1)S(1)} %get-tuple-element.30), channel_id=1, source_target_pairs={{0,1},{1,2},{2,3},{3,4},{4,5},{5,6},{6,7},{7,0},{8,15},{9,8},{10,9... | collective-permute-start | bytes 589832 | tf_op jit(solution)/shard_map/ppermute | solution.py:217
  85.0 3.4 %collective-permute-done.1.r_ref = bf16[128,768]{1,0:T(8,128)(2,1)S(1)} collective-permute-done((bf16[128,768]{1,0:T(8,128)(2,1)S(1)}, bf16[128,768]{1,0:T(8,128)(2,1)S(1)}, u32[]{:S(2)}, u32[]{:S(2)}) %collective-permute-start.1) | collective-permute-done | bytes 196640 | tf_op jit(solution)/shard_map/ppermute | solution.py:217
  88.5 0.1 shard_map.52
  88.6 5.5 %collective-permute-start.2 = (bf16[128,1536]{1,0:T(8,128)(2,1)S(1)}, bf16[128,1536]{1,0:T(8,128)(2,1)S(1)}, u32[]{:S(2)}, u32[]{:S(2)}) collective-permute-start(bf16[128,1536]{1,0:T(8,128)(2,1)S(1)} %shard_map.52), channel_id=1, source_target_pairs={{0,1},{1,2},{2,3},{3,4},{4,5},{5,6},{6,7},{7,0},{8,15},{9,8},{10,9... | collective-permute-start | bytes 1179656 | tf_op jit(solution)/shard_map/ppermute | solution.py:217
  94.1 12.9 %collective-permute-done.2.r_ref = bf16[128,1536]{1,0:T(8,128)(2,1)S(1)} collective-permute-done((bf16[128,1536]{1,0:T(8,128)(2,1)S(1)}, bf16[128,1536]{1,0:T(8,128)(2,1)S(1)}, u32[]{:S(2)}, u32[]{:S(2)}) %collective-permute-start.2) | collective-permute-done | bytes 393248 | tf_op jit(solution)/shard_map/ppermute | solution.py:217
  107.0 0.1 shard_map.53
  107.1 5.4 %collective-permute-start.3 = (bf16[128,1536]{1,0:T(8,128)(2,1)S(1)}, bf16[128,1536]{1,0:T(8,128)(2,1)S(1)}, u32[]{:S(2)}, u32[]{:S(2)}) collective-permute-start(bf16[128,1536]{1,0:T(8,128)(2,1)S(1)} %shard_map.53), channel_id=1, source_target_pairs={{0,1},{1,2},{2,3},{3,4},{4,5},{5,6},{6,7},{7,0},{8,15},{9,8},{10,9... | collective-permute-start | bytes 1179656 | tf_op jit(solution)/shard_map/ppermute | solution.py:217
  112.5 10.3 %collective-permute-done.3.r_ref = bf16[128,1536]{1,0:T(8,128)(2,1)S(1)} collective-permute-done((bf16[128,1536]{1,0:T(8,128)(2,1)S(1)}, bf16[128,1536]{1,0:T(8,128)(2,1)S(1)}, u32[]{:S(2)}, u32[]{:S(2)}) %collective-permute-start.3) | collective-permute-done | bytes 393248 | tf_op jit(solution)/shard_map/ppermute | solution.py:217
  122.8 0.1 shard_map.54
  122.9 3.9 %collective-permute-start.4 = (bf16[128,1536]{1,0:T(8,128)(2,1)S(1)}, bf16[128,1536]{1,0:T(8,128)(2,1)S(1)}, u32[]{:S(2)}, u32[]{:S(2)}) collective-permute-start(bf16[128,1536]{1,0:T(8,128)(2,1)S(1)} %shard_map.54), channel_id=1, source_target_pairs={{0,1},{1,2},{2,3},{3,4},{4,5},{5,6},{6,7},{7,0},{8,15},{9,8},{10,9... | collective-permute-start | bytes 1179656 | tf_op jit(solution)/shard_map/ppermute | solution.py:217
  126.8 4.9 %collective-permute-done.4.r_ref = bf16[128,1536]{1,0:T(8,128)(2,1)S(1)} collective-permute-done((bf16[128,1536]{1,0:T(8,128)(2,1)S(1)}, bf16[128,1536]{1,0:T(8,128)(2,1)S(1)}, u32[]{:S(2)}, u32[]{:S(2)}) %collective-permute-start.4) | collective-permute-done | bytes 393248 | tf_op jit(solution)/shard_map/ppermute | solution.py:217
  131.7 5.6 %collective-permute-start.5 = (bf16[64,1536]{1,0:T(8,128)(2,1)S(1)}, bf16[64,1536]{1,0:T(8,128)(2,1)S(1)}, u32[]{:S(2)}, u32[]{:S(2)}) collective-permute-start(bf16[64,1536]{1,0:T(8,128)(2,1)S(1)} %get-tuple-element.32), channel_id=1, source_target_pairs={{0,8},{8,0},{1,9},{9,1},{2,10},{10,2},{3,11},{11,3},{4,12},{12,4},... | collective-permute-start | bytes 589832 | tf_op jit(solution)/shard_map/ppermute | solution.py:231
  137.3 1.0 collective-permute-done.5
  138.4 0.1 add_convert_fusion
  138.5 0.0 reduce-scatter.2.cloned.1.call-done
  138.5 1.8 %pad_maximum_fusion = bf16[64,4096]{1,0:T(8,128)(2,1)} fusion(bf16[64,1536]{1,0:T(8,128)(2,1)S(1)} %add_convert_fusion, bf16[64,2560]{1,0:T(8,128)(2,1)} %reduce-scatter.2.cloned.1.call-done), kind=kLoop, calls=%fused_computation | loop fusion | flops 1048576 | bytes 1048576 | tf_op jit(solution)/shard_map/concatenate | solution.py:269
  (8 shorter events, 0.1 us)
Async XLA Ops:
  6.5 64.1 %all-gather.2.cloned.1.call-start = ((), (), s32[]{:S(2)}) async-start(), calls=%async_computation.5 | async-start | bytes 4456448 | tf_op jit(solution)/shard_map/all_gather | solution.py:247
  35.5 16.0 %all-to-all-start.2 = ((bf16[8,64,128]{2,1,0:T(8,128)(2,1)}), bf16[8,64,128]{2,1,0:T(8,128)(2,1)S(1)}, u32[]{:S(2)}, u32[]{:S(2)}) async-start(bf16[8,64,128]{2,1,0:T(8,128)(2,1)} %get-tuple-element.20), calls=%async_computation.2 | async-start | bytes 262144 | tf_op jit(solution)/shard_map/all_to_all | solution.py:255
  41.3 97.2 %reduce-scatter.2.cloned.1.call-start = ((), (), s32[]{:S(2)}) async-start(), calls=%async_computation.6 | async-start | bytes 2949120 | tf_op jit(solution)/shard_map/reduce_scatter | solution.py:264
  66.1 4.5 %collective-permute-start = (bf16[512,512]{1,0:T(8,128)(2,1)}, bf16[512,512]{1,0:T(8,128)(2,1)S(1)}, u32[]{:S(2)}, u32[]{:S(2)}) collective-permute-start(bf16[512,512]{1,0:T(8,128)(2,1)} %shard_map.49.n_ref), channel_id=1, source_target_pairs={{0,8},{8,0},{1,9},{9,1},{2,10},{10,2},{3,11},{11,3},{4,12},{12,4},... | collective-permute-start | bytes 1572872 | tf_op jit(solution)/shard_map/ppermute | solution.py:261
  75.8 1.7 %copy-start = (bf16[512,512]{1,0:T(8,128)(2,1)S(1)}, bf16[512,512]{1,0:T(8,128)(2,1)}, u32[]{:S(2)}) copy-start(bf16[512,512]{1,0:T(8,128)(2,1)} %shard_map.49.n_ref) | copy-start | bytes 1572868
  79.6 8.8 %collective-permute-start.1 = (bf16[128,768]{1,0:T(8,128)(2,1)S(1)}, bf16[128,768]{1,0:T(8,128)(2,1)S(1)}, u32[]{:S(2)}, u32[]{:S(2)}) collective-permute-start(bf16[128,768]{1,0:T(8,128)(2,1)S(1)} %get-tuple-element.30), channel_id=1, source_target_pairs={{0,1},{1,2},{2,3},{3,4},{4,5},{5,6},{6,7},{7,0},{8,15},{9,8},{10,9... | collective-permute-start | bytes 589832 | tf_op jit(solution)/shard_map/ppermute | solution.py:217
  88.6 18.4 %collective-permute-start.2 = (bf16[128,1536]{1,0:T(8,128)(2,1)S(1)}, bf16[128,1536]{1,0:T(8,128)(2,1)S(1)}, u32[]{:S(2)}, u32[]{:S(2)}) collective-permute-start(bf16[128,1536]{1,0:T(8,128)(2,1)S(1)} %shard_map.52), channel_id=1, source_target_pairs={{0,1},{1,2},{2,3},{3,4},{4,5},{5,6},{6,7},{7,0},{8,15},{9,8},{10,9... | collective-permute-start | bytes 1179656 | tf_op jit(solution)/shard_map/ppermute | solution.py:217
  107.1 15.7 %collective-permute-start.3 = (bf16[128,1536]{1,0:T(8,128)(2,1)S(1)}, bf16[128,1536]{1,0:T(8,128)(2,1)S(1)}, u32[]{:S(2)}, u32[]{:S(2)}) collective-permute-start(bf16[128,1536]{1,0:T(8,128)(2,1)S(1)} %shard_map.53), channel_id=1, source_target_pairs={{0,1},{1,2},{2,3},{3,4},{4,5},{5,6},{6,7},{7,0},{8,15},{9,8},{10,9... | collective-permute-start | bytes 1179656 | tf_op jit(solution)/shard_map/ppermute | solution.py:217
  122.9 8.8 %collective-permute-start.4 = (bf16[128,1536]{1,0:T(8,128)(2,1)S(1)}, bf16[128,1536]{1,0:T(8,128)(2,1)S(1)}, u32[]{:S(2)}, u32[]{:S(2)}) collective-permute-start(bf16[128,1536]{1,0:T(8,128)(2,1)S(1)} %shard_map.54), channel_id=1, source_target_pairs={{0,1},{1,2},{2,3},{3,4},{4,5},{5,6},{6,7},{7,0},{8,15},{9,8},{10,9... | collective-permute-start | bytes 1179656 | tf_op jit(solution)/shard_map/ppermute | solution.py:217
  131.7 6.6 %collective-permute-start.5 = (bf16[64,1536]{1,0:T(8,128)(2,1)S(1)}, bf16[64,1536]{1,0:T(8,128)(2,1)S(1)}, u32[]{:S(2)}, u32[]{:S(2)}) collective-permute-start(bf16[64,1536]{1,0:T(8,128)(2,1)S(1)} %get-tuple-element.32), channel_id=1, source_target_pairs={{0,8},{8,0},{1,9},{9,1},{2,10},{10,2},{3,11},{11,3},{4,12},{12,4},... | collective-permute-start | bytes 589832 | tf_op jit(solution)/shard_map/ppermute | solution.py:231
Sparse Core Ops, SparseCore 0:
  17.8 52.0 all-gather.1
  75.9 45.7 reduce-scatter.1

commit v9 on v6

--- a/solution.py
+++ b/solution.py
@@ -124,7 +124,7 @@
 
 
 def tile(n, w, z):
-    w = jnp.concatenate([w[z, c, x] for x in range(X) for c in range(C)], axis=0)
+    w = jnp.concatenate([w[c, z, x] for x in range(X) for c in range(C)], axis=0)
     return lax.dot_general(n, w, NT, preferred_element_type=F32).astype(BF16)
 
 
@@ -133,7 +133,7 @@
     incoming = []
     for i in pairs:
         two = pl.ds(2 * i, 2)
-        incoming.append(pltpu.make_async_copy(w_hbm.at[two], w_buf.at[two], in_sems.at[i]))
+        incoming.append(pltpu.make_async_copy(w_hbm.at[:, two], w_buf.at[:, two], in_sems.at[i]))
         incoming[i].start()
     n = n_ref[...]
     outgoing = []
@@ -156,7 +156,7 @@
         out_specs=HBM,
         out_shape=shape(512, MAIN * 512),
         scratch_shapes=[
-            pltpu.VMEM((MAIN, C, X, 64, 512), BF16),
+            pltpu.VMEM((C, MAIN, X, 64, 512), BF16),
             pltpu.VMEM((512, MAIN * 512), BF16),
             pltpu.SemaphoreType.DMA((MAIN // 2,)),
             pltpu.SemaphoreType.DMA((MAIN,)),
@@ -223,8 +223,8 @@
     plane = ("x", "core")
     w_x = everywhere(out_weight.T, "x", X)
     w_x, keys = lax.optimization_barrier((w_x, keys))
-    weight = lax.all_gather(w_x.reshape(X * 64, 512), ("z", "core"), axis=0, tiled=True)
-    weight = weight.reshape(Z, C, X, 64, 512)
+    weight = lax.all_gather(w_x.reshape(X * 64, 512), ("core", "z"), axis=0, tiled=True)
+    weight = weight.reshape(C, Z, X, 64, 512)
 
     state = states(keys, values).reshape(8, 64, HD)
     pieces = lax.all_to_all(state, plane, 0, 0)
@@ -239,7 +239,7 @@
     normed = attention(queries, keys, values, carried)
     terms = project(normed, weight)
     summed = lax.psum_scatter(terms, "tp", scatter_dimension=0, tiled=True)
-    side_weight, _ = lax.optimization_barrier((weight[MAIN:], terms))
+    side_weight, _ = lax.optimization_barrier((weight[:, MAIN:], terms))
     y = lax.axis_index("tp").astype(jnp.int32)[None]
     side = ring_sum(y, normed, side_weight)
     return jnp.concatenate([summed, side], axis=1)

time: 138 us -> 138 us (level)
  no operation moved by 1% of the time
where the time goes in v9:
time: 138 us
  waiting for transfers between devices  39 us (28%)
  blocking collectives  34.7 us (25%)
  starting transfers between devices  31.9 us (23%)
  Pallas kernels  14.4 us (10%)
  between operations  13.6 us (10%)
  local copies, waits for them, and re-layouts  2.23 us (2%)
  other arithmetic  1.88 us (1%)
    all_to_all x1, blocking collectives, on_device(): pieces = lax.all_to_all(state, plane, 0, 0)  14.9 us
    ppermute x4, starting transfers between devices, ring(): up = lax.ppermute(up, 'tp', [(i, (i + 1) % Y) for i in range(Y)])  13.8 us
    ppermute x4, starting transfers between devices, ring(): down = lax.ppermute(down, 'tp', [(i, (i - 1) % Y) for i in range(Y)])  12.2 us
    ppermute x4, waiting for transfers between devices, ring(): up = lax.ppermute(up, 'tp', [(i, (i + 1) % Y) for i in range(Y)])  11.8 us
    all_to_all x1, blocking collectives, everywhere(): lax.all_to_all(jnp.broadcast_to(part[None], (size,) + part.shape), axis,...  10.3 us
    all_to_all x1, waiting for transfers between devices, on_device(): totals = lax.all_to_all(total, 'z', 0, 0)  10.1 us
    ppermute x4, waiting for transfers between devices, ring(): down = lax.ppermute(down, 'tp', [(i, (i - 1) % Y) for i in range(Y)])  9.68 us
    all_to_all x1, blocking collectives, on_device(): carried = lax.all_to_all(carried, plane, 0, 0).reshape(4 * HD, HD)  9.49 us
  transfers between devices with their start and end apart: 11, of which 10 were waited for; matrix products, arithmetic and copies ran while one was open for 1% of the time, Pallas kernels for 7%

profile of v9, /device:TPU:1, one launch (start us, length us, event | category | flops | bytes accessed | tf_op | source)
XLA Modules:
  0.0 137.6 jit_solution(15130788325322700437)
XLA Ops:
  6.5 0.9 broadcast_in_dim.12
  7.4 10.3 %all_to_all.20 = bf16[4,64,512]{2,1,0:T(8,128)(2,1)} all-to-all(bf16[4,64,512]{2,1,0:T(8,128)(2,1)S(1)} %broadcast_in_dim.12), channel_id=1, replica_groups=mesh['z'=8,'x'=4,'core'=2,'tp'=8] {'x'}, dimensions={0} | all-to-all | bytes 524288 | tf_op jit(solution)/shard_map/all_to_all | solution.py:219
  17.7 2.2 %shard_map.46 = bf16[512,128]{1,0:T(8,128)(2,1)} custom-call(bf16[512,512]{1,0:T(8,128)(2,1)} %k_hbm.1, bf16[512,512]{1,0:T(8,128)(2,1)} %v_hbm.3), custom_call_target="tpu_custom_call" | custom-call | flops 67108864 | bytes 1048576 | tf_op jit(solution)/shard_map/pallas_call | solution.py:72
  19.9 14.9 %all_to_all.21.p_ref = bf16[8,64,128]{2,1,0:T(8,128)(2,1)S(1)} all-to-all(bf16[8,64,128]{2,1,0:T(8,128)(2,1)} %bitcast.9), channel_id=1, replica_groups=mesh['z'=8,'x'=4,'core'=2,'tp'=8] {'x','core'}, dimensions={0} | all-to-all | bytes 262144 | tf_op jit(solution)/shard_map/all_to_all | solution.py:230
  34.8 0.7 shard_map.47
  35.5 5.8 %all-to-all-start.2 = ((bf16[8,64,128]{2,1,0:T(8,128)(2,1)}), bf16[8,64,128]{2,1,0:T(8,128)(2,1)S(1)}, u32[]{:S(2)}, u32[]{:S(2)}) async-start(bf16[8,64,128]{2,1,0:T(8,128)(2,1)} %get-tuple-element.34), calls=%async_computation.2 | async-start | bytes 262144 | tf_op jit(solution)/shard_map/all_to_all | solution.py:234
  41.4 10.1 %all-to-all-done.2.t_ref = bf16[8,64,128]{2,1,0:T(8,128)(2,1)S(1)} async-done(((bf16[8,64,128]{2,1,0:T(8,128)(2,1)}), bf16[8,64,128]{2,1,0:T(8,128)(2,1)S(1)}, u32[]{:S(2)}, u32[]{:S(2)}) %all-to-all-start.2) | async-done | bytes 131104 | tf_op jit(solution)/shard_map/all_to_all | solution.py:234
  51.5 9.5 %all_to_all.22 = bf16[8,64,128]{2,1,0:T(8,128)(2,1)} all-to-all(bf16[8,64,128]{2,1,0:T(8,128)(2,1)S(1)} %shard_map.48), channel_id=1, replica_groups=mesh['z'=8,'x'=4,'core'=2,'tp'=8] {'x','core'}, dimensions={0} | all-to-all | bytes 262144 | tf_op jit(solution)/shard_map/all_to_all | solution.py:237
  61.0 5.1 %shard_map.49.n_ref = bf16[512,512]{1,0:T(8,128)(2,1)} custom-call(bf16[512,512]{1,0:T(8,128)(2,1)} %q_hbm.1, bf16[512,512]{1,0:T(8,128)(2,1)} %k_hbm.1, bf16[512,512]{1,0:T(8,128)(2,1)} %v_hbm.3, bf16[512,128]{1,0:T(8,128)(2,1)} %bitcast.8), custom_call_target="tpu_custom_call" | custom-call | flops 536870912 | bytes 2097152 | tf_op jit(solution)/shard_map/pallas_call | solution.py:115
  66.1 3.7 %all-gather.2.cloned.1.call-done = bf16[4096,512]{1,0:T(8,128)(2,1)} async-done(((bf16[256,512]{1,0:T(8,128)(2,1)}), bf16[4096,512]{1,0:T(8,128)(2,1)}) %all-gather.2.cloned.1.call-update) | async-done | bytes 4194320 | tf_op jit(solution)/shard_map/all_gather | solution.py:226
  69.8 5.4 %shard_map.50 = bf16[512,3072]{1,0:T(8,128)(2,1)} custom-call(bf16[512,512]{1,0:T(8,128)(2,1)} %shard_map.49.n_ref, bf16[2,8,4,64,512]{4,3,2,1,0:T(8,128)(2,1)} %bitcast.10), custom_call_target="tpu_custom_call" | custom-call | flops 2147483648 | bytes 6291456 | tf_op jit(solution)/shard_map/pallas_call | solution.py:153
  75.3 1.4 slice.4.w_ref
  76.7 0.7 shard_map.51
  77.4 3.1 %collective-permute-start = (bf16[64,512]{1,0:T(8,128)(2,1)S(1)}, bf16[64,512]{1,0:T(8,128)(2,1)S(1)}, u32[]{:S(2)}, u32[]{:S(2)}) collective-permute-start(bf16[64,512]{1,0:T(8,128)(2,1)S(1)} %get-tuple-element.42), channel_id=1, source_target_pairs={{0,1},{1,2},{2,3},{3,4},{4,5},{5,6},{6,7},{7,0},{8,9},{9,10},{10,1... | collective-permute-start | bytes 196616 | tf_op jit(solution)/shard_map/ppermute | solution.py:197
  80.6 3.4 %collective-permute-start.1 = (bf16[64,512]{1,0:T(8,128)(2,1)S(1)}, bf16[64,512]{1,0:T(8,128)(2,1)S(1)}, u32[]{:S(2)}, u32[]{:S(2)}) collective-permute-start(bf16[64,512]{1,0:T(8,128)(2,1)S(1)} %get-tuple-element.43), channel_id=1, source_target_pairs={{0,7},{1,0},{2,1},{3,2},{4,3},{5,4},{6,5},{7,6},{8,15},{9,8},{10,9... | collective-permute-start | bytes 196616 | tf_op jit(solution)/shard_map/ppermute | solution.py:198
  83.9 1.6 %collective-permute-done.1.down_ref = bf16[64,512]{1,0:T(8,128)(2,1)S(1)} collective-permute-done((bf16[64,512]{1,0:T(8,128)(2,1)S(1)}, bf16[64,512]{1,0:T(8,128)(2,1)S(1)}, u32[]{:S(2)}, u32[]{:S(2)}) %collective-permute-start.1) | collective-permute-done | bytes 65568 | tf_op jit(solution)/shard_map/ppermute | solution.py:198
  85.6 3.2 %collective-permute-start.2 = (bf16[64,1024]{1,0:T(8,128)(2,1)S(1)}, bf16[64,1024]{1,0:T(8,128)(2,1)S(1)}, u32[]{:S(2)}, u32[]{:S(2)}) collective-permute-start(bf16[64,1024]{1,0:T(8,128)(2,1)S(1)} %get-tuple-element.47), channel_id=1, source_target_pairs={{0,1},{1,2},{2,3},{3,4},{4,5},{5,6},{6,7},{7,0},{8,9},{9,10},{10,1... | collective-permute-start | bytes 393224 | tf_op jit(solution)/shard_map/ppermute | solution.py:197
  88.8 3.3 %collective-permute-start.3 = (bf16[64,1024]{1,0:T(8,128)(2,1)S(1)}, bf16[64,1024]{1,0:T(8,128)(2,1)S(1)}, u32[]{:S(2)}, u32[]{:S(2)}) collective-permute-start(bf16[64,1024]{1,0:T(8,128)(2,1)S(1)} %get-tuple-element.48), channel_id=1, source_target_pairs={{0,7},{1,0},{2,1},{3,2},{4,3},{5,4},{6,5},{7,6},{8,15},{9,8},{10,9... | collective-permute-start | bytes 393224 | tf_op jit(solution)/shard_map/ppermute | solution.py:198
  92.1 3.9 %collective-permute-done.2.up_ref = bf16[64,1024]{1,0:T(8,128)(2,1)S(1)} collective-permute-done((bf16[64,1024]{1,0:T(8,128)(2,1)S(1)}, bf16[64,1024]{1,0:T(8,128)(2,1)S(1)}, u32[]{:S(2)}, u32[]{:S(2)}) %collective-permute-start.2) | collective-permute-done | bytes 131104 | tf_op jit(solution)/shard_map/ppermute | solution.py:197
  96.0 3.3 %collective-permute-done.3.down_ref = bf16[64,1024]{1,0:T(8,128)(2,1)S(1)} collective-permute-done((bf16[64,1024]{1,0:T(8,128)(2,1)S(1)}, bf16[64,1024]{1,0:T(8,128)(2,1)S(1)}, u32[]{:S(2)}, u32[]{:S(2)}) %collective-permute-start.3) | collective-permute-done | bytes 131104 | tf_op jit(solution)/shard_map/ppermute | solution.py:198
  99.2 0.1 shard_map.53
  99.3 4.6 %collective-permute-start.4 = (bf16[64,1024]{1,0:T(8,128)(2,1)S(1)}, bf16[64,1024]{1,0:T(8,128)(2,1)S(1)}, u32[]{:S(2)}, u32[]{:S(2)}) collective-permute-start(bf16[64,1024]{1,0:T(8,128)(2,1)S(1)} %get-tuple-element.52), channel_id=1, source_target_pairs={{0,1},{1,2},{2,3},{3,4},{4,5},{5,6},{6,7},{7,0},{8,9},{9,10},{10,1... | collective-permute-start | bytes 393224 | tf_op jit(solution)/shard_map/ppermute | solution.py:197
  103.9 1.9 %collective-permute-start.5 = (bf16[64,1024]{1,0:T(8,128)(2,1)S(1)}, bf16[64,1024]{1,0:T(8,128)(2,1)S(1)}, u32[]{:S(2)}, u32[]{:S(2)}) collective-permute-start(bf16[64,1024]{1,0:T(8,128)(2,1)S(1)} %get-tuple-element.53), channel_id=1, source_target_pairs={{0,7},{1,0},{2,1},{3,2},{4,3},{5,4},{6,5},{7,6},{8,15},{9,8},{10,9... | collective-permute-start | bytes 393224 | tf_op jit(solution)/shard_map/ppermute | solution.py:198
  105.9 4.2 %collective-permute-done.4.up_ref = bf16[64,1024]{1,0:T(8,128)(2,1)S(1)} collective-permute-done((bf16[64,1024]{1,0:T(8,128)(2,1)S(1)}, bf16[64,1024]{1,0:T(8,128)(2,1)S(1)}, u32[]{:S(2)}, u32[]{:S(2)}) %collective-permute-start.4) | collective-permute-done | bytes 131104 | tf_op jit(solution)/shard_map/ppermute | solution.py:197
  110.1 2.8 %collective-permute-done.5.down_ref = bf16[64,1024]{1,0:T(8,128)(2,1)S(1)} collective-permute-done((bf16[64,1024]{1,0:T(8,128)(2,1)S(1)}, bf16[64,1024]{1,0:T(8,128)(2,1)S(1)}, u32[]{:S(2)}, u32[]{:S(2)}) %collective-permute-start.5) | collective-permute-done | bytes 131104 | tf_op jit(solution)/shard_map/ppermute | solution.py:198
  112.9 0.1 shard_map.54
  112.9 2.9 %collective-permute-start.6 = (bf16[64,1024]{1,0:T(8,128)(2,1)S(1)}, bf16[64,1024]{1,0:T(8,128)(2,1)S(1)}, u32[]{:S(2)}, u32[]{:S(2)}) collective-permute-start(bf16[64,1024]{1,0:T(8,128)(2,1)S(1)} %get-tuple-element.57), channel_id=1, source_target_pairs={{0,1},{1,2},{2,3},{3,4},{4,5},{5,6},{6,7},{7,0},{8,9},{9,10},{10,1... | collective-permute-start | bytes 393224 | tf_op jit(solution)/shard_map/ppermute | solution.py:197
  115.9 3.6 %collective-permute-start.7 = (bf16[64,1024]{1,0:T(8,128)(2,1)S(1)}, bf16[64,1024]{1,0:T(8,128)(2,1)S(1)}, u32[]{:S(2)}, u32[]{:S(2)}) collective-permute-start(bf16[64,1024]{1,0:T(8,128)(2,1)S(1)} %get-tuple-element.58), channel_id=1, source_target_pairs={{0,7},{1,0},{2,1},{3,2},{4,3},{5,4},{6,5},{7,6},{8,15},{9,8},{10,9... | collective-permute-start | bytes 393224 | tf_op jit(solution)/shard_map/ppermute | solution.py:198
  119.5 3.7 %collective-permute-done.6 = bf16[64,1024]{1,0:T(8,128)(2,1)S(1)} collective-permute-done((bf16[64,1024]{1,0:T(8,128)(2,1)S(1)}, bf16[64,1024]{1,0:T(8,128)(2,1)S(1)}, u32[]{:S(2)}, u32[]{:S(2)}) %collective-permute-start.6) | collective-permute-done | bytes 131104 | tf_op jit(solution)/shard_map/ppermute | solution.py:197
  123.2 2.0 %collective-permute-done.7 = bf16[64,1024]{1,0:T(8,128)(2,1)S(1)} collective-permute-done((bf16[64,1024]{1,0:T(8,128)(2,1)S(1)}, bf16[64,1024]{1,0:T(8,128)(2,1)S(1)}, u32[]{:S(2)}, u32[]{:S(2)}) %collective-permute-start.7) | collective-permute-done | bytes 131104 | tf_op jit(solution)/shard_map/ppermute | solution.py:198
  125.2 3.7 %reduce-scatter.2.cloned.1.call-done = bf16[64,3072]{1,0:T(8,128)(2,1)} async-done(((bf16[512,3072]{1,0:T(8,128)(2,1)}), bf16[64,3072]{1,0:T(8,128)(2,1)}) %reduce-scatter.2.cloned.1.call-update) | async-done | bytes 393232 | tf_op jit(solution)/shard_map/reduce_scatter | solution.py:241
  128.9 1.8 %pad_maximum_fusion = bf16[64,4096]{1,0:T(8,128)(2,1)} fusion(bf16[64,1024]{1,0:T(8,128)(2,1)S(1)} %add_convert_fusion, bf16[64,3072]{1,0:T(8,128)(2,1)} %reduce-scatter.2.cloned.1.call-done), kind=kLoop, calls=%fused_computation | loop fusion | flops 1048576 | bytes 1048576 | tf_op jit(solution)/shard_map/concatenate | solution.py:245
  (10 shorter events, 0.2 us)
Async XLA Ops:
  6.5 63.3 %all-gather.2.cloned.1.call-start = ((), (), s32[]{:S(2)}) async-start(), calls=%async_computation.5 | async-start | bytes 4456448 | tf_op jit(solution)/shard_map/all_gather | solution.py:226
  35.5 15.9 %all-to-all-start.2 = ((bf16[8,64,128]{2,1,0:T(8,128)(2,1)}), bf16[8,64,128]{2,1,0:T(8,128)(2,1)S(1)}, u32[]{:S(2)}, u32[]{:S(2)}) async-start(bf16[8,64,128]{2,1,0:T(8,128)(2,1)} %get-tuple-element.34), calls=%async_computation.2 | async-start | bytes 262144 | tf_op jit(solution)/shard_map/all_to_all | solution.py:234
  41.3 87.6 %reduce-scatter.2.cloned.1.call-start = ((), (), s32[]{:S(2)}) async-start(), calls=%async_computation.6 | async-start | bytes 3538944 | tf_op jit(solution)/shard_map/reduce_scatter | solution.py:241
  75.2 1.4 %copy-start = (bf16[512,512]{1,0:T(8,128)(2,1)S(1)}, bf16[512,512]{1,0:T(8,128)(2,1)}, u32[]{:S(2)}) copy-start(bf16[512,512]{1,0:T(8,128)(2,1)} %shard_map.49.n_ref) | copy-start | bytes 1572868
  77.4 6.5 %collective-permute-start = (bf16[64,512]{1,0:T(8,128)(2,1)S(1)}, bf16[64,512]{1,0:T(8,128)(2,1)S(1)}, u32[]{:S(2)}, u32[]{:S(2)}) collective-permute-start(bf16[64,512]{1,0:T(8,128)(2,1)S(1)} %get-tuple-element.42), channel_id=1, source_target_pairs={{0,1},{1,2},{2,3},{3,4},{4,5},{5,6},{6,7},{7,0},{8,9},{9,10},{10,1... | collective-permute-start | bytes 196616 | tf_op jit(solution)/shard_map/ppermute | solution.py:197
  80.6 5.0 %collective-permute-start.1 = (bf16[64,512]{1,0:T(8,128)(2,1)S(1)}, bf16[64,512]{1,0:T(8,128)(2,1)S(1)}, u32[]{:S(2)}, u32[]{:S(2)}) collective-permute-start(bf16[64,512]{1,0:T(8,128)(2,1)S(1)} %get-tuple-element.43), channel_id=1, source_target_pairs={{0,7},{1,0},{2,1},{3,2},{4,3},{5,4},{6,5},{7,6},{8,15},{9,8},{10,9... | collective-permute-start | bytes 196616 | tf_op jit(solution)/shard_map/ppermute | solution.py:198
  85.6 10.4 %collective-permute-start.2 = (bf16[64,1024]{1,0:T(8,128)(2,1)S(1)}, bf16[64,1024]{1,0:T(8,128)(2,1)S(1)}, u32[]{:S(2)}, u32[]{:S(2)}) collective-permute-start(bf16[64,1024]{1,0:T(8,128)(2,1)S(1)} %get-tuple-element.47), channel_id=1, source_target_pairs={{0,1},{1,2},{2,3},{3,4},{4,5},{5,6},{6,7},{7,0},{8,9},{9,10},{10,1... | collective-permute-start | bytes 393224 | tf_op jit(solution)/shard_map/ppermute | solution.py:197
  88.8 10.5 %collective-permute-start.3 = (bf16[64,1024]{1,0:T(8,128)(2,1)S(1)}, bf16[64,1024]{1,0:T(8,128)(2,1)S(1)}, u32[]{:S(2)}, u32[]{:S(2)}) collective-permute-start(bf16[64,1024]{1,0:T(8,128)(2,1)S(1)} %get-tuple-element.48), channel_id=1, source_target_pairs={{0,7},{1,0},{2,1},{3,2},{4,3},{5,4},{6,5},{7,6},{8,15},{9,8},{10,9... | collective-permute-start | bytes 393224 | tf_op jit(solution)/shard_map/ppermute | solution.py:198
  99.3 10.8 %collective-permute-start.4 = (bf16[64,1024]{1,0:T(8,128)(2,1)S(1)}, bf16[64,1024]{1,0:T(8,128)(2,1)S(1)}, u32[]{:S(2)}, u32[]{:S(2)}) collective-permute-start(bf16[64,1024]{1,0:T(8,128)(2,1)S(1)} %get-tuple-element.52), channel_id=1, source_target_pairs={{0,1},{1,2},{2,3},{3,4},{4,5},{5,6},{6,7},{7,0},{8,9},{9,10},{10,1... | collective-permute-start | bytes 393224 | tf_op jit(solution)/shard_map/ppermute | solution.py:197
  103.9 8.9 %collective-permute-start.5 = (bf16[64,1024]{1,0:T(8,128)(2,1)S(1)}, bf16[64,1024]{1,0:T(8,128)(2,1)S(1)}, u32[]{:S(2)}, u32[]{:S(2)}) collective-permute-start(bf16[64,1024]{1,0:T(8,128)(2,1)S(1)} %get-tuple-element.53), channel_id=1, source_target_pairs={{0,7},{1,0},{2,1},{3,2},{4,3},{5,4},{6,5},{7,6},{8,15},{9,8},{10,9... | collective-permute-start | bytes 393224 | tf_op jit(solution)/shard_map/ppermute | solution.py:198
  112.9 10.2 %collective-permute-start.6 = (bf16[64,1024]{1,0:T(8,128)(2,1)S(1)}, bf16[64,1024]{1,0:T(8,128)(2,1)S(1)}, u32[]{:S(2)}, u32[]{:S(2)}) collective-permute-start(bf16[64,1024]{1,0:T(8,128)(2,1)S(1)} %get-tuple-element.57), channel_id=1, source_target_pairs={{0,1},{1,2},{2,3},{3,4},{4,5},{5,6},{6,7},{7,0},{8,9},{9,10},{10,1... | collective-permute-start | bytes 393224 | tf_op jit(solution)/shard_map/ppermute | solution.py:197
  115.9 9.3 %collective-permute-start.7 = (bf16[64,1024]{1,0:T(8,128)(2,1)S(1)}, bf16[64,1024]{1,0:T(8,128)(2,1)S(1)}, u32[]{:S(2)}, u32[]{:S(2)}) collective-permute-start(bf16[64,1024]{1,0:T(8,128)(2,1)S(1)} %get-tuple-element.58), channel_id=1, source_target_pairs={{0,7},{1,0},{2,1},{3,2},{4,3},{5,4},{6,5},{7,6},{8,15},{9,8},{10,9... | collective-permute-start | bytes 393224 | tf_op jit(solution)/shard_map/ppermute | solution.py:198
Sparse Core Ops, SparseCore 0:
  17.8 51.9 all-gather.1
  75.4 53.4 reduce-scatter.1
